TPU v7x, 32 devices: a whole 2x2x4 slice. The times are simulated.
32 devices in a mesh: dp: 8 (over z, y), head: 4 (over x, core).
Axes of the slice: x: 2, y: 2, z: 4, core: 2. Of those that a mesh axis runs over, the one named last changes fastest.
Arguments:
- tokens: bfloat16 [16384, 1024], P('dp'), may hold values from -6 to 6
- segments: int32 [16, 1024], P('dp'), may hold values from 0 to 15, never falling along the last dimension, each value on 1 to 512 neighbouring positions
- cotangent: bfloat16 [16384, 1024], P('dp'), may hold values from -6 to 6
- gain_in: float32 [1024], replicated, may hold values from 0.5 to 1.5
- mamba_gate_weight: float32 [1024, 1536], P('dp', 'head'), may hold values from -0.1875 to 0.1875
- mamba_input_weight: float32 [1024, 1536], P('dp', 'head'), may hold values from -0.1875 to 0.1875
- w_dt: float32 [1024, 24], P('dp', 'head'), may hold values from -0.1875 to 0.1875
- w_bc: float32 [1024, 256], P('dp'), may hold values from -0.1875 to 0.1875
- convolution_input_taps: float32 [4, 1536], P(None, 'head'), may hold values from -3 to 3
- convolution_input_bias: float32 [1536], P('head'), may hold values from -0.5 to 0.5
- conv_bc: float32 [4, 256], replicated, may hold values from -3 to 3
- conv_bc_bias: float32 [256], replicated, may hold values from -0.5 to 0.5
- dt_bias: float32 [24], P('head'), may hold values from -4 to -1
- a_log: float32 [24], P('head'), may hold values from -3 to 1
- d_skip: float32 [24], P('head'), may hold values from 0.5 to 1.5
- w_q: float32 [1024, 512], P('dp', 'head'), may hold values from -0.1875 to 0.1875
- w_k: float32 [1024, 128], P('dp'), may hold values from -0.1875 to 0.1875
- w_v: float32 [1024, 128], P('dp'), may hold values from -0.1875 to 0.1875
- w_o: float32 [512, 1024], P('head', 'dp'), may hold values from -0.75 to 0.75
- mamba_output_weight: float32 [1536, 1024], P('head', 'dp'), may hold values from -0.15625 to 0.15625
- gain_ffn: float32 [1024], replicated, may hold values from 0.5 to 1.5
- w_gate: float32 [1024, 2048], P('dp', 'head'), may hold values from -0.1875 to 0.1875
- w_up: float32 [1024, 2048], P('dp', 'head'), may hold values from -0.1875 to 0.1875
- w_down: float32 [2048, 1024], P('head', 'dp'), may hold values from -0.125 to 0.125
Outputs:
- output: bfloat16 [16384, 1024], P('dp')
- grad_tokens: bfloat16 [16384, 1024], P('dp')
- grad_gain_in: float32 [1024], P('dp')
- grad_w_z: float32 [1024, 1536], P('dp', 'head')
- grad_w_x: float32 [1024, 1536], P('dp', 'head')
- grad_w_dt: float32 [1024, 24], P('dp', 'head')
- grad_w_bc: float32 [1024, 256], P(('dp', 'head'))
- grad_conv_x: float32 [4, 1536], P(None, 'head')
- grad_conv_x_bias: float32 [1536], P('head')
- grad_conv_bc: float32 [4, 256], P(None, ('dp', 'head'))
- grad_conv_bc_bias: float32 [256], P(('dp', 'head'))
- grad_dt_bias: float32 [24], P('head')
- grad_a_log: float32 [24], P('head')
- grad_d_skip: float32 [24], P('head')
- grad_w_q: float32 [1024, 512], P('dp', 'head')
- grad_w_k: float32 [1024, 128], P(('dp', 'head'))
- grad_w_v: float32 [1024, 128], P(('dp', 'head'))
- grad_w_o: float32 [512, 1024], P('head', 'dp')
- grad_w_out: float32 [1536, 1024], P('head', 'dp')
- grad_gain_ffn: float32 [1024], P('dp')
- grad_w_gate: float32 [1024, 2048], P('dp', 'head')
- grad_w_up: float32 [1024, 2048], P('dp', 'head')
- grad_w_down: float32 [2048, 1024], P('head', 'dp')
Inputs may be any that keep to these rules, and one draw needn't show every extreme that they name: `segments`: document numbers never fall along a sequence, and a document has at most 512 tokens.
All inputs are finite; a program needn't handle non-finite values.
Results may differ from a plain program's by a relative error of at most 0.025.
Values may be sent and summed in bfloat16 or wider, within the bound.
No kernel may reach another device: no remote copies, remote signals or barrier semaphores. Data moves between devices by JAX's collectives and lax.ppermute only.
A program may use at most 320 MiB of HBM per device.

v0:
```python
import math

import jax
import jax.numpy as jnp
from jax import lax
from jax.sharding import PartitionSpec as P

QHEADS = 8
KVHEADS = 2
HD = 64


HIGHEST = lax.Precision.HIGHEST
EPSILON = 1e-05
THETA = 100000000000.0


def for_sending(value):

    def short(part):
        return part.astype(jnp.bfloat16) if part.dtype == jnp.float32 else part

    return jax.tree.map(short, value)


def round_value(values):
    return lax.optimization_barrier(values.astype(jnp.bfloat16)).astype(jnp.float32)


def round_keep(values):
    return (round_value(values), None)


def round_pass(kept, grad):
    return (grad,)


def plain_value(values):
    return values


def plain_keep(values):
    return (values, None)


def plain_round(kept, grad):
    return (round_value(grad),)


def low(values):
    rounding = jax.custom_vjp(round_value)
    rounding.defvjp(round_keep, round_pass)
    return rounding(values)


def low_back(values):
    passing = jax.custom_vjp(plain_value)
    passing.defvjp(plain_keep, plain_round)
    return passing(values)


def matmul_local(left, right):
    return jnp.dot(left, right, preferred_element_type=jnp.float32)


def silu_value(values):
    return values * jax.nn.sigmoid(values)


def softplus_value(values):
    return jnp.log1p(jnp.exp(values))


def norm_round(values, gain):
    return low(
        values * lax.rsqrt(jnp.mean(values * values, axis=-1, keepdims=True) + EPSILON) * gain
    )


def rope_tables(length, width):
    position = jnp.arange(length).astype(jnp.float32)
    freqs = jnp.exp(-(jnp.arange(0, width, 2).astype(jnp.float32) / width) * math.log(THETA))
    angle = position[:, None] * freqs[None, :]
    angle = jnp.concatenate([angle, angle], axis=-1)
    return (jnp.cos(angle), jnp.sin(angle))


def rotary(values, cosine, sine):
    half = values.shape[-1] // 2
    turned = jnp.concatenate([-values[..., half:], values[..., :half]], axis=-1)
    return values * cosine[:, None, :] + turned * sine[:, None, :]


def doc_mask(seg):
    places = jnp.arange(seg.shape[0])
    return (places[:, None] >= places[None, :]) & (seg[:, None] == seg[None, :])


def causal_conv(values, taps, bias, seg):
    result = bias + taps[0] * values
    for offset in range(1, taps.shape[0]):
        shifted = jnp.concatenate(
            [jnp.zeros((offset, values.shape[1]), values.dtype), values[:-offset]], axis=0
        )
        keep = jnp.concatenate([jnp.zeros((offset,), jnp.bool_), seg[offset:] == seg[:-offset]])
        result = result + taps[offset] * jnp.where(keep[:, None], shifted, 0.0)
    return result


def ssd_core(conv_inner, conv_pair, step, a_log, d_skip, seg):
    length, heads = step.shape
    state = conv_pair.shape[1] // 2
    input_b = low(conv_pair[:, :state])
    output_c = low(conv_pair[:, state:])
    intersection = low_back(matmul_local(output_c, input_b.T))
    decay_log = jnp.cumsum(step * -jnp.exp(a_log), axis=0).T
    mask = doc_mask(seg)
    decay = jnp.exp(jnp.where(mask[None], decay_log[:, :, None] - decay_log[:, None, :], -1e30))
    mixing = low(intersection[None] * decay)
    inner_heads = conv_inner.reshape(length, heads, -1)
    driven = low(step[:, :, None] * inner_heads)
    scanned = (
        jnp.einsum("hij,jhd->ihd", mixing, driven, preferred_element_type=jnp.float32)
        + d_skip[None, :, None] * inner_heads
    )
    return low_back(scanned).reshape(length, -1)


def attention_core(query_raw, key_raw, value_raw, kv_map, seg):
    length = query_raw.shape[0]
    cosine, sine = rope_tables(length, HD)
    query = low(rotary(query_raw.reshape(length, -1, HD), cosine, sine))
    key = low(rotary(key_raw.reshape(length, -1, HD), cosine, sine))
    value = low(value_raw).reshape(length, -1, HD)
    key_sel = jnp.einsum("lkd,hk->lhd", key, kv_map, precision=HIGHEST)
    value_sel = jnp.einsum("lkd,hk->lhd", value, kv_map, precision=HIGHEST)
    scores = low_back(
        jnp.einsum("qhd,khd->hqk", query, key_sel, preferred_element_type=jnp.float32)
        * HD ** (-0.5)
    )
    scores = jnp.where(doc_mask(seg)[None], scores, -1e30)
    peak = jnp.max(scores, axis=-1, keepdims=True)
    weights = jnp.exp(scores - peak)
    probs = low(weights / jnp.sum(weights, axis=-1, keepdims=True))
    attended = jnp.einsum("hqk,khd->qhd", probs, value_sel, preferred_element_type=jnp.float32)
    return low(low_back(attended.reshape(length, -1)))


def mixer(
    normed,
    mamba_gate_weight,
    mamba_input_weight,
    w_dt,
    w_bc,
    w_q,
    w_k,
    w_v,
    w_o,
    mamba_output_weight,
    convolution_input_taps,
    convolution_input_bias,
    conv_bc,
    conv_bc_bias,
    dt_bias,
    a_log,
    d_skip,
    seg,
    kv_map,
):
    gate_z = low_back(matmul_local(normed, mamba_gate_weight))
    inner = low_back(matmul_local(normed, mamba_input_weight))
    pair = low_back(matmul_local(normed, w_bc))
    step_raw = low_back(matmul_local(normed, w_dt))
    conv_inner = silu_value(causal_conv(inner, convolution_input_taps, convolution_input_bias, seg))
    conv_pair = silu_value(causal_conv(pair, conv_bc, conv_bc_bias, seg))
    step = softplus_value(step_raw + dt_bias)
    scanned = jax.checkpoint(ssd_core)(conv_inner, conv_pair, step, a_log, d_skip, seg)
    gated = low(scanned * silu_value(gate_z))
    attended = jax.checkpoint(attention_core)(
        low_back(matmul_local(normed, w_q)),
        low_back(matmul_local(normed, w_k)),
        low_back(matmul_local(normed, w_v)),
        kv_map,
        seg,
    )
    return matmul_local(gated, mamba_output_weight) + matmul_local(attended, w_o)


def feed_forward(normed, w_gate, w_up, w_down):
    gate = low_back(matmul_local(normed, w_gate))
    upward = low_back(matmul_local(normed, w_up))
    hidden = low(silu_value(gate) * upward)
    return matmul_local(hidden, w_down)


def reduce_grads(mixer_grads, ffn_grads, gain_grads):
    (
        g_z,
        g_x,
        g_dt,
        g_bc,
        g_q,
        g_k,
        g_v,
        g_o,
        g_out,
        g_convx,
        g_convxb,
        g_convbc,
        g_convbcb,
        g_dtb,
        g_alog,
        g_dskip,
    ) = mixer_grads
    g_gate, g_up, g_down = ffn_grads
    g_gain_in, g_gain_ffn = gain_grads
    heads_part = (
        lax.psum_scatter(g_z.astype(jnp.bfloat16), "dp", scatter_dimension=0, tiled=True).astype(
            jnp.float32
        ),
        lax.psum_scatter(g_x.astype(jnp.bfloat16), "dp", scatter_dimension=0, tiled=True).astype(
            jnp.float32
        ),
        lax.psum_scatter(g_dt.astype(jnp.bfloat16), "dp", scatter_dimension=0, tiled=True).astype(
            jnp.float32
        ),
        lax.psum_scatter(g_q.astype(jnp.bfloat16), "dp", scatter_dimension=0, tiled=True).astype(
            jnp.float32
        ),
        lax.psum_scatter(g_o.astype(jnp.bfloat16), "dp", scatter_dimension=1, tiled=True).astype(
            jnp.float32
        ),
        lax.psum_scatter(g_out.astype(jnp.bfloat16), "dp", scatter_dimension=1, tiled=True).astype(
            jnp.float32
        ),
        lax.psum_scatter(g_gate.astype(jnp.bfloat16), "dp", scatter_dimension=0, tiled=True).astype(
            jnp.float32
        ),
        lax.psum_scatter(g_up.astype(jnp.bfloat16), "dp", scatter_dimension=0, tiled=True).astype(
            jnp.float32
        ),
        lax.psum_scatter(g_down.astype(jnp.bfloat16), "dp", scatter_dimension=1, tiled=True).astype(
            jnp.float32
        ),
        lax.psum_scatter(
            g_gain_in.astype(jnp.bfloat16), "dp", scatter_dimension=0, tiled=True
        ).astype(jnp.float32),
        lax.psum_scatter(
            g_gain_ffn.astype(jnp.bfloat16), "dp", scatter_dimension=0, tiled=True
        ).astype(jnp.float32),
    )
    shared_part = (
        lax.psum_scatter(g_bc, ("dp", "head"), scatter_dimension=0, tiled=True),
        lax.psum_scatter(g_k, ("dp", "head"), scatter_dimension=0, tiled=True),
        lax.psum_scatter(g_v, ("dp", "head"), scatter_dimension=0, tiled=True),
        lax.psum_scatter(g_convbc, ("dp", "head"), scatter_dimension=1, tiled=True),
        lax.psum_scatter(g_convbcb, ("dp", "head"), scatter_dimension=0, tiled=True),
    )
    small_part = lax.psum((g_convx, g_convxb, g_dtb, g_alog, g_dskip), "dp")
    return (heads_part, shared_part, small_part)


def body(
    tokens,
    segments,
    cotangent,
    gain_in,
    mamba_gate_weight,
    mamba_input_weight,
    w_dt,
    w_bc,
    convolution_input_taps,
    convolution_input_bias,
    conv_bc,
    conv_bc_bias,
    dt_bias,
    a_log,
    d_skip,
    w_q,
    w_k,
    w_v,
    w_o,
    mamba_output_weight,
    gain_ffn,
    w_gate,
    w_up,
    w_down,
):
    micro, length = segments.shape
    head_rank = lax.axis_index("head")
    local_query = w_q.shape[1] // HD
    global_query = head_rank * local_query + jnp.arange(local_query)
    kv_map = (global_query[:, None] // (QHEADS // KVHEADS) == jnp.arange(KVHEADS)[None, :]).astype(
        jnp.float32
    )
    small_weights = (
        convolution_input_taps,
        convolution_input_bias,
        conv_bc,
        conv_bc_bias,
        dt_bias,
        a_log,
        d_skip,
    )
    weights = None
    outputs = []
    grads_in = []
    totals = None
    for index in range(micro):
        gathered = (
            lax.all_gather(mamba_gate_weight.astype(jnp.bfloat16), "dp", axis=0, tiled=True),
            lax.all_gather(mamba_input_weight.astype(jnp.bfloat16), "dp", axis=0, tiled=True),
            lax.all_gather(w_dt.astype(jnp.bfloat16), "dp", axis=0, tiled=True),
            lax.all_gather(w_bc.astype(jnp.bfloat16), "dp", axis=0, tiled=True),
            lax.all_gather(w_q.astype(jnp.bfloat16), "dp", axis=0, tiled=True),
            lax.all_gather(w_k.astype(jnp.bfloat16), "dp", axis=0, tiled=True),
            lax.all_gather(w_v.astype(jnp.bfloat16), "dp", axis=0, tiled=True),
            lax.all_gather(w_o.astype(jnp.bfloat16), "dp", axis=1, tiled=True),
            lax.all_gather(mamba_output_weight.astype(jnp.bfloat16), "dp", axis=1, tiled=True),
            lax.all_gather(w_gate.astype(jnp.bfloat16), "dp", axis=0, tiled=True),
            lax.all_gather(w_up.astype(jnp.bfloat16), "dp", axis=0, tiled=True),
            lax.all_gather(w_down.astype(jnp.bfloat16), "dp", axis=1, tiled=True),
        )
        weights = tuple((piece.astype(jnp.float32) for piece in gathered))
        (
            full_z,
            full_x,
            full_dt,
            full_bc,
            full_query,
            full_key,
            full_value,
            full_attn,
            full_mamba,
            full_gate,
            full_up,
            full_down,
        ) = weights
        seg = segments[index]
        rows = tokens[index * length : (index + 1) * length].astype(jnp.float32)
        upstream = cotangent[index * length : (index + 1) * length].astype(jnp.float32)
        normed, norm_pull = jax.vjp(norm_round, rows, gain_in)
        mixer_in = (
            normed,
            full_z,
            full_x,
            full_dt,
            full_bc,
            full_query,
            full_key,
            full_value,
            full_attn,
            full_mamba,
        ) + small_weights
        mix_part, mix_pull = jax.vjp(lambda *values: mixer(*values, seg, kv_map), *mixer_in)
        mixed = jax.tree.map(
            lambda part: part.astype(jnp.float32), lax.psum(for_sending(mix_part), "head")
        )
        hidden_state = rows + mixed
        normed_ffn, ffn_norm_pull = jax.vjp(norm_round, hidden_state, gain_ffn)
        ffn_part, ffn_pull = jax.vjp(feed_forward, normed_ffn, full_gate, full_up, full_down)
        ffn_whole = jax.tree.map(
            lambda part: part.astype(jnp.float32), lax.psum(for_sending(ffn_part), "head")
        )
        outputs.append((hidden_state + ffn_whole).astype(jnp.bfloat16))
        back_ffn = ffn_pull(upstream)
        grad_normed_ffn = jax.tree.map(
            lambda part: part.astype(jnp.float32), lax.psum(for_sending(back_ffn[0]), "head")
        )
        grad_state, grad_gain_ffn = ffn_norm_pull(grad_normed_ffn)
        grad_state = upstream + grad_state
        back_mix = mix_pull(round_value(grad_state))
        grad_normed = jax.tree.map(
            lambda part: part.astype(jnp.float32), lax.psum(for_sending(back_mix[0]), "head")
        )
        grad_rows, grad_gain_in = norm_pull(grad_normed)
        grads_in.append((grad_state + grad_rows).astype(jnp.bfloat16))
        current = (tuple(back_mix[1:]), tuple(back_ffn[1:]), (grad_gain_in, grad_gain_ffn))
        totals = current if totals is None else jax.tree.map(jnp.add, totals, current)
    totals = reduce_grads(totals[0], totals[1], totals[2])
    heads_part, shared_part, small_part = totals
    g_z, g_x, g_dt, g_q, g_o, g_out, g_gate, g_up, g_down, g_gain_in, g_gain_ffn = heads_part
    g_bc, g_k, g_v, g_convbc, g_convbcb = shared_part
    g_convx, g_convxb, g_dtb, g_alog, g_dskip = small_part
    output = jnp.concatenate(outputs, axis=0)
    grad_tokens = jnp.concatenate(grads_in, axis=0)
    return (
        output,
        grad_tokens,
        g_gain_in,
        g_z,
        g_x,
        g_dt,
        g_bc,
        g_convx,
        g_convxb,
        g_convbc,
        g_convbcb,
        g_dtb,
        g_alog,
        g_dskip,
        g_q,
        g_k,
        g_v,
        g_o,
        g_out,
        g_gain_ffn,
        g_gate,
        g_up,
        g_down,
    )


def solution(mesh):
    in_specs = (
        P("dp", None),
        P("dp", None),
        P("dp", None),
        P(),
        P("dp", "head"),
        P("dp", "head"),
        P("dp", "head"),
        P("dp", None),
        P(None, "head"),
        P("head"),
        P(),
        P(),
        P("head"),
        P("head"),
        P("head"),
        P("dp", "head"),
        P("dp", None),
        P("dp", None),
        P("head", "dp"),
        P("head", "dp"),
        P(),
        P("dp", "head"),
        P("dp", "head"),
        P("head", "dp"),
    )
    out_specs = (
        P("dp", None),
        P("dp", None),
        P("dp"),
        P("dp", "head"),
        P("dp", "head"),
        P("dp", "head"),
        P(("dp", "head"), None),
        P(None, "head"),
        P("head"),
        P(None, ("dp", "head")),
        P(("dp", "head")),
        P("head"),
        P("head"),
        P("head"),
        P("dp", "head"),
        P(("dp", "head"), None),
        P(("dp", "head"), None),
        P("head", "dp"),
        P("head", "dp"),
        P("dp"),
        P("dp", "head"),
        P("dp", "head"),
        P("head", "dp"),
    )
    return jax.shard_map(body, mesh=mesh, in_specs=in_specs, out_specs=out_specs, check_vma=False)
```

profile of v0, /device:TPU:0, one launch (start us, length us, event | category | flops | bytes accessed | tf_op | source)
XLA Modules:
  0.0 1712.0 jit_solution(2625644595777987760)
XLA Ops:
  17.4 34.1 %all_gather.50 = bf16[1024,256]{1,0:T(8,128)(2,1)S(1)} all-gather(bf16[128,256]{1,0:T(8,128)(2,1)S(1)} %convert_element_type.562), channel_id=1, replica_groups=mesh['dp'=8,'head'=4] {'dp'}, dimensions={0}, use_global_device_ids=true | all-gather | bytes 589824 | tf_op jit(solution)/shard_map/all_gather | solution.py:314
  53.1 26.0 %all_gather.48 = bf16[1024,6]{0,1:T(8,128)(2,1)S(1)} all-gather(bf16[128,6]{0,1:T(8,128)(2,1)S(1)} %convert_element_type.559), channel_id=1, replica_groups=mesh['dp'=8,'head'=4] {'dp'}, dimensions={0}, use_global_device_ids=true | all-gather | bytes 13824 | tf_op jit(solution)/shard_map/all_gather | solution.py:313
  80.5 32.2 %all_gather.49 = bf16[1024,384]{1,0:T(8,128)(2,1)S(1)} all-gather(bf16[128,384]{1,0:T(8,128)(2,1)S(1)} %convert_element_type.560), channel_id=1, replica_groups=mesh['dp'=8,'head'=4] {'dp'}, dimensions={0}, use_global_device_ids=true | all-gather | bytes 884736 | tf_op jit(solution)/shard_map/all_gather | solution.py:312
  117.1 30.7 %all_gather.55 = bf16[1024,128]{1,0:T(8,128)(2,1)S(1)} all-gather(bf16[128,128]{1,0:T(8,128)(2,1)S(1)} %convert_element_type.573), channel_id=1, replica_groups=mesh['dp'=8,'head'=4] {'dp'}, dimensions={0}, use_global_device_ids=true | all-gather | bytes 294912 | tf_op jit(solution)/shard_map/all_gather | solution.py:316
  149.6 30.7 %all_gather.54 = bf16[1024,128]{1,0:T(8,128)(2,1)S(1)} all-gather(bf16[128,128]{1,0:T(8,128)(2,1)S(1)} %convert_element_type.569), channel_id=1, replica_groups=mesh['dp'=8,'head'=4] {'dp'}, dimensions={0}, use_global_device_ids=true | all-gather | bytes 294912 | tf_op jit(solution)/shard_map/all_gather | solution.py:315
  183.6 31.0 %all_gather.53 = bf16[1024,128]{1,0:T(8,128)(2,1)S(1)} all-gather(bf16[128,128]{1,0:T(8,128)(2,1)S(1)} %convert_element_type.567), channel_id=1, replica_groups=mesh['dp'=8,'head'=4] {'dp'}, dimensions={0}, use_global_device_ids=true | all-gather | bytes 294912 | tf_op jit(solution)/shard_map/all_gather | solution.py:317
  247.3 32.1 %all_gather.51 = bf16[1024,384]{1,0:T(8,128)(2,1)S(1)} all-gather(bf16[128,384]{1,0:T(8,128)(2,1)S(1)} %convert_element_type.564), channel_id=1, replica_groups=mesh['dp'=8,'head'=4] {'dp'}, dimensions={0}, use_global_device_ids=true | all-gather | bytes 884736 | tf_op jit(solution)/shard_map/all_gather | solution.py:311
  318.7 27.7 %all_gather.56 = bf16[128,1024]{1,0:T(8,128)(2,1)} all-gather(bf16[128,128]{1,0:T(8,128)(2,1)S(1)} %convert_element_type.579), channel_id=1, replica_groups=mesh['dp'=8,'head'=4] {'dp'}, dimensions={1}, use_global_device_ids=true | all-gather | bytes 294912 | tf_op jit(solution)/shard_map/all_gather | solution.py:318
  403.3 28.1 %all_gather.52 = bf16[384,1024]{1,0:T(8,128)(2,1)S(1)} all-gather(bf16[384,128]{1,0:T(8,128)(2,1)S(1)} %convert_element_type.566), channel_id=1, replica_groups=mesh['dp'=8,'head'=4] {'dp'}, dimensions={1}, use_global_device_ids=true | all-gather | bytes 884736 | tf_op jit(solution)/shard_map/all_gather | solution.py:319
  446.7 72.8 %all-reduce.74.cloned.1.call-done = (bf16[1024,1024]{1,0:T(8,128)(2,1)}, bf16[1024,1024]{1,0:T(8,128)(2,1)}) async-done(((bf16[1024,1024]{1,0:T(8,128)(2,1)}, bf16[1024,1024]{1,0:T(8,128)(2,1)}), (bf16[1024,1024]{1,0:T(8,128)(2,1)}, bf16[1024,1024]{1,0:T(8,128)(2,1)})) %all-reduce.74.cloned.1.call-update) | async-done | bytes 4194320 | tf_op jit(solution)/shard_map/psum | solution.py:357
  583.7 56.3 %all-reduce.72.cloned.1.call-done = (bf16[1024,1024]{1,0:T(8,128)(2,1)}, bf16[1024,1024]{1,0:T(8,128)(2,1)}) async-done(((bf16[1024,1024]{1,0:T(8,128)(2,1)}, bf16[1024,1024]{1,0:T(8,128)(2,1)}), (bf16[1024,1024]{1,0:T(8,128)(2,1)}, bf16[1024,1024]{1,0:T(8,128)(2,1)})) %all-reduce.72.cloned.1.call-update) | async-done | bytes 4194320 | tf_op jit(solution)/shard_map/psum | solution.py:368
  701.3 12.4 convert_reduce_fusion
  753.8 19.2 %fusion.5 = (f32[6,1024]{1,0:T(8,128)}, f32[6,1024]{1,0:T(8,128)}, bf16[1024,1024]{1,0:T(8,128)(2,1)S(1)}, bf16[6,1024,1024]{2,1,0:T(8,128)(2,1)}) fusion(f32[6,1024]{1,0:T(8,128)S(1)} %bitcast.625, f32[1024,1024]{1,0:T(8,128)S(1)} %fusion.318, pred[1024,1024]{1,0:T(8,128)(4,1)S(1)} %copy-done.154, bf16[1024,6,64]{0,2,1:T(8,128)(2,1)S(1)} %copy-done.163, ...), kind=kOutput, calls=%fused_computation.15 | convolution fusion | flops 873451520 | bytes 21569536 | tf_op jit(solution)/shard_map/transpose(jvp(jvp()))/checkpoint/hij,jhd->ihd/dot_general | solution.py:123
  791.1 18.2 %fusion.3 = (f32[6,1024]{1,0:T(8,128)}, f32[6,1024]{1,0:T(8,128)}, bf16[1024,1024]{1,0:T(8,128)(2,1)S(1)}, bf16[6,1024,1024]{2,1,0:T(8,128)(2,1)S(1)}) fusion(f32[6,1024]{1,0:T(8,128)S(1)} %bitcast.626, f32[1024,1024]{1,0:T(8,128)S(1)} %fusion.306, pred[1024,1024]{1,0:T(8,128)(4,1)S(1)} %copy-done.155, bf16[1024,6,64]{0,2,1:T(8,128)(2,1)S(1)} %copy-done.164, ...), kind=kOutput, calls=%fused_computation.13 | convolution fusion | flops 873451520 | bytes 21569536 | tf_op jit(solution)/shard_map/transpose(jvp(jvp()))/checkpoint/hij,jhd->ihd/dot_general | solution.py:123
  1010.1 41.1 %all-reduce.60 = (f32[4,256]{1,0:T(4,128)S(1)}, f32[256]{0:T(256)S(1)}) all-reduce(f32[4,256]{1,0:T(4,128)S(1)} %add_add_fusion.5, f32[256]{0:T(256)S(1)} %add.518), channel_id=7, replica_groups=mesh['dp'=8,'head'=4] {'dp','head'}, use_global_device_ids=true, to_apply=%region_77.78.clone | all-reduce | flops 1280 | bytes 10240
  1056.9 22.3 %all-reduce.61 = (f32[4,384]{1,0:T(4,128)}, f32[384]{0:T(512)}, f32[6]{0:T(128)}, f32[6]{0:T(128)}, f32[6]{0:T(128)}) all-reduce(f32[4,384]{1,0:T(4,128)S(1)} %add_add_fusion.4, f32[384]{0:T(512)S(1)} %add.516, f32[6]{0:T(128)S(1)} %add.519, f32[6]{0:T(128)S(1)} %multiply_add_fusion.8, ...), channel_id=1, replica_groups=mesh['dp'=8,'head'=4] {'dp'}, use_global_device_ids=true, to_apply=%region_65.66 | all-reduce | flops 1938 | bytes 15504 | tf_op jit(solution)/shard_map/psum | solution.py:259
  1085.5 22.5 %reduce-scatter.28.cloned.1.call-done = bf16[128,128]{1,0:T(8,128)(2,1)} async-done(((bf16[1024,128]{1,0:T(8,128)(2,1)}), bf16[128,128]{1,0:T(8,128)(2,1)}) %reduce-scatter.28.cloned.1.call-update) | async-done | bytes 32784 | tf_op jit(solution)/shard_map/reduce_scatter | solution.py:227
  1109.4 63.7 %reduce-scatter.42.cloned.1.call-done = bf16[128,384]{1,0:T(8,128)(2,1)} async-done(((bf16[1024,384]{1,0:T(8,128)(2,1)}), bf16[128,384]{1,0:T(8,128)(2,1)}) %reduce-scatter.42.cloned.1.call-update) | async-done | bytes 98320
  1174.8 63.1 %reduce-scatter.24.cloned.1.call-done = bf16[128,384]{1,0:T(8,128)(2,1)} async-done(((bf16[1024,384]{1,0:T(8,128)(2,1)}), bf16[128,384]{1,0:T(8,128)(2,1)}) %reduce-scatter.24.cloned.1.call-update) | async-done | bytes 98320 | tf_op jit(solution)/shard_map/reduce_scatter | solution.py:221
  1239.4 63.4 %reduce-scatter.22.cloned.1.call-done = bf16[128,384]{1,0:T(8,128)(2,1)} async-done(((bf16[1024,384]{1,0:T(8,128)(2,1)}), bf16[128,384]{1,0:T(8,128)(2,1)}) %reduce-scatter.22.cloned.1.call-update) | async-done | bytes 98320 | tf_op jit(solution)/shard_map/reduce_scatter | solution.py:218
  1310.3 19.4 %all-reduce.62 = (bf16[1024]{0:T(1024)(128)(2,1)S(1)}, bf16[1024]{0:T(1024)(128)(2,1)S(1)}) all-reduce(bf16[1024]{0:T(1024)(128)(2,1)S(1)} %add_convert_fusion.19, bf16[1024]{0:T(1024)(128)(2,1)S(1)} %add_convert_fusion.18), channel_id=2, replica_groups=mesh['dp'=8,'head'=4] {'dp'}, use_global_device_ids=true, to_apply=%region_52.53.clone | all-reduce | flops 2048 | bytes 8192
  1347.4 91.0 %reduce-scatter.32.cloned.1.call-done = f32[32,128]{1,0:T(8,128)} async-done(((f32[1024,128]{1,0:T(8,128)}), f32[32,128]{1,0:T(8,128)}) %reduce-scatter.32.cloned.1.call-update) | async-done | bytes 16400 | tf_op jit(solution)/shard_map/reduce_scatter | solution.py:255
  1438.4 132.7 %reduce-scatter.30.cloned.1.call-done = f32[32,128]{1,0:T(8,128)} async-done(((f32[1024,128]{1,0:T(8,128)}), f32[32,128]{1,0:T(8,128)}) %reduce-scatter.30.cloned.1.call-update) | async-done | bytes 16400 | tf_op jit(solution)/shard_map/reduce_scatter | solution.py:254
  1571.1 133.3 %reduce-scatter.26.cloned.1.call-done = f32[32,256]{1,0:T(8,128)} async-done(((f32[1024,256]{1,0:T(8,128)}), f32[32,256]{1,0:T(8,128)}) %reduce-scatter.26.cloned.1.call-update) | async-done | bytes 32784 | tf_op jit(solution)/shard_map/reduce_scatter | solution.py:253
  (1023 shorter events, 587.8 us)
Async XLA Ops:
  8.0 431.2 %all-gather.8.cloned.1.call-start = ((), (), s32[]{:S(2)}) async-start(), calls=%async_computation.14 | async-start | bytes 1179648 | tf_op jit(solution)/shard_map/all_gather | solution.py:322
  9.7 509.9 %all-reduce.74.cloned.1.call-start = ((), (), s32[]{:S(2)}) async-start(), calls=%async_computation.29 | async-start | bytes 8388608 | tf_op jit(solution)/shard_map/psum | solution.py:357
  17.4 362.8 %copy-start.4 = (bf16[1024,1024]{1,0:T(8,128)(2,1)}, bf16[1024,1024]{1,0:T(8,128)(2,1)S(1)}, u32[]{:S(2)}) copy-start(bf16[1024,1024]{1,0:T(8,128)(2,1)S(1)} %get-tuple-element.185) | copy-start | bytes 6291460
  217.9 351.2 %copy-start.215 = (pred[1024]{0:T(1024)(128)(4,1)}, pred[1024]{0:T(1024)(128)(4,1)S(1)}, u32[]{:S(2)}) copy-start(pred[1024]{0:T(1024)(128)(4,1)S(1)} %pad_add_fusion) | copy-start | bytes 3076
  293.1 369.9 %copy-start.68 = (f32[1024,64]{0,1:T(8,128)}, f32[1024,64]{0,1:T(8,128)S(1)}, u32[]{:S(2)}) copy-start(f32[1024,64]{0,1:T(8,128)S(1)} %get-tuple-element.243) | copy-start | bytes 786436
  436.8 91.8 %all-gather.6.cloned.1.call-start = ((), (), s32[]{:S(2)}) async-start(), calls=%async_computation.13 | async-start | bytes 1179648 | tf_op jit(solution)/shard_map/all_gather | solution.py:321
  438.4 94.6 %all-gather.4.cloned.1.call-start = ((), (), s32[]{:S(2)}) async-start(), calls=%async_computation.12 | async-start | bytes 1179648 | tf_op jit(solution)/shard_map/all_gather | solution.py:320
  439.2 200.8 %all-reduce.72.cloned.1.call-start = ((), (), s32[]{:S(2)}) async-start(), calls=%async_computation.28 | async-start | bytes 8388608 | tf_op jit(solution)/shard_map/psum | solution.py:368
  554.3 454.0 %reduce-scatter.44.cloned.1.call-start = ((), (), s32[]{:S(2)}) async-start(), calls=%async_computation.26 | async-start | bytes 1179648
  562.5 516.8 %reduce-scatter.36.cloned.1.call-start = ((), (), s32[]{:S(2)}) async-start(), calls=%async_computation.22 | async-start | bytes 1179648 | tf_op jit(solution)/shard_map/reduce_scatter | solution.py:239
  568.4 512.5 %reduce-scatter.34.cloned.1.call-start = ((), (), s32[]{:S(2)}) async-start(), calls=%async_computation.21 | async-start | bytes 1179648 | tf_op jit(solution)/shard_map/reduce_scatter | solution.py:236
  576.7 505.9 %reduce-scatter.38.cloned.1.call-start = ((), (), s32[]{:S(2)}) async-start(), calls=%async_computation.23 | async-start | bytes 294912
  918.4 165.6 %reduce-scatter.40.cloned.1.call-start = ((), (), s32[]{:S(2)}) async-start(), calls=%async_computation.24 | async-start | bytes 294912
  927.3 180.7 %reduce-scatter.28.cloned.1.call-start = ((), (), s32[]{:S(2)}) async-start(), calls=%async_computation.18 | async-start | bytes 294912 | tf_op jit(solution)/shard_map/reduce_scatter | solution.py:227
  933.8 239.3 %reduce-scatter.42.cloned.1.call-start = ((), (), s32[]{:S(2)}) async-start(), calls=%async_computation.25 | async-start | bytes 884736
  939.9 297.9 %reduce-scatter.24.cloned.1.call-start = ((), (), s32[]{:S(2)}) async-start(), calls=%async_computation.16 | async-start | bytes 884736 | tf_op jit(solution)/shard_map/reduce_scatter | solution.py:221
  956.4 346.4 %reduce-scatter.22.cloned.1.call-start = ((), (), s32[]{:S(2)}) async-start(), calls=%async_computation.15 | async-start | bytes 884736 | tf_op jit(solution)/shard_map/reduce_scatter | solution.py:218
  971.3 333.1 %all-reduce.70.cloned.1.call-start = ((), (), s32[]{:S(2)}) async-start(), calls=%async_computation.27 | async-start | bytes 16777216 | tf_op jit(solution)/shard_map/psum | solution.py:363
  997.4 441.0 %reduce-scatter.32.cloned.1.call-start = ((), (), s32[]{:S(2)}) async-start(), calls=%async_computation.20 | async-start | bytes 540672 | tf_op jit(solution)/shard_map/reduce_scatter | solution.py:255
  1002.3 568.8 %reduce-scatter.30.cloned.1.call-start = ((), (), s32[]{:S(2)}) async-start(), calls=%async_computation.19 | async-start | bytes 540672 | tf_op jit(solution)/shard_map/reduce_scatter | solution.py:254
  1008.0 696.5 %reduce-scatter.26.cloned.1.call-start = ((), (), s32[]{:S(2)}) async-start(), calls=%async_computation.17 | async-start | bytes 1081344 | tf_op jit(solution)/shard_map/reduce_scatter | solution.py:253
  1056.8 247.6 %copy-start.200 = (f32[1024]{0:T(1024)S(1)}, f32[1024]{0:T(1024)}, u32[]{:S(2)}) copy-start(f32[1024]{0:T(1024)} %param.27) | copy-start | bytes 12292
  1056.8 247.6 %copy-start.202 = (f32[1024]{0:T(1024)S(1)}, f32[1024]{0:T(1024)}, u32[]{:S(2)}) copy-start(f32[1024]{0:T(1024)} %copy-done.201) | copy-start | bytes 12292
  1056.8 247.6 %copy-start.204 = (f32[1024]{0:T(1024)S(1)}, f32[1024]{0:T(1024)}, u32[]{:S(2)}) copy-start(f32[1024]{0:T(1024)} %copy-done.203) | copy-start | bytes 12292
  (321 other events, 4259.1 us)
Sparse Core Ops, SparseCore 0:
  11.7 46.0 all-gather.7
  440.6 37.2 all-gather.5
  480.7 38.7 all-gather.3
  562.6 63.7 reduce-scatter.43
  630.0 62.3 reduce-scatter.35
  695.6 62.4 reduce-scatter.33
  918.5 61.3 reduce-scatter.37
  983.6 60.2 reduce-scatter.39
  1047.6 60.3 reduce-scatter.27
  1111.5 61.5 reduce-scatter.41
  1176.4 61.4 reduce-scatter.23
  1241.4 61.3 reduce-scatter.21
  1305.6 132.7 reduce-scatter.31
  1441.2 129.9 reduce-scatter.29
  1573.8 130.6 reduce-scatter.25
Sparse Core Ops, SparseCore 1:
  436.9 82.6 all-reduce.73
  554.4 85.6 all-reduce.71
  997.5 155.3 all-reduce.69
where the time goes:
time: 1720 us; the launch traced here: 1710 us
  waiting for transfers between devices  699 us (41%)
  blocking collectives  355 us (21%)
  matrix products  327 us (19%)
  other arithmetic  230 us (13%)
  local copies, waits for them, and re-layouts  78.3 us (5%)
  between operations  20.2 us (1%)
    dot_general x80, matrix products, matmul_local(): return jnp.dot(left, right, preferred_element_type=jnp.float32)  189 us
    reduce_scatter x1, waiting for transfers between devices, reduce_grads(): lax.psum_scatter(g_bc, ('dp', 'head'), scatter_dimension=0, tiled=True)  133 us
    reduce_scatter x1, waiting for transfers between devices, reduce_grads(): lax.psum_scatter(g_k, ('dp', 'head'), scatter_dimension=0, tiled=True)  133 us
    reduce_scatter x1, waiting for transfers between devices, reduce_grads(): lax.psum_scatter(g_v, ('dp', 'head'), scatter_dimension=0, tiled=True)  91 us
    psum x1, waiting for transfers between devices, body(): lax.psum(for_sending(mix_part), 'head')  72.8 us
    unnamed x22, waiting for transfers between devices  64 us
    reduce_scatter x1, waiting for transfers between devices, reduce_grads(): lax.psum_scatter(g_z.astype(jnp.bfloat16), 'dp', scatter_dimension=0, til...  63.4 us
    reduce_scatter x1, waiting for transfers between devices, reduce_grads(): lax.psum_scatter(g_x.astype(jnp.bfloat16), 'dp', scatter_dimension=0, til...  63.1 us
  transfers between devices with their start and end apart: 18, of which 9 were waited for; matrix products, arithmetic and copies ran while one was open for 34% of the time, Pallas kernels for 0%

commit v1 on v0

v1 whole, which is shorter than its diff:
```python
import math

import jax
import jax.numpy as jnp
from jax import lax
from jax.experimental import pallas as pl
from jax.experimental.pallas import tpu as pltpu
from jax.sharding import PartitionSpec as P

QHEADS = 8
KVHEADS = 2
HD = 64
STATE = 128
CHUNK = 128
TAPS = 4
EPSILON = 1e-05
THETA = 100000000000.0
NEG = -1e30
HIGHEST = lax.Precision.HIGHEST
BF = jnp.bfloat16
F32 = jnp.float32
VMEM_LIMIT = 48 * 1024 * 1024


def dot(left, right, dims=((1,), (0,))):
    return lax.dot_general(left, right, (dims, ((), ())), preferred_element_type=F32)


def dot_exact(left, right):
    return lax.dot_general(
        left, right, (((1,), (0,)), ((), ())), precision=HIGHEST, preferred_element_type=F32
    )


def sigmoid(values):
    return 1.0 / (1.0 + jnp.exp(-values))


def pick(low_half, table, first):
    return jnp.where(low_half, table[:, first : first + 1], table[:, first + 1 : first + 2])


def halves(low_half, tile):
    zero = jnp.zeros_like(tile)
    return jnp.concatenate(
        [jnp.where(low_half, tile, zero), jnp.where(low_half, zero, tile)], axis=0
    )


def ssd_tables(dt_raw, dt_bias, rate, emask, fmask, total, lower):
    step = jnp.log1p(jnp.exp(dt_raw + dt_bias))
    decay = dot_exact(lower, step * rate)
    last = decay[CHUNK - 1 : CHUNK, :]
    enter = jnp.exp(decay) * emask
    leave = jnp.exp(last - decay) * fmask
    whole = jnp.exp(last) * total
    return step, decay, enter, leave, whole


def conv_rows(buf, width, aux, taps, bias):
    result = bias + taps[0:1] * buf[8 : 8 + CHUNK, width]
    for k in range(1, TAPS):
        result = result + taps[k : k + 1] * (aux[:, k : k + 1] * buf[8 - k : 8 - k + CHUNK, width])
    return result


def ssd_forward_kernel(
    h_ref, z_ref, aux_ref, segrow_ref, xpar_ref, bcpar_ref, hpar_ref,
    gated_ref, scan_ref, start_ref, xbuf, pbuf, state,
):
    inner = z_ref.shape[1]
    pairs = inner // 128
    lane = lax.broadcasted_iota(jnp.int32, (CHUNK, 128), 1)
    sub = lax.broadcasted_iota(jnp.int32, (CHUNK, 128), 0)
    low_half = lane < 64

    @pl.when(pl.program_id(0) == 0)
    def _():
        xbuf[0:8, :] = jnp.zeros((8, inner), F32)
        pbuf[0:8, :] = jnp.zeros((8, 2 * STATE), F32)
        state[...] = jnp.zeros_like(state)

    xbuf[8 : 8 + CHUNK, :] = h_ref[:, :inner]
    pbuf[8 : 8 + CHUNK, :] = h_ref[:, inner : inner + 2 * STATE]
    aux = aux_ref[...]
    pre_pair = conv_rows(pbuf, slice(None), aux, bcpar_ref[0:4, :], bcpar_ref[4:5, :])
    act_pair = pre_pair * sigmoid(pre_pair)
    in_b = act_pair[:, :STATE].astype(BF)
    out_c = act_pair[:, STATE:].astype(BF)
    inter = dot(out_c, in_b, ((1,), (1,)))
    allowed = (sub >= lane) & (aux[:, 0:1] == segrow_ref[0])
    hide = jnp.where(allowed, 0.0, NEG)
    lower = (sub >= lane).astype(F32)
    emask = aux[:, 7:8]
    step, decay, enter, leave, whole = ssd_tables(
        h_ref[:, inner + 2 * STATE :], hpar_ref[0:1, :], hpar_ref[1:2, :],
        emask, aux[:, 8:9], emask[CHUNK - 1 : CHUNK, :], lower,
    )
    decay_t = decay.T
    for p in range(pairs):
        cols = slice(128 * p, 128 * p + 128)
        pre = conv_rows(xbuf, cols, aux, xpar_ref[0:4, cols], xpar_ref[4:5, cols])
        act = pre * sigmoid(pre)
        driven = (pick(low_half, step, 2 * p) * act).astype(BF)
        mixes = []
        for head in (2 * p, 2 * p + 1):
            gap = decay[:, head : head + 1] - decay_t[head : head + 1, :]
            mixes.append((inter * jnp.exp(gap + hide)).astype(BF))
        before = state[:, cols]
        start = before.astype(BF)
        start_ref[:, cols] = start
        scanned = dot(jnp.concatenate(mixes, axis=1), halves(low_half, driven))
        scanned = scanned + dot(out_c, start) * pick(low_half, enter, 2 * p)
        scanned = scanned + xpar_ref[5:6, cols] * act
        scan_ref[:, cols] = scanned.astype(scan_ref.dtype)
        gate = z_ref[:, cols].astype(F32)
        gated_ref[:, cols] = (scanned * (gate * sigmoid(gate))).astype(BF)
        sent = (pick(low_half, leave, 2 * p) * driven.astype(F32)).astype(BF)
        state[:, cols] = pick(low_half[0:1], whole, 2 * p) * before + dot(
            in_b, sent, ((0,), (0,))
        )
    xbuf[0:8, :] = xbuf[CHUNK : CHUNK + 8, :]
    pbuf[0:8, :] = pbuf[CHUNK : CHUNK + 8, :]


def ssd_forward(h1, z, aux, segrow, xpar, bcpar, hpar):
    length, inner = z.shape
    chunks = length // CHUNK
    width = h1.shape[1]
    whole = lambda arr: pl.BlockSpec(arr.shape, lambda c: (0,) * arr.ndim)
    rows = lambda cols: pl.BlockSpec((CHUNK, cols), lambda c: (c, 0))
    return pl.pallas_call(
        ssd_forward_kernel,
        grid=(chunks,),
        in_specs=[
            rows(width), rows(inner), rows(128),
            pl.BlockSpec((1, 1, CHUNK), lambda c: (c, 0, 0)),
            whole(xpar), whole(bcpar), whole(hpar),
        ],
        out_specs=[rows(inner), rows(inner), rows(inner)],
        out_shape=[
            jax.ShapeDtypeStruct((length, inner), BF),
            jax.ShapeDtypeStruct((length, inner), F32),
            jax.ShapeDtypeStruct((chunks * STATE, inner), BF),
        ],
        scratch_shapes=[
            pltpu.VMEM((CHUNK + 8, inner), F32),
            pltpu.VMEM((CHUNK + 8, 2 * STATE), F32),
            pltpu.VMEM((STATE, inner), F32),
        ],
        compiler_params=pltpu.CompilerParams(vmem_limit_bytes=VMEM_LIMIT),
        name="ssd_forward",
    )(h1, z, aux, segrow, xpar, bcpar, hpar)


def head_sums(low_half, tile):
    zero = jnp.zeros_like(tile)
    return (
        jnp.sum(jnp.where(low_half, tile, zero), axis=1, keepdims=True),
        jnp.sum(jnp.where(low_half, zero, tile), axis=1, keepdims=True),
    )


def ssd_backward_kernel(
    h_ref, prev_ref, z_ref, scan_ref, dgated_ref, start_ref, aux_ref, segrow_ref,
    xpar_ref, bcpar_ref, hpar_ref,
    dh_ref, dz_ref, xacc_ref, bcacc_ref, hacc_ref, xbuf, pbuf, dxbuf, dpbuf, dstate,
):
    inner = z_ref.shape[1]
    pairs = inner // 128
    lane = lax.broadcasted_iota(jnp.int32, (CHUNK, 128), 1)
    sub = lax.broadcasted_iota(jnp.int32, (CHUNK, 128), 0)
    low_half = lane < 64
    low_row = low_half[0:1]

    @pl.when(pl.program_id(0) == 0)
    def _():
        dxbuf[CHUNK : CHUNK + 8, :] = jnp.zeros((8, inner), F32)
        dpbuf[CHUNK : CHUNK + 8, :] = jnp.zeros((8, 2 * STATE), F32)
        dstate[...] = jnp.zeros_like(dstate)
        xacc_ref[...] = jnp.zeros_like(xacc_ref)
        bcacc_ref[...] = jnp.zeros_like(bcacc_ref)
        hacc_ref[...] = jnp.zeros_like(hacc_ref)

    xbuf[0:8, :] = prev_ref[:, :inner]
    xbuf[8 : 8 + CHUNK, :] = h_ref[:, :inner]
    pbuf[0:8, :] = prev_ref[:, inner : inner + 2 * STATE]
    pbuf[8 : 8 + CHUNK, :] = h_ref[:, inner : inner + 2 * STATE]
    aux = aux_ref[...]
    pre_pair = conv_rows(pbuf, slice(None), aux, bcpar_ref[0:4, :], bcpar_ref[4:5, :])
    sig_pair = sigmoid(pre_pair)
    act_pair = pre_pair * sig_pair
    in_b = act_pair[:, :STATE].astype(BF)
    out_c = act_pair[:, STATE:].astype(BF)
    inter_t = dot(in_b, out_c, ((1,), (1,)))
    allowed_t = (lane >= sub) & (aux[:, 0:1] == segrow_ref[0])
    hide_t = jnp.where(allowed_t, 0.0, NEG)
    lower = (sub >= lane).astype(F32)
    upper = (sub <= lane).astype(F32)
    strict = (sub > lane).astype(F32)
    emask = aux[:, 7:8]
    rate = hpar_ref[1:2, :]
    dt_full = h_ref[:, inner + 2 * STATE :] + hpar_ref[0:1, :]
    step, decay, enter, leave, whole = ssd_tables(
        h_ref[:, inner + 2 * STATE :], hpar_ref[0:1, :], rate,
        emask, aux[:, 8:9], emask[CHUNK - 1 : CHUNK, :], lower,
    )
    decay_t = decay.T
    zeros = jnp.zeros((CHUNK, 128), F32)
    grad_inter_t = zeros
    grad_b = zeros
    grad_c = zeros
    col_intra = zeros
    row_inter = zeros
    direct = zeros
    direct_inter = zeros
    across = jnp.zeros((1, 128), F32)
    row_list = []
    for p in range(pairs):
        cols = slice(128 * p, 128 * p + 128)
        pre = conv_rows(xbuf, cols, aux, xpar_ref[0:4, cols], xpar_ref[4:5, cols])
        sig = sigmoid(pre)
        act = pre * sig
        gate = z_ref[:, cols].astype(F32)
        sig_gate = sigmoid(gate)
        dgated = dgated_ref[:, cols]
        scanned = scan_ref[:, cols]
        dz_ref[:, cols] = (
            dgated * scanned * (sig_gate * (1.0 + gate * (1.0 - sig_gate)))
        ).astype(BF)
        dscan = (dgated * (gate * sig_gate)).astype(BF)
        dscan_f = dscan.astype(F32)
        step_p = pick(low_half, step, 2 * p)
        driven = (step_p * act).astype(BF)
        zero_b = jnp.zeros_like(driven)
        mixes = []
        for head in (2 * p, 2 * p + 1):
            gap = decay_t[head : head + 1, :] - decay[:, head : head + 1]
            damp = jnp.exp(gap + hide_t)
            mixed = inter_t * damp
            mixes.append(mixed.astype(BF))
            own = jnp.where(low_half == (head % 2 == 0), driven, zero_b)
            grad_mix = dot(own, dscan, ((1,), (1,)))
            grad_inter_t = grad_inter_t + grad_mix * damp
            flow = grad_mix * mixed
            row_list.append(jnp.sum(flow, axis=0, keepdims=True))
            col_intra = jnp.where(lane == head, jnp.sum(flow, axis=1, keepdims=True), col_intra)
        start = start_ref[:, cols]
        dst = dstate[:, cols]
        dst_b = dst.astype(BF)
        enter_p = pick(low_half, enter, 2 * p)
        leave_p = pick(low_half, leave, 2 * p)
        whole_p = pick(low_row, whole, 2 * p)
        from_inter = dot(in_b, dst_b) * leave_p
        ddriven = dot(jnp.concatenate(mixes, axis=1), halves(low_half, dscan)) + from_inter
        dact = xpar_ref[5:6, cols] * dscan_f + step_p * ddriven
        came = dot(out_c, start) * enter_p
        sums = (
            head_sums(low_half, act * ddriven),
            head_sums(low_half, act * from_inter),
            head_sums(low_half, dscan_f * came),
            head_sums(low_row, whole_p * jnp.sum(dst * start.astype(F32), axis=0, keepdims=True)),
        )
        for side in (0, 1):
            here = lane == 2 * p + side
            direct = jnp.where(here, sums[0][side], direct)
            direct_inter = jnp.where(here, sums[1][side], direct_inter)
            row_inter = jnp.where(here, sums[2][side], row_inter)
            across = jnp.where(here[0:1], sums[3][side], across)
        dcame = (enter_p * dscan_f).astype(BF)
        sent = (leave_p * driven.astype(F32)).astype(BF)
        grad_c = grad_c + dot(dcame, start, ((1,), (1,)))
        grad_b = grad_b + dot(sent, dst_b, ((1,), (1,)))
        dstate[:, cols] = whole_p * dst + dot(out_c, dcame, ((0,), (0,)))
        dpre = dact * (sig * (1.0 + pre * (1.0 - sig)))
        dxbuf[0:CHUNK, cols] = dpre
        dval = xpar_ref[0:1, cols] * dpre
        xacc_ref[0:1, cols] += jnp.sum(dpre * xbuf[8 : 8 + CHUNK, cols], axis=0, keepdims=True)
        for k in range(1, TAPS):
            dval = dval + xpar_ref[k : k + 1, cols] * (
                aux[:, 3 + k : 4 + k] * dxbuf[k : k + CHUNK, cols]
            )
            xacc_ref[k : k + 1, cols] += jnp.sum(
                dpre * (aux[:, k : k + 1] * xbuf[8 - k : 8 - k + CHUNK, cols]),
                axis=0, keepdims=True,
            )
        xacc_ref[4:5, cols] += jnp.sum(dpre, axis=0, keepdims=True)
        xacc_ref[5:6, cols] += jnp.sum(dscan_f * act, axis=0, keepdims=True)
        dh_ref[:, cols] = dval.astype(BF)
    dxbuf[CHUNK : CHUNK + 8, :] = dxbuf[0:8, :]
    grad_inter_b = grad_inter_t.astype(BF)
    grad_b = grad_b + dot(grad_inter_b, out_c)
    grad_c = grad_c + dot(grad_inter_b, in_b, ((0,), (0,)))
    grad_act = jnp.concatenate([grad_b, grad_c], axis=1)
    dpre = grad_act * (sig_pair * (1.0 + pre_pair * (1.0 - sig_pair)))
    dpbuf[0:CHUNK, :] = dpre
    dval = bcpar_ref[0:1, :] * dpre
    bcacc_ref[0:1, :] += jnp.sum(dpre * pbuf[8 : 8 + CHUNK, :], axis=0, keepdims=True)
    for k in range(1, TAPS):
        dval = dval + bcpar_ref[k : k + 1, :] * (
            aux[:, 3 + k : 4 + k] * dpbuf[k : k + CHUNK, :]
        )
        bcacc_ref[k : k + 1, :] += jnp.sum(
            dpre * (aux[:, k : k + 1] * pbuf[8 - k : 8 - k + CHUNK, :]), axis=0, keepdims=True
        )
    bcacc_ref[4:5, :] += jnp.sum(dpre, axis=0, keepdims=True)
    dh_ref[:, inner : inner + 2 * STATE] = dval.astype(BF)
    dpbuf[CHUNK : CHUNK + 8, :] = dpbuf[0:8, :]
    rows = jnp.concatenate(row_list + [jnp.zeros((CHUNK - 2 * pairs, 128), F32)], axis=0).T
    grad_decay = dot_exact(upper, rows - col_intra + row_inter) + across
    grad_decay = grad_decay + dot_exact(strict, step * direct_inter)
    dstep = direct + grad_decay * rate
    draw = dstep * sigmoid(dt_full)
    hacc_ref[0:1, :] += jnp.sum(draw, axis=0, keepdims=True)
    hacc_ref[1:2, :] += jnp.sum(grad_decay * step, axis=0, keepdims=True) * rate
    dh_ref[:, inner + 2 * STATE :] = draw.astype(BF)


def ssd_backward(h1, z, scan, dgated, start, aux, segrow, xpar, bcpar, hpar):
    length, inner = z.shape
    chunks = length // CHUNK
    width = h1.shape[1]
    whole = lambda arr: pl.BlockSpec(arr.shape, lambda c: (0,) * arr.ndim)
    rows = lambda cols: pl.BlockSpec((CHUNK, cols), lambda c: (chunks - 1 - c, 0))
    fixed = lambda r, cols: pl.BlockSpec((r, cols), lambda c: (0, 0))
    return pl.pallas_call(
        ssd_backward_kernel,
        grid=(chunks,),
        in_specs=[
            rows(width),
            pl.BlockSpec((8, width), lambda c: (jnp.maximum((chunks - 1 - c) * (CHUNK // 8) - 1, 0), 0)),
            rows(inner), rows(inner), rows(inner), rows(inner), rows(128),
            pl.BlockSpec((1, 1, CHUNK), lambda c: (chunks - 1 - c, 0, 0)),
            whole(xpar), whole(bcpar), whole(hpar),
        ],
        out_specs=[
            rows(width), rows(inner),
            fixed(8, inner), fixed(8, 2 * STATE), fixed(8, 128),
        ],
        out_shape=[
            jax.ShapeDtypeStruct((length, width), BF),
            jax.ShapeDtypeStruct((length, inner), BF),
            jax.ShapeDtypeStruct((8, inner), F32),
            jax.ShapeDtypeStruct((8, 2 * STATE), F32),
            jax.ShapeDtypeStruct((8, 128), F32),
        ],
        scratch_shapes=[
            pltpu.VMEM((CHUNK + 8, inner), F32),
            pltpu.VMEM((CHUNK + 8, 2 * STATE), F32),
            pltpu.VMEM((CHUNK + 8, inner), F32),
            pltpu.VMEM((CHUNK + 8, 2 * STATE), F32),
            pltpu.VMEM((STATE, inner), F32),
        ],
        compiler_params=pltpu.CompilerParams(vmem_limit_bytes=VMEM_LIMIT),
        name="ssd_backward",
    )(h1, h1, z, scan, dgated, start, aux, segrow, xpar, bcpar, hpar)


def segment_tables(seg):
    length = seg.shape[0]
    chunks = length // CHUNK
    value = seg.astype(F32)
    far = jnp.full((TAPS,), -1.0, F32)
    cols = [value]
    for k in range(1, TAPS):
        cols.append((value == jnp.concatenate([far[:k], value[:-k]])).astype(F32))
    for k in range(1, TAPS):
        cols.append((value == jnp.concatenate([value[k:], far[:k]])).astype(F32))
    by_chunk = value.reshape(chunks, CHUNK)
    ends = by_chunk[:, -1:]
    before = jnp.concatenate([far[:1, None], ends[:-1]], axis=0)
    cols.append((by_chunk == before).astype(F32).reshape(-1))
    cols.append((by_chunk == ends).astype(F32).reshape(-1))
    aux = jnp.stack(cols, axis=1)
    return jnp.pad(aux, ((0, 0), (0, 128 - aux.shape[1]))), by_chunk[:, None, :]


BLOCK = 256
REACH = 512


def rope_tables(length):
    position = jnp.arange(length).astype(F32)
    freqs = jnp.exp(-(jnp.arange(0, HD, 2).astype(F32) / HD) * math.log(THETA))
    angle = position[:, None] * freqs[None, :]
    cosine, sine = jnp.cos(angle), jnp.sin(angle)
    return (
        jnp.concatenate([cosine] * 4, axis=1),
        jnp.concatenate([-sine, sine, -sine, sine], axis=1),
    )


def turn(values, cosine, sine):
    lane = lax.broadcasted_iota(jnp.int32, values.shape, 1)
    swapped = jnp.where(
        lane % HD < HD // 2, pltpu.roll(values, 128 - HD // 2, 1), pltpu.roll(values, HD // 2, 1)
    )
    return values * cosine + swapped * sine


def attention_forward_kernel(
    qkv_ref, cos_ref, sin_ref, segcol_ref, segrow_ref, out_ref, turned_ref, lse_ref
):
    length = qkv_ref.shape[0]
    groups = KVHEADS
    cosine, sine = cos_ref[...], sin_ref[...]
    for t in range(groups + 1):
        cols = slice(128 * t, 128 * t + 128)
        turned_ref[:, cols] = turn(qkv_ref[:, cols].astype(F32), cosine, sine).astype(BF)
    key_at, value_at = 128 * groups, 128 * (groups + 1)
    lane = lax.broadcasted_iota(jnp.int32, (BLOCK, 128), 1)
    for b in range(length // BLOCK):
        rows = slice(b * BLOCK, (b + 1) * BLOCK)
        first = max(0, b * BLOCK - REACH)
        keys = slice(first, (b + 1) * BLOCK)
        many = (b + 1) * BLOCK - first
        at_row = lax.broadcasted_iota(jnp.int32, (BLOCK, many), 0) + b * BLOCK
        at_col = lax.broadcasted_iota(jnp.int32, (BLOCK, many), 1) + first
        allowed = (at_row >= at_col) & (segcol_ref[rows, 0:1] == segrow_ref[:, keys])
        lse = jnp.zeros((BLOCK, 128), F32)
        for g in range(groups):
            key = turned_ref[keys, key_at + 64 * g : key_at + 64 * g + 64]
            value = qkv_ref[keys, value_at + 64 * g : value_at + 64 * g + 64]
            parts = []
            for s in range(2):
                query = turned_ref[rows, 128 * g + 64 * s : 128 * g + 64 * s + 64]
                scores = dot(query, key, ((1,), (1,))) * HD ** (-0.5)
                scores = jnp.where(allowed, scores, NEG)
                peak = jnp.max(scores, axis=1, keepdims=True)
                weights = jnp.exp(scores - peak)
                total = jnp.sum(weights, axis=1, keepdims=True)
                probs = (weights * (1.0 / total)).astype(BF)
                parts.append(dot(probs, value))
                lse = jnp.where(lane == 2 * g + s, peak + jnp.log(total), lse)
            out_ref[rows, 128 * g : 128 * g + 128] = jnp.concatenate(parts, axis=1).astype(BF)
        lse_ref[rows, :] = lse


def attention_forward(qkv, cosine, sine, aux, segrow):
    length = qkv.shape[0]
    return pl.pallas_call(
        attention_forward_kernel,
        out_shape=[
            jax.ShapeDtypeStruct((length, 128 * KVHEADS), BF),
            jax.ShapeDtypeStruct((length, 128 * (KVHEADS + 1)), BF),
            jax.ShapeDtypeStruct((length, 128), F32),
        ],
        compiler_params=pltpu.CompilerParams(vmem_limit_bytes=VMEM_LIMIT),
        name="attention_forward",
    )(qkv, cosine, sine, aux, segrow)


def attention_backward_kernel(
    qkv_ref, turned_ref, datt_ref, lse_ref, delta_ref, cos_ref, sin_ref, segcol_ref, segrow_ref,
    dqkv_ref, dkey, dvalue,
):
    length = qkv_ref.shape[0]
    groups = KVHEADS
    key_at, value_at = 128 * groups, 128 * (groups + 1)
    dkey[...] = jnp.zeros_like(dkey)
    dvalue[...] = jnp.zeros_like(dvalue)
    for b in range(length // BLOCK):
        rows = slice(b * BLOCK, (b + 1) * BLOCK)
        first = max(0, b * BLOCK - REACH)
        keys = slice(first, (b + 1) * BLOCK)
        many = (b + 1) * BLOCK - first
        at_key = lax.broadcasted_iota(jnp.int32, (many, BLOCK), 0) + first
        at_row = lax.broadcasted_iota(jnp.int32, (many, BLOCK), 1) + b * BLOCK
        allowed = (at_row >= at_key) & (segcol_ref[keys, 0:1] == segrow_ref[:, rows])
        dquery = []
        for g in range(groups):
            key = turned_ref[keys, key_at + 64 * g : key_at + 64 * g + 64]
            value = qkv_ref[keys, value_at + 64 * g : value_at + 64 * g + 64]
            dk = jnp.zeros((many, HD), F32)
            dv = jnp.zeros((many, HD), F32)
            for s in range(2):
                head = 2 * g + s
                half = slice(128 * g + 64 * s, 128 * g + 64 * s + 64)
                query = turned_ref[rows, half]
                datt = datt_ref[rows, half]
                scores = dot(key, query, ((1,), (1,))) * HD ** (-0.5)
                probs = jnp.exp(jnp.where(allowed, scores, NEG) - lse_ref[head : head + 1, rows])
                dprobs = dot(value, datt, ((1,), (1,)))
                dscores = (probs * (dprobs - delta_ref[head : head + 1, rows])).astype(BF)
                dk = dk + dot(dscores, query)
                dv = dv + dot(probs.astype(BF), datt)
                dquery.append(dot(dscores, key, ((0,), (0,))) * HD ** (-0.5))
            dkey[keys, 64 * g : 64 * g + 64] += dk * HD ** (-0.5)
            dvalue[keys, 64 * g : 64 * g + 64] += dv
        for g in range(groups):
            tile = jnp.concatenate([dquery[2 * g], dquery[2 * g + 1]], axis=1)
            dqkv_ref[rows, 128 * g : 128 * g + 128] = turn(
                tile, cos_ref[rows, :], -sin_ref[rows, :]
            ).astype(BF)
    dqkv_ref[:, key_at : key_at + 128] = turn(dkey[...], cos_ref[...], -sin_ref[...]).astype(BF)
    dqkv_ref[:, value_at : value_at + 128] = dvalue[...].astype(BF)


def attention_backward(qkv, turned, datt, lse, delta, cosine, sine, aux, segrow):
    length = qkv.shape[0]
    return pl.pallas_call(
        attention_backward_kernel,
        out_shape=jax.ShapeDtypeStruct(qkv.shape, BF),
        scratch_shapes=[pltpu.VMEM((length, 128), F32), pltpu.VMEM((length, 128), F32)],
        compiler_params=pltpu.CompilerParams(vmem_limit_bytes=VMEM_LIMIT),
        name="attention_backward",
    )(qkv, turned, datt, lse, delta, cosine, sine, aux, segrow)


def core_swap(value):
    return lax.ppermute(value, "head", [(0, 1), (1, 0), (2, 3), (3, 2)])


def half_swap(value):
    return lax.ppermute(value, "head", [(0, 2), (2, 0), (1, 3), (3, 1)])


def half_groups(dp):
    return [[d * 4 + 2 * half + core for d in range(dp) for half in range(2)] for core in range(2)]


def ordered(is_first, mine, other, axis):
    return jnp.where(
        is_first,
        jnp.concatenate([mine, other], axis=axis),
        jnp.concatenate([other, mine], axis=axis),
    )


def gather(piece, dp, is_first):
    rows, cols = piece.shape
    both = lax.all_gather(
        piece, ("dp", "head"), axis=0, tiled=False, axis_index_groups=half_groups(dp)
    ).reshape(dp, 2, rows, cols)
    zero, one = both[:, 0], both[:, 1]
    mine = jnp.where(is_first, zero, one).reshape(dp * rows, cols)
    other = jnp.where(is_first, one, zero).reshape(dp * rows, cols)
    return mine, other


def scatter_sum(mine, other, dp, is_first):
    cols = mine.shape[1]
    rows = mine.shape[0] // dp
    mine = mine.astype(BF).reshape(dp, 1, rows, cols)
    other = other.astype(BF).reshape(dp, 1, rows, cols)
    both = ordered(is_first, mine, other, 1).reshape(dp * 2 * rows, cols)
    return lax.psum_scatter(
        both, ("dp", "head"), scatter_dimension=0, tiled=True, axis_index_groups=half_groups(dp)
    )


def core_sum(part):
    part = part.astype(BF)
    return part.astype(F32) + core_swap(part).astype(F32)


def wide(mine, other, width):
    return jnp.concatenate([mine[:, :width], other[:, :width]], axis=1)


def norm_back(grad, values, scale, gain):
    weighted = grad * gain
    inner = jnp.mean(weighted * values, axis=-1, keepdims=True)
    return scale * weighted - values * (scale * scale * scale * inner), jnp.sum(
        grad * (values * scale), axis=0
    )


def body(
    tokens, segments, cotangent, gain_in, mamba_gate_weight, mamba_input_weight, w_dt, w_bc,
    convolution_input_taps, convolution_input_bias, conv_bc, conv_bc_bias, dt_bias, a_log, d_skip,
    w_q, w_k, w_v, w_o, mamba_output_weight, gain_ffn, w_gate, w_up, w_down,
):
    length = segments.shape[1]
    width = tokens.shape[1]
    rows_here = mamba_gate_weight.shape[0]
    dp = width // rows_here
    inner = mamba_gate_weight.shape[1]
    heads = w_dt.shape[1]
    qcols = w_q.shape[1]
    hidden_cols = w_gate.shape[1]
    slot = lax.axis_index("head")
    half = slot // 2
    core = slot % 2
    is_first = half == 0
    seg = lax.dynamic_index_in_dim(segments, half, 0, keepdims=False)
    rows = lax.dynamic_slice_in_dim(tokens, half * length, length, 0).astype(F32)
    upstream = lax.dynamic_slice_in_dim(cotangent, half * length, length, 0)

    shared = jnp.concatenate([w_bc, w_k, w_v], axis=1).astype(BF)
    quarter = lax.dynamic_slice_in_dim(shared, slot * 128, 128, 1)
    short = lambda value: value.astype(BF)
    pad_dt = jnp.zeros((rows_here, 128 - heads), BF)
    piece1 = jnp.concatenate([short(mamba_input_weight), short(w_dt), pad_dt, quarter], axis=1)
    piece2 = jnp.concatenate([short(mamba_gate_weight), short(w_q)], axis=1)
    piece3 = jnp.concatenate([short(mamba_output_weight).T, short(w_o).T], axis=1)
    piece4 = jnp.concatenate([short(w_gate), short(w_up)], axis=1)
    piece5 = short(w_down).T
    full1 = gather(piece1, dp, is_first)
    full2 = gather(piece2, dp, is_first)
    full3 = gather(piece3, dp, is_first)
    full4 = gather(piece4, dp, is_first)
    full5 = gather(piece5, dp, is_first)

    at = inner + 128
    quarters = jnp.concatenate(
        [jnp.where(is_first, full1[0][:, at:], full1[1][:, at:]),
         jnp.where(is_first, full1[1][:, at:], full1[0][:, at:])], axis=1)
    others = core_swap(quarters)
    first_core = core == 0
    bc_full = jnp.concatenate(
        [jnp.where(first_core, quarters[:, :128], others[:, :128]),
         jnp.where(first_core, others[:, :128], quarters[:, :128])], axis=1)
    flip = lambda tile: jnp.where(is_first, tile, jnp.concatenate([tile[:, HD:], tile[:, :HD]], axis=1))
    key_full = flip(jnp.where(first_core, quarters[:, 128:], others[:, 128:]))
    value_full = flip(jnp.where(first_core, others[:, 128:], quarters[:, 128:]))
    dt_full = jnp.concatenate(
        [full1[0][:, inner : inner + heads], full1[1][:, inner : inner + heads],
         jnp.zeros((width, 128 - 2 * heads), BF)], axis=1)
    weight1 = jnp.concatenate([wide(*full1, inner), bc_full, dt_full], axis=1)
    weight_z = wide(*full2, inner)
    weight_qkv = jnp.concatenate([full2[0][:, inner:], full2[1][:, inner:], key_full, value_full], axis=1)
    weight_out = wide(*full3, inner)
    weight_o = jnp.concatenate([full3[0][:, inner:], full3[1][:, inner:]], axis=1)
    weight_gate = wide(*full4, hidden_cols)
    weight_up = jnp.concatenate([full4[0][:, hidden_cols:], full4[1][:, hidden_cols:]], axis=1)
    weight_down = jnp.concatenate(full5, axis=1)

    per_head = jnp.pad(jnp.stack([dt_bias, a_log, d_skip]), ((0, 5), (0, 128 - heads)))
    small = jnp.concatenate(
        [jnp.concatenate([convolution_input_taps, convolution_input_bias[None],
                          jnp.repeat(d_skip, HD)[None], jnp.zeros((2, inner), F32)], axis=0), per_head],
        axis=1)
    small_other = half_swap(small)
    xpar = jnp.concatenate([small[:, :inner], small_other[:, :inner]], axis=1)
    head_par = jnp.concatenate(
        [small[:2, inner : inner + heads], small_other[:2, inner : inner + heads],
         jnp.zeros((2, 128 - 2 * heads), F32)], axis=1)
    lane = jnp.arange(128) < 2 * heads
    hpar = jnp.concatenate(
        [head_par[:1], jnp.where(lane, -jnp.exp(head_par[1:]), 0.0), jnp.zeros((6, 128), F32)], axis=0)
    bcpar = jnp.concatenate([conv_bc, conv_bc_bias[None], jnp.zeros((3, conv_bc.shape[1]), F32)], axis=0)
    aux, segrow = segment_tables(seg)
    seg_line = aux[:, 0][None]
    cosine, sine = rope_tables(length)

    scale = lax.rsqrt(jnp.mean(rows * rows, axis=-1, keepdims=True) + EPSILON)
    normed = short(rows * scale * gain_in)
    h1 = dot(normed, weight1)
    z = short(dot(normed, weight_z))
    qkv = short(dot(normed, weight_qkv))
    gated, scan, start = ssd_forward(h1, z, aux, segrow, xpar, bcpar, hpar)
    attended, turned, lse = attention_forward(qkv, cosine, sine, aux, seg_line)
    mixed = dot(gated, weight_out, ((1,), (1,))) + dot(attended, weight_o, ((1,), (1,)))
    state = rows + core_sum(mixed)
    scale_ffn = lax.rsqrt(jnp.mean(state * state, axis=-1, keepdims=True) + EPSILON)
    normed_ffn = short(state * scale_ffn * gain_ffn)
    gate = dot(normed_ffn, weight_gate)
    up = dot(normed_ffn, weight_up)
    sig = jax.nn.sigmoid(gate)
    hidden = short(gate * sig * up)
    whole = core_sum(dot(hidden, weight_down, ((1,), (1,))))
    out_mine = short(state + whole)

    dhidden = dot(upstream, weight_down)
    dgate = short(dhidden * up * (sig * (1.0 + gate * (1.0 - sig))))
    dup = short(dhidden * (gate * sig))
    dnormed_ffn = core_sum(
        dot(dgate, weight_gate, ((1,), (1,))) + dot(dup, weight_up, ((1,), (1,))))
    cols = ((0,), (0,))
    grad_down = short(dot(upstream, hidden, cols))
    grad_gate = short(dot(normed_ffn, dgate, cols))
    grad_up = short(dot(normed_ffn, dup, cols))
    dstate_norm, grad_gain_ffn = norm_back(dnormed_ffn, state, scale_ffn, gain_ffn)
    dstate = upstream.astype(F32) + dstate_norm
    dmixed = short(dstate)

    split = lambda grad, size: (grad[:, :size], grad[:, size:])
    sent5 = scatter_sum(*split(grad_down, hidden_cols), dp, is_first)
    gate_m, gate_o = split(grad_gate, hidden_cols)
    up_m, up_o = split(grad_up, hidden_cols)
    sent4 = scatter_sum(
        jnp.concatenate([gate_m, up_m], axis=1), jnp.concatenate([gate_o, up_o], axis=1), dp, is_first)

    dgated = dot(dmixed, weight_out)
    datt = short(dot(dmixed, weight_o))
    grad_out = short(dot(dmixed, gated, cols))
    grad_o = short(dot(dmixed, attended, cols))
    out_m, out_o = split(grad_out, inner)
    o_m, o_o = split(grad_o, qcols)
    sent3 = scatter_sum(
        jnp.concatenate([out_m, o_m], axis=1), jnp.concatenate([out_o, o_o], axis=1), dp, is_first)
    delta = jnp.sum(
        (datt.astype(F32) * attended.astype(F32)).reshape(length, -1, HD), axis=-1).T
    delta = jnp.pad(delta, ((0, 8 - delta.shape[0]), (0, 0)))
    dqkv = attention_backward(
        qkv, turned, datt, lse[:, :8].T, delta, cosine, sine, aux, seg_line)
    dh1, dz, xacc, bcacc, hacc = ssd_backward(
        h1, z, scan, dgated, start, aux, segrow, xpar, bcpar, hpar)
    dnormed = core_sum(
        dot(dh1, weight1, ((1,), (1,)))
        + dot(dz, weight_z, ((1,), (1,)))
        + dot(dqkv, weight_qkv, ((1,), (1,))))
    grad1 = short(dot(normed, dh1, cols))
    grad_z = short(dot(normed, dz, cols))
    grad_qkv = short(dot(normed, dqkv, cols))
    drows, grad_gain_in = norm_back(dnormed, rows, scale, gain_in)
    grad_mine = short(dstate + drows)

    unflip = flip
    shared_grad = jnp.concatenate(
        [grad1[:, 2 * inner : 2 * inner + 2 * STATE],
         unflip(grad_qkv[:, 2 * qcols : 2 * qcols + 128]), unflip(grad_qkv[:, 2 * qcols + 128 :])], axis=1)
    quarter_rows = rows_here // 4
    by_slot = shared_grad.reshape(dp, 2, 2, quarter_rows, shared_grad.shape[1])
    to_keep = jnp.where(first_core, by_slot[:, :, 0], by_slot[:, :, 1])
    to_send = jnp.where(first_core, by_slot[:, :, 1], by_slot[:, :, 0])
    kept = short(to_keep.astype(F32) + core_swap(to_send).astype(F32))
    kept = kept.reshape(dp, 2, quarter_rows, 4, 128).swapaxes(2, 3).reshape(dp, 2, rows_here, 128)
    shared_m = jnp.where(is_first, kept[:, 0], kept[:, 1]).reshape(width, 128)
    shared_o = jnp.where(is_first, kept[:, 1], kept[:, 0]).reshape(width, 128)
    gains = jnp.stack([grad_gain_in, grad_gain_ffn], axis=1)
    dt_at = 2 * inner + 2 * STATE
    fill = jnp.zeros((width, 128 - heads - 2), BF)
    extra = lambda cols_dt: jnp.concatenate([cols_dt, short(gains), fill], axis=1)
    sent1 = scatter_sum(
        jnp.concatenate(
            [grad1[:, :inner], extra(grad1[:, dt_at : dt_at + heads]), shared_m], axis=1),
        jnp.concatenate(
            [grad1[:, inner : 2 * inner], extra(grad1[:, dt_at + heads : dt_at + 2 * heads]), shared_o],
            axis=1),
        dp, is_first)
    z_m, z_o = split(grad_z, inner)
    sent2 = scatter_sum(
        jnp.concatenate([z_m, grad_qkv[:, :qcols]], axis=1),
        jnp.concatenate([z_o, grad_qkv[:, qcols : 2 * qcols]], axis=1), dp, is_first)

    skip = xacc[5].reshape(2, heads, HD).sum(axis=-1)
    stretches = []
    for side in range(2):
        stretches.append(jnp.concatenate([
            xacc[:5, side * inner : (side + 1) * inner].reshape(-1),
            hacc[0, side * heads : (side + 1) * heads], hacc[1, side * heads : (side + 1) * heads],
            skip[side]]))
    stretch = stretches[0].shape[0]
    table = jnp.where(
        jnp.arange(4)[:, None] == slot, stretches[0][None],
        jnp.where(jnp.arange(4)[:, None] == (slot + 2) % 4, stretches[1][None], 0.0))
    vector = lax.psum(jnp.concatenate([table.reshape(-1), bcacc[:5].reshape(-1)]), ("dp", "head"))
    own = lax.dynamic_slice_in_dim(vector, slot * stretch, stretch, 0)
    taps = own[: 5 * inner].reshape(5, inner)
    per = own[5 * inner :].reshape(3, heads)
    place = lax.axis_index("dp") * 4 + slot
    bc_cols = conv_bc.shape[1] // (4 * dp)
    bc_own = lax.dynamic_slice_in_dim(
        vector[4 * stretch :].reshape(5, -1), place * bc_cols, bc_cols, 1)

    swap_out = half_swap(out_mine)
    swap_grad = half_swap(grad_mine)
    output = ordered(is_first, out_mine, swap_out, 0)
    grad_tokens = ordered(is_first, grad_mine, swap_grad, 0)

    sent1, sent2, sent3, sent4, sent5 = [v.astype(F32) for v in (sent1, sent2, sent3, sent4, sent5)]
    shared_own = sent1[:, inner + 128 :].reshape(4, quarter_rows, 128).swapaxes(0, 1).reshape(quarter_rows, -1)
    return (
        output,
        grad_tokens,
        sent1[:, inner + heads],
        sent2[:, :inner],
        sent1[:, :inner],
        sent1[:, inner : inner + heads],
        shared_own[:, : 2 * STATE],
        taps[:4],
        taps[4],
        bc_own[:4],
        bc_own[4],
        per[0],
        per[1],
        per[2],
        sent2[:, inner:],
        shared_own[:, 2 * STATE : 2 * STATE + 128],
        shared_own[:, 2 * STATE + 128 :],
        sent3[:, inner:].T,
        sent3[:, :inner].T,
        sent1[:, inner + heads + 1],
        sent4[:, :hidden_cols],
        sent4[:, hidden_cols:],
        sent5.T,
    )


def solution(mesh):
    in_specs = (
        P("dp", None),
        P("dp", None),
        P("dp", None),
        P(),
        P("dp", "head"),
        P("dp", "head"),
        P("dp", "head"),
        P("dp", None),
        P(None, "head"),
        P("head"),
        P(),
        P(),
        P("head"),
        P("head"),
        P("head"),
        P("dp", "head"),
        P("dp", None),
        P("dp", None),
        P("head", "dp"),
        P("head", "dp"),
        P(),
        P("dp", "head"),
        P("dp", "head"),
        P("head", "dp"),
    )
    out_specs = (
        P("dp", None),
        P("dp", None),
        P("dp"),
        P("dp", "head"),
        P("dp", "head"),
        P("dp", "head"),
        P(("dp", "head"), None),
        P(None, "head"),
        P("head"),
        P(None, ("dp", "head")),
        P(("dp", "head")),
        P("head"),
        P("head"),
        P("head"),
        P("dp", "head"),
        P(("dp", "head"), None),
        P(("dp", "head"), None),
        P("head", "dp"),
        P("head", "dp"),
        P("dp"),
        P("dp", "head"),
        P("dp", "head"),
        P("head", "dp"),
    )
    return jax.shard_map(body, mesh=mesh, in_specs=in_specs, out_specs=out_specs, check_vma=False)
```

time: 1720 us -> 890 us (0.52)
  waiting for transfers between devices: 699 us -> 261 us
  matrix products: 327 us -> 72.7 us
  other arithmetic: 230 us -> 86.8 us
  blocking collectives: 355 us -> 212 us
  Pallas kernels: 0 us -> 74.1 us
  local copies, waits for them, and re-layouts: 78.3 us -> 151 us
    reduce_scatter x8 -> x3, waiting for transfers between devices: 506 us -> 68.9 us  [scatter_sum(): lax.psum_scatter(both, ('dp', 'head'), scatter_dimension=0, tiled=True, a...]
    all_gather x9 -> x0, blocking collectives: 273 us -> none  [the longest x1 34.1 us: body(): lax.all_gather(w_bc.astype(jnp.bfloat16), 'dp', axis=0, tiled=True)]
    dot_general x110 -> x24, matrix products: 311 us -> 72.7 us  [dot(): lax.dot_general(left, right, (dims, ((), ())), preferred_element_type=F32)]
    all_gather x3 -> x5, waiting for transfers between devices: 0.02 us -> 192 us  [gather(): lax.all_gather(piece, ('dp', 'head'), axis=0, tiled=False, axis_index_gro...]
    psum x1, blocking collectives: 22.3 us -> 212 us  [body(): lax.psum(jnp.concatenate([table.reshape(-1), bcacc[:5].reshape(-1)]), ('d...]
    psum x3 -> x0, waiting for transfers between devices: 129 us -> none  [the longest x1 72.8 us: body(): lax.psum(for_sending(mix_part), 'head')]
    convert_element_type x50 -> x17, other arithmetic: 103 us -> 19.9 us  [the longest x10 18.8 us: body(): short = lambda value: value.astype(BF)]
    pallas_call x0 -> x4, Pallas kernels: none -> 74.1 us  [the longest x1 43 us: ssd_backward(): pl.pallas_call(ssd_backward_kernel, grid=(chunks,), in_specs=[rows(width)...]
  transfers between devices with their start and end apart: 18 -> 19, of which waited for: 9 -> 6; matrix products, arithmetic and copies ran while one was open for 34% -> 29% of each run, Pallas kernels for 0% -> 8%
where the time goes in v1:
time: 890 us; the launch traced here: 882 us
  waiting for transfers between devices  261 us (29%)
  blocking collectives  212 us (24%)
  local copies, waits for them, and re-layouts  151 us (17%)
  other arithmetic  86.8 us (10%)
  Pallas kernels  74.1 us (8%)
  matrix products  72.7 us (8%)
  between operations  16.2 us (2%)
    psum x1, blocking collectives, body(): lax.psum(jnp.concatenate([table.reshape(-1), bcacc[:5].reshape(-1)]), ('d...  212 us
    all_gather x5, waiting for transfers between devices, gather(): lax.all_gather(piece, ('dp', 'head'), axis=0, tiled=False, axis_index_gro...  192 us
    dot_general x24, matrix products, dot(): lax.dot_general(left, right, (dims, ((), ())), preferred_element_type=F32)  72.7 us
    reduce_scatter x3, waiting for transfers between devices, scatter_sum(): lax.psum_scatter(both, ('dp', 'head'), scatter_dimension=0, tiled=True, a...  68.9 us
    unnamed x187, local copies, waits for them, and re-layouts  62.5 us
    pallas_call x1, Pallas kernels, ssd_backward(): pl.pallas_call(ssd_backward_kernel, grid=(chunks,), in_specs=[rows(width)...  43 us
    select_n x6, other arithmetic, ordered(): jnp.where(is_first, jnp.concatenate([mine, other], axis=axis), jnp.concat...  20.5 us
    convert_element_type x10, other arithmetic, body(): short = lambda value: value.astype(BF)  18.8 us
  transfers between devices with their start and end apart: 19, of which 6 were waited for; matrix products, arithmetic and copies ran while one was open for 29% of the time, Pallas kernels for 8%

profile of v1, /device:TPU:0, one launch (start us, length us, event | category | flops | bytes accessed | tf_op | source)
XLA Modules:
  0.0 881.6 jit_solution(2432959630006732427)
XLA Ops:
  28.6 48.8 %all-gather.15.cloned.1.call-done = bf16[2048,512]{0,1:T(8,128)(2,1)} async-done(((bf16[128,512]{0,1:T(8,128)(2,1)}), bf16[2048,512]{0,1:T(8,128)(2,1)}) %all-gather.15.cloned.1.call-update) | async-done | bytes 2097168 | tf_op jit(solution)/shard_map/all_gather | solution.py:532
  81.8 7.0 fusion.66
  93.4 6.3 copy.285
  102.6 40.3 %all-gather.11.cloned.1.call-done = bf16[2048,640]{1,0:T(8,128)(2,1)} async-done(((bf16[128,640]{1,0:T(8,128)(2,1)}), bf16[2048,640]{1,0:T(8,128)(2,1)}) %all-gather.11.cloned.1.call-update) | async-done | bytes 2621456 | tf_op jit(solution)/shard_map/all_gather | solution.py:532
  147.9 58.0 %all-gather.13.cloned.1.call-done = bf16[2048,512]{1,0:T(8,128)(2,1)} async-done(((bf16[128,512]{1,0:T(8,128)(2,1)}), bf16[2048,512]{1,0:T(8,128)(2,1)}) %all-gather.13.cloned.1.call-update) | async-done | bytes 2097168 | tf_op jit(solution)/shard_map/all_gather | solution.py:532
  221.4 8.2 attention_forward.1
  233.9 5.2 concatenate.221
  239.1 7.4 fusion.56.h_ref.prev_ref
  246.6 13.9 %ssd_forward.1 = (bf16[1024,768]{1,0:T(8,128)(2,1)S(1)}, f32[1024,768]{1,0:T(8,128)}, bf16[1024,768]{1,0:T(8,128)(2,1)S(1)}) custom-call(f32[1024,1152]{1,0:T(8,128)} %fusion.56.h_ref.prev_ref, bf16[1024,768]{1,0:T(8,128)(2,1)S(1)} %convolution_convert_fusion.7.z_ref, f32[1024,128]{1,0:T(8,128)S(1)} %pad.16.aux_ref.segcol_ref, ...), custom_call_target="tpu_custom_call" | custom-call | tf_op jit(solution)/shard_map/ssd_forward/pallas_call | solution.py:132
  264.4 6.0 all-gather.19.cloned.1.call-done
  274.8 6.9 fusion.63
  281.8 5.8 copy.286
  287.6 5.8 copy.287
  307.8 39.3 %all-gather.17.cloned.1.call-done = bf16[2048,1024]{1,0:T(8,128)(2,1)} async-done(((bf16[128,1024]{1,0:T(8,128)(2,1)}), bf16[2048,1024]{1,0:T(8,128)(2,1)}) %all-gather.17.cloned.1.call-update) | async-done | bytes 4194320 | tf_op jit(solution)/shard_map/all_gather | solution.py:532
  353.7 6.0 multiply_convert_fusion
  387.9 5.0 multiply_reduce_fusion
  413.5 9.0 %attention_backward.1 = bf16[1024,512]{1,0:T(8,128)(2,1)S(1)} custom-call(bf16[1024,512]{1,0:T(8,128)(2,1)S(1)} %copy-done.1, bf16[1024,384]{1,0:T(8,128)(2,1)S(1)} %copy-done.11, bf16[1024,256]{1,0:T(8,128)(2,1)S(1)} %copy-done.5, f32[8,1024]{1,0:T(8,128)S(1)} %slice_bitcast_fusion.6.lse_ref, f32[8,1024]{1,0:T(8,128)S(1)} %pad.18.delta_ref, ...), custom_call_target="tpu_custom_call" | custom-call | tf_op jit(solution)/shard_map/attention_backward/pallas_call | solution.py:501
  426.8 5.6 fusion.19.dgated_ref
  432.4 43.0 %ssd_backward.1 = (bf16[1024,1152]{1,0:T(8,128)(2,1)}, bf16[1024,768]{1,0:T(8,128)(2,1)S(1)}, f32[8,768]{1,0:T(8,128)S(1)}, f32[8,256]{1,0:T(8,128)S(1)}, f32[8,128]{1,0:T(8,128)S(1)}) custom-call(f32[1024,1152]{1,0:T(8,128)} %fusion.56.h_ref.prev_ref, f32[1024,1152]{1,0:T(8,128)} %fusion.56.h_ref.prev_ref, ...), custom_call_target="tpu_custom_call" | custom-call | tf_op jit(solution)/shard_map/ssd_backward/pallas_call | solution.py:326
  502.4 6.8 copy.261
  552.5 9.8 %fusion.8 = (bf16[1024,1024]{1,0:T(8,128)(2,1)}, bf16[1024,1024]{1,0:T(8,128)(2,1)}) fusion(bf16[1024,1024]{1,0:T(8,128)(2,1)} %collective-permute-done.6, bf16[1024,1024]{1,0:T(8,128)(2,1)S(1)} %add_convert_fusion, f32[1024]{0:T(1024)S(1)} %fusion.29, f32[1024]{0:T(1024)S(1)} %copy-done.72, f32[1024]{0:T(1024)S(1)} %add_rsqrt_fusion.1, ...), kind=kLoop, calls=%fused_computation.13 | loop fusion | flops 25165824 | bytes 25190404 | tf_op jit(solution)/shard_map/convert_element_type | solution.py:592
  564.9 212.2 %psum.7 = f32[9032]{0:T(1024)S(1)} all-reduce(f32[9032]{0:T(1024)S(1)} %pad_maximum_fusion.29), channel_id=1, replica_groups=mesh['dp'=8,'head'=4] {'dp','head'}, use_global_device_ids=true, to_apply=%region_10.11 | all-reduce | flops 9032 | bytes 72256 | tf_op jit(solution)/shard_map/psum | solution.py:749
  787.4 4.8 maximum_select_fusion.1
  798.8 68.8 %reduce-scatter.10.cloned.1.call-done = bf16[128,640]{1,0:T(8,128)(2,1)} async-done(((bf16[2048,640]{1,0:T(8,128)(2,1)}), bf16[128,640]{1,0:T(8,128)(2,1)}) %reduce-scatter.10.cloned.1.call-update) | async-done | bytes 163856 | tf_op jit(solution)/shard_map/reduce_scatter | solution.py:547
  (427 shorter events, 235.3 us)
Async XLA Ops:
  7.3 12.9 %copy-start.59 = (f32[128,512]{1,0:T(8,128)S(1)}, f32[128,512]{1,0:T(8,128)}, u32[]{:S(2)}) copy-start(f32[128,512]{1,0:T(8,128)} %param.45) | copy-start | bytes 786436
  7.3 12.9 %copy-start.60 = (f32[128,512]{1,0:T(8,128)S(1)}, f32[128,512]{1,0:T(8,128)}, u32[]{:S(2)}) copy-start(f32[128,512]{1,0:T(8,128)} %param.46) | copy-start | bytes 786436
  7.3 70.1 %all-gather.15.cloned.1.call-start = ((), (), s32[]{:S(2)}) async-start(), calls=%async_computation.10 | async-start | bytes 2228224 | tf_op jit(solution)/shard_map/all_gather | solution.py:532
  10.0 132.9 %all-gather.11.cloned.1.call-start = ((), (), s32[]{:S(2)}) async-start(), calls=%async_computation.8 | async-start | bytes 2785280 | tf_op jit(solution)/shard_map/all_gather | solution.py:532
  15.3 190.6 %all-gather.13.cloned.1.call-start = ((), (), s32[]{:S(2)}) async-start(), calls=%async_computation.9 | async-start | bytes 2228224 | tf_op jit(solution)/shard_map/all_gather | solution.py:532
  16.1 254.3 %all-gather.19.cloned.1.call-start = ((), (), s32[]{:S(2)}) async-start(), calls=%async_computation.12 | async-start | bytes 2228224 | tf_op jit(solution)/shard_map/all_gather | solution.py:532
  16.9 330.2 %all-gather.17.cloned.1.call-start = ((), (), s32[]{:S(2)}) async-start(), calls=%async_computation.11 | async-start | bytes 4456448 | tf_op jit(solution)/shard_map/all_gather | solution.py:532
  17.1 11.2 %collective-permute-start.1 = (f32[8,512]{1,0:T(8,128)S(1)}, f32[8,512]{1,0:T(8,128)S(1)}, u32[]{:S(2)}, u32[]{:S(2)}) collective-permute-start(f32[8,512]{1,0:T(8,128)S(1)} %pad_maximum_fusion.31), channel_id=1, source_target_pairs={{0,2},{2,0},{1,3},{3,1},{4,6},{6,4},{5,7},{7,5},{8,10},{10,8},{9,1... | collective-permute-start | bytes 49160 | tf_op jit(solution)/shard_map/ppermute | solution.py:515
  21.0 759.3 %reduce-scatter.18.cloned.1.call-start = ((), (), s32[]{:S(2)}) async-start(), calls=%async_computation.14 | async-start | bytes 2228224
  147.9 69.6 %collective-permute-start = (bf16[1024,256]{1,0:T(8,128)(2,1)}, bf16[1024,256]{1,0:T(8,128)(2,1)}, u32[]{:S(2)}, u32[]{:S(2)}) collective-permute-start(bf16[1024,256]{1,0:T(8,128)(2,1)} %pad_maximum_fusion.17), channel_id=1, source_target_pairs={{0,1},{1,0},{2,3},{3,2},{4,5},{5,4},{6,7},{7,6},{8,9},{9,8},{10,11... | collective-permute-start | bytes 1572872 | tf_op jit(solution)/shard_map/ppermute | solution.py:511
  246.6 13.9 %copy-start.56 = (bf16[1024,384]{1,0:T(8,128)(2,1)S(1)}, bf16[1024,384]{1,0:T(8,128)(2,1)}, u32[]{:S(2)}) copy-start(bf16[1024,384]{1,0:T(8,128)(2,1)} %slice.509) | copy-start | bytes 2359300
  246.6 13.9 %copy-start.57 = (bf16[1024,384]{1,0:T(8,128)(2,1)S(1)}, bf16[1024,384]{1,0:T(8,128)(2,1)}, u32[]{:S(2)}) copy-start(bf16[1024,384]{1,0:T(8,128)(2,1)} %slice.508) | copy-start | bytes 2359300
  264.4 36.3 %collective-permute-start.2 = (bf16[1024,1024]{1,0:T(8,128)(2,1)}, bf16[1024,1024]{1,0:T(8,128)(2,1)}, u32[]{:S(2)}, u32[]{:S(2)}) collective-permute-start(bf16[1024,1024]{1,0:T(8,128)(2,1)} %add_convert_fusion.3), channel_id=1, source_target_pairs={{0,1},{1,0},{2,3},{3,2},{4,5},{5,4},{6,7},{7,6},{8,9},{9,8},{10,11... | collective-permute-start | bytes 6291464 | tf_op jit(solution)/shard_map/ppermute | solution.py:511
  365.8 22.1 %collective-permute-start.5 = (bf16[1024,1024]{1,0:T(8,128)(2,1)}, bf16[1024,1024]{1,0:T(8,128)(2,1)}, u32[]{:S(2)}, u32[]{:S(2)}) collective-permute-start(bf16[1024,1024]{1,0:T(8,128)(2,1)} %add_convert_fusion.1), channel_id=1, source_target_pairs={{0,1},{1,0},{2,3},{3,2},{4,5},{5,4},{6,7},{7,6},{8,9},{9,8},{10,11... | collective-permute-start | bytes 6291464 | tf_op jit(solution)/shard_map/ppermute | solution.py:511
  387.8 394.1 %reduce-scatter.16.cloned.1.call-start = ((), (), s32[]{:S(2)}) async-start(), calls=%async_computation.13 | async-start | bytes 2228224
  432.4 43.0 %copy-start.22 = (bf16[2048,1024]{1,0:T(8,128)(2,1)S(1)}, bf16[2048,1024]{1,0:T(8,128)(2,1)}, u32[]{:S(2)}) copy-start(bf16[2048,1024]{1,0:T(8,128)(2,1)} %param.24) | copy-start | bytes 12582916
  485.4 297.7 %reduce-scatter.12.cloned.1.call-start = ((), (), s32[]{:S(2)}) async-start(), calls=%async_computation.6 | async-start | bytes 2228224 | tf_op jit(solution)/shard_map/reduce_scatter | solution.py:547
  488.1 308.9 %reduce-scatter.14.cloned.1.call-start = ((), (), s32[]{:S(2)}) async-start(), calls=%async_computation.7 | async-start | bytes 4456448 | tf_op jit(solution)/shard_map/reduce_scatter | solution.py:547
  509.3 358.4 %reduce-scatter.10.cloned.1.call-start = ((), (), s32[]{:S(2)}) async-start(), calls=%async_computation.5 | async-start | bytes 2785280 | tf_op jit(solution)/shard_map/reduce_scatter | solution.py:547
  518.8 15.9 %collective-permute-start.6 = (bf16[1024,1024]{1,0:T(8,128)(2,1)S(1)}, bf16[1024,1024]{1,0:T(8,128)(2,1)}, u32[]{:S(2)}, u32[]{:S(2)}) collective-permute-start(bf16[1024,1024]{1,0:T(8,128)(2,1)S(1)} %add_convert_fusion), channel_id=1, source_target_pairs={{0,1},{1,0},{2,3},{3,2},{4,5},{5,4},{6,7},{7,6},{8,9},{9,8},{10,11... | collective-permute-start | bytes 6291464 | tf_op jit(solution)/shard_map/ppermute | solution.py:511
  523.1 29.4 %collective-permute-start.3 = (bf16[1024,1024]{1,0:T(8,128)(2,1)}, bf16[1024,1024]{1,0:T(8,128)(2,1)}, u32[]{:S(2)}, u32[]{:S(2)}) collective-permute-start(bf16[1024,1024]{1,0:T(8,128)(2,1)} %convolution_convert_fusion.4), channel_id=1, source_target_pairs={{0,1},{1,0},{2,3},{3,2},{4,5},{5,4},{6,7},{7,6},{8,9},{9,8},{10,11... | collective-permute-start | bytes 6291464 | tf_op jit(solution)/shard_map/ppermute | solution.py:511
  527.6 2.9 collective-permute-start.8
  562.3 225.1 %collective-permute-start.7 = (bf16[1024,1024]{1,0:T(8,128)(2,1)}, bf16[1024,1024]{1,0:T(8,128)(2,1)S(1)}, u32[]{:S(2)}, u32[]{:S(2)}) collective-permute-start(bf16[1024,1024]{1,0:T(8,128)(2,1)} %get-tuple-element.171), channel_id=1, source_target_pairs={{0,2},{2,0},{1,3},{3,1},{4,6},{6,4},{5,7},{7,5},{8,10},{10,8},{9,1... | collective-permute-start | bytes 6291464 | tf_op jit(solution)/shard_map/ppermute | solution.py:515
  564.0 228.2 %collective-permute-start.4 = (bf16[1024,1024]{1,0:T(8,128)(2,1)}, bf16[1024,1024]{1,0:T(8,128)(2,1)}, u32[]{:S(2)}, u32[]{:S(2)}) collective-permute-start(bf16[1024,1024]{1,0:T(8,128)(2,1)} %get-tuple-element.172), channel_id=1, source_target_pairs={{0,2},{2,0},{1,3},{3,1},{4,6},{6,4},{5,7},{7,5},{8,10},{10,8},{9,1... | collective-permute-start | bytes 6291464 | tf_op jit(solution)/shard_map/ppermute | solution.py:515
  (80 other events, 300.1 us)
Sparse Core Ops, SparseCore 0:
  11.4 65.9 all-gather.14
  80.7 62.1 all-gather.10
  146.2 59.6 all-gather.12
  208.5 61.8 all-gather.18
  273.0 73.9 all-gather.16
  388.0 79.2 reduce-scatter.17
  485.5 79.3 reduce-scatter.15
  567.2 90.4 reduce-scatter.11
  660.0 123.9 reduce-scatter.13
  786.2 81.4 reduce-scatter.9

commit v2 on v1

v2 whole, which is shorter than its diff:
```python
import functools
import math

import jax
import jax.numpy as jnp
from jax import lax
from jax.experimental import pallas as pl
from jax.experimental.pallas import tpu as pltpu
from jax.sharding import PartitionSpec as P

QHEADS = 8
KVHEADS = 2
HD = 64
STATE = 128
CHUNK = 128
TAPS = 4
EPSILON = 1e-05
THETA = 100000000000.0
NEG = -1e30
HIGHEST = lax.Precision.HIGHEST
BF = jnp.bfloat16
F32 = jnp.float32
VMEM_LIMIT = 48 * 1024 * 1024


def dot(left, right, dims=((1,), (0,))):
    return lax.dot_general(left, right, (dims, ((), ())), preferred_element_type=F32)


def dot_exact(left, right):
    return lax.dot_general(
        left, right, (((1,), (0,)), ((), ())), precision=HIGHEST, preferred_element_type=F32
    )


def sigmoid(values):
    return 0.5 + 0.5 * jnp.tanh(0.5 * values)


def pick(low_half, table, first):
    return jnp.where(low_half, table[:, first : first + 1], table[:, first + 1 : first + 2])


def halves(low_half, tile):
    zero = jnp.zeros_like(tile)
    return jnp.concatenate(
        [jnp.where(low_half, tile, zero), jnp.where(low_half, zero, tile)], axis=0
    )


def ssd_tables(dt_raw, dt_bias, rate, emask, fmask, total, lower):
    step = jnp.log1p(jnp.exp(dt_raw + dt_bias))
    decay = dot_exact(lower, step * rate)
    last = decay[CHUNK - 1 : CHUNK, :]
    enter = jnp.exp(decay) * emask
    leave = jnp.exp(last - decay) * fmask
    whole = jnp.exp(last) * total
    return step, decay, enter, leave, whole


def shifted_rows(buf, cols, keeps):
    return [keep * buf[8 - k : 8 - k + CHUNK, cols] for k, keep in enumerate(keeps, 1)]


def conv_rows(now, shifted, taps, bias):
    result = bias + taps[0:1] * now
    for k, earlier in enumerate(shifted, 1):
        result = result + taps[k : k + 1] * earlier
    return result


def column(table, at):
    return jnp.broadcast_to(table[:, at : at + 1], (table.shape[0], 128))


def wide_column(tile):
    return jnp.concatenate([tile, tile], axis=1)


def head_lanes(inner):
    head = lax.broadcasted_iota(jnp.int32, (128, inner), 0)
    channel = lax.broadcasted_iota(jnp.int32, (128, inner), 1)
    return (head == channel // 64).astype(BF)


def spread(table, lanes2):
    high = table.astype(BF)
    rest = (table - high.astype(F32)).astype(BF)
    return dot(jnp.concatenate([high, rest], axis=1), lanes2)


def place_of(cols, inner):
    return slice(cols.start + 128 * (2 * cols.start // inner), cols.stop + 128 * (2 * cols.start // inner))


def steps_of(h_ref, inner, lane, heads):
    mid = inner // 2
    mine, other = h_ref[:, mid : mid + 128], h_ref[:, inner + 128 :]
    return jnp.where(lane < heads, mine, jnp.where(lane < 2 * heads, other, 0.0))


def ssd_forward_kernel(
    h_ref, pair_ref, z_ref, aux_ref, segrow_ref, xpar_ref, bcpar_ref, hpar_ref,
    gated_ref, scan_ref, start_ref, xbuf, pbuf, state, lanes2, step_s, enter_s, leave_s,
):
    inner = z_ref.shape[1]
    pairs = inner // 128
    lane = lax.broadcasted_iota(jnp.int32, (CHUNK, 128), 1)
    sub = lax.broadcasted_iota(jnp.int32, (CHUNK, 128), 0)
    low_half = lane < 64

    @pl.when(pl.program_id(0) == 0)
    def _():
        xbuf[0:8, :] = jnp.zeros((8, inner), F32)
        pbuf[0:8, :] = jnp.zeros((8, 2 * STATE), F32)
        state[...] = jnp.zeros_like(state)
        lanes2[0:128, :] = head_lanes(inner)
        lanes2[128:256, :] = head_lanes(inner)

    for first in (0, inner // 2):
        cols = slice(first, first + inner // 2)
        xbuf[8 : 8 + CHUNK, cols] = h_ref[:, place_of(cols, inner)]
    pbuf[8 : 8 + CHUNK, :] = pair_ref[...]
    aux = aux_ref[...]
    keeps = [column(aux, k) for k in range(1, TAPS)]
    pre_pair = conv_rows(
        pbuf[8 : 8 + CHUNK, :], shifted_rows(pbuf, slice(None), [wide_column(v) for v in keeps]),
        bcpar_ref[0:4, :], bcpar_ref[4:5, :])
    act_pair = pre_pair * sigmoid(pre_pair)
    in_b = act_pair[:, :STATE].astype(BF)
    out_c = act_pair[:, STATE:].astype(BF)
    inter = dot(out_c, in_b, ((1,), (1,)))
    allowed = (sub >= lane) & (column(aux, 0) == segrow_ref[0])
    hide = jnp.where(allowed, 0.0, NEG)
    lower = (sub >= lane).astype(F32)
    emask = aux[:, 7:8]
    step, decay, enter, leave, whole = ssd_tables(
        steps_of(h_ref, inner, lane, pairs), hpar_ref[0:1, :], hpar_ref[1:2, :],
        emask, aux[:, 8:9], emask[CHUNK - 1 : CHUNK, :], lower,
    )
    step_s[...] = spread(step, lanes2[...])
    enter_s[...] = spread(enter, lanes2[...])
    leave_s[...] = spread(leave, lanes2[...])
    decay_t = decay.T
    start = state[...].astype(BF)
    start_ref[...] = start
    enter_s[...] = dot(out_c, start) * enter_s[...]
    for p in range(pairs):
        cols = slice(128 * p, 128 * p + 128)
        pre = conv_rows(
            xbuf[8 : 8 + CHUNK, cols], shifted_rows(xbuf, cols, keeps),
            xpar_ref[0:4, cols], xpar_ref[4:5, cols])
        act = pre * sigmoid(pre)
        driven = (step_s[:, cols] * act).astype(BF)
        mixes = []
        for head in (2 * p, 2 * p + 1):
            gap = column(decay, head) - decay_t[head : head + 1, :]
            mixes.append((inter * jnp.exp(gap + hide)).astype(BF))
        scanned = dot(jnp.concatenate(mixes, axis=1), halves(low_half, driven))
        scanned = scanned + enter_s[:, cols] + xpar_ref[5:6, cols] * act
        scan_ref[:, cols] = scanned.astype(scan_ref.dtype)
        gate = z_ref[:, cols].astype(F32)
        gated_ref[:, cols] = (scanned * (gate * sigmoid(gate))).astype(BF)
        sent = (leave_s[:, cols] * driven.astype(F32)).astype(BF)
        state[:, cols] = pick(low_half[0:1], whole, 2 * p) * state[:, cols] + dot(
            in_b, sent, ((0,), (0,))
        )
    xbuf[0:8, :] = xbuf[CHUNK : CHUNK + 8, :]
    pbuf[0:8, :] = pbuf[CHUNK : CHUNK + 8, :]


def ssd_forward(h1, pair, z, aux, segrow, xpar, bcpar, hpar):
    length, inner = z.shape
    chunks = length // CHUNK
    width = h1.shape[1]
    whole = lambda arr: pl.BlockSpec(arr.shape, lambda c: (0,) * arr.ndim)
    rows = lambda cols: pl.BlockSpec((CHUNK, cols), lambda c: (c, 0))
    return pl.pallas_call(
        ssd_forward_kernel,
        grid=(chunks,),
        in_specs=[
            rows(width), rows(2 * STATE), rows(inner), rows(128),
            pl.BlockSpec((1, 1, CHUNK), lambda c: (c, 0, 0)),
            whole(xpar), whole(bcpar), whole(hpar),
        ],
        out_specs=[rows(inner), rows(inner), rows(inner)],
        out_shape=[
            jax.ShapeDtypeStruct((length, inner), BF),
            jax.ShapeDtypeStruct((length, inner), BF),
            jax.ShapeDtypeStruct((chunks * STATE, inner), BF),
        ],
        scratch_shapes=[
            pltpu.VMEM((CHUNK + 8, inner), F32),
            pltpu.VMEM((CHUNK + 8, 2 * STATE), F32),
            pltpu.VMEM((STATE, inner), F32),
            pltpu.VMEM((256, inner), BF),
            pltpu.VMEM((CHUNK, inner), F32),
            pltpu.VMEM((CHUNK, inner), F32),
            pltpu.VMEM((CHUNK, inner), F32),
        ],
        compiler_params=pltpu.CompilerParams(vmem_limit_bytes=VMEM_LIMIT),
        name="ssd_forward",
    )(h1, pair, z, aux, segrow, xpar, bcpar, hpar)


def ssd_backward_kernel(
    h_ref, prev_ref, pair_ref, pair_prev_ref, z_ref, dgated_ref, start_ref, aux_ref,
    segrow_ref, xpar_ref, bcpar_ref, hpar_ref,
    dh_ref, dpair_ref, xacc_ref, bcacc_ref, hacc_ref,
    xbuf, pbuf, dxbuf, dpbuf, dstate, lanes2, step_s, enter_s, leave_s, came_s, dcame_s, sent_s,
    direct_s, inter_s, row_s, across_s,
):
    inner = z_ref.shape[1]
    pairs = inner // 128
    lane = lax.broadcasted_iota(jnp.int32, (CHUNK, 128), 1)
    sub = lax.broadcasted_iota(jnp.int32, (CHUNK, 128), 0)
    low_half = lane < 64
    low_row = low_half[0:1]

    @pl.when(pl.program_id(0) == 0)
    def _():
        dxbuf[CHUNK : CHUNK + 8, :] = jnp.zeros((8, inner), F32)
        dpbuf[CHUNK : CHUNK + 8, :] = jnp.zeros((8, 2 * STATE), F32)
        dstate[...] = jnp.zeros_like(dstate)
        xacc_ref[...] = jnp.zeros_like(xacc_ref)
        bcacc_ref[...] = jnp.zeros_like(bcacc_ref)
        hacc_ref[...] = jnp.zeros_like(hacc_ref)
        across_s[...] = jnp.zeros_like(across_s)
        lanes2[0:128, :] = head_lanes(inner)
        lanes2[128:256, :] = head_lanes(inner)

    for first in (0, inner // 2):
        cols = slice(first, first + inner // 2)
        xbuf[0:8, cols] = prev_ref[:, place_of(cols, inner)]
        xbuf[8 : 8 + CHUNK, cols] = h_ref[:, place_of(cols, inner)]
    pbuf[0:8, :] = pair_prev_ref[...]
    pbuf[8 : 8 + CHUNK, :] = pair_ref[...]
    aux = aux_ref[...]
    keeps = [column(aux, k) for k in range(1, TAPS)]
    later = [column(aux, 3 + k) for k in range(1, TAPS)]
    shifted_pair = shifted_rows(pbuf, slice(None), [wide_column(v) for v in keeps])
    pre_pair = conv_rows(
        pbuf[8 : 8 + CHUNK, :], shifted_pair, bcpar_ref[0:4, :], bcpar_ref[4:5, :])
    sig_pair = sigmoid(pre_pair)
    act_pair = pre_pair * sig_pair
    in_b = act_pair[:, :STATE].astype(BF)
    out_c = act_pair[:, STATE:].astype(BF)
    inter_t = dot(in_b, out_c, ((1,), (1,)))
    allowed_t = (lane >= sub) & (column(aux, 0) == segrow_ref[0])
    hide_t = jnp.where(allowed_t, 0.0, NEG)
    lower = sub >= lane
    emask = aux[:, 7:8]
    rate = hpar_ref[1:2, :]
    dt_raw = steps_of(h_ref, inner, lane, pairs)
    step, decay, enter, leave, whole = ssd_tables(
        dt_raw, hpar_ref[0:1, :], rate,
        emask, aux[:, 8:9], emask[CHUNK - 1 : CHUNK, :], lower.astype(F32),
    )
    step_s[...] = spread(step, lanes2[...])
    enter_s[...] = spread(enter, lanes2[...])
    leave_s[...] = spread(leave, lanes2[...])
    came_s[...] = dot(out_c, start_ref[...]) * enter_s[...]
    leave_b = leave_s[...]
    row_s[...] = (dot(in_b, dstate[...].astype(BF)) * leave_b).astype(BF)
    decay_t = decay.T
    lower_b = lower.astype(BF)
    grad_inter_t = jnp.zeros((CHUNK, 128), F32)
    row_list = []
    for p in range(pairs):
        cols = slice(128 * p, 128 * p + 128)
        shifted = shifted_rows(xbuf, cols, keeps)
        now = xbuf[8 : 8 + CHUNK, cols]
        pre = conv_rows(now, shifted, xpar_ref[0:4, cols], xpar_ref[4:5, cols])
        sig = sigmoid(pre)
        act = pre * sig
        gate = z_ref[:, cols].astype(F32)
        dscan = (dgated_ref[:, cols].astype(F32) * (gate * sigmoid(gate))).astype(BF)
        dscan_f = dscan.astype(F32)
        step_p = step_s[:, cols]
        driven = (step_p * act).astype(BF)
        zero_b = jnp.zeros_like(driven)
        mixes = []
        for head in (2 * p, 2 * p + 1):
            gap = decay_t[head : head + 1, :] - column(decay, head)
            damp = jnp.exp(gap + hide_t)
            mixed = inter_t * damp
            mixes.append(mixed.astype(BF))
            own = jnp.where(low_half == (head % 2 == 0), driven, zero_b)
            grad_mix = dot(own, dscan, ((1,), (1,)))
            grad_inter_t = grad_inter_t + grad_mix * damp
            flow = dot((grad_mix * mixed).astype(BF), lower_b)
            row_list.append(jnp.sum(jnp.where(lane > sub, flow, 0.0), axis=0, keepdims=True))
        from_inter = row_s[:, cols].astype(F32)
        ddriven = dot(jnp.concatenate(mixes, axis=1), halves(low_half, dscan)) + from_inter
        dact = xpar_ref[5:6, cols] * dscan_f + step_p * ddriven
        direct_s[:, cols] = (act * ddriven).astype(BF)
        inter_s[:, cols] = (act * from_inter).astype(BF)
        row_s[:, cols] = (dscan_f * came_s[:, cols]).astype(BF)
        dst = dstate[:, cols]
        whole_p = pick(low_row, whole, 2 * p)
        across_s[0:1, cols] = whole_p * jnp.sum(
            dst * start_ref[:, cols].astype(F32), axis=0, keepdims=True)
        dcame_s[:, cols] = (enter_s[:, cols] * dscan_f).astype(BF)
        sent_s[:, cols] = (leave_s[:, cols] * driven.astype(F32)).astype(BF)
        dpre = dact * (sig * (1.0 + pre * (1.0 - sig)))
        dxbuf[0:CHUNK, cols] = dpre
        dval = xpar_ref[0:1, cols] * dpre
        sums = [jnp.sum(dpre * now, axis=0, keepdims=True)]
        for k in range(1, TAPS):
            dval = dval + xpar_ref[k : k + 1, cols] * (later[k - 1] * dxbuf[k : k + CHUNK, cols])
            sums.append(jnp.sum(dpre * shifted[k - 1], axis=0, keepdims=True))
        sums.append(jnp.sum(dpre, axis=0, keepdims=True))
        sums.append(jnp.sum(dscan_f * act, axis=0, keepdims=True))
        sums.append(jnp.zeros((2, 128), F32))
        xacc_ref[:, cols] += jnp.concatenate(sums, axis=0)
        dh_ref[:, place_of(cols, inner)] = dval.astype(BF)
    dxbuf[CHUNK : CHUNK + 8, :] = dxbuf[0:8, :]
    grad_inter_b = grad_inter_t.astype(BF)
    dstate_b = dstate[...].astype(BF)
    grad_b = dot(grad_inter_b, out_c) + dot(sent_s[...], dstate_b, ((1,), (1,)))
    grad_c = dot(grad_inter_b, in_b, ((0,), (0,))) + dot(dcame_s[...], start_ref[...], ((1,), (1,)))
    for p in range(pairs):
        cols = slice(128 * p, 128 * p + 128)
        dstate[:, cols] = pick(low_row, whole, 2 * p) * dstate[:, cols] + dot(
            out_c, dcame_s[:, cols], ((0,), (0,)))
    grad_act = jnp.concatenate([grad_b, grad_c], axis=1)
    dpre = grad_act * (sig_pair * (1.0 + pre_pair * (1.0 - sig_pair)))
    dpbuf[0:CHUNK, :] = dpre
    dval = bcpar_ref[0:1, :] * dpre
    sums = [jnp.sum(dpre * pbuf[8 : 8 + CHUNK, :], axis=0, keepdims=True)]
    for k in range(1, TAPS):
        dval = dval + bcpar_ref[k : k + 1, :] * (wide_column(later[k - 1]) * dpbuf[k : k + CHUNK, :])
        sums.append(jnp.sum(dpre * shifted_pair[k - 1], axis=0, keepdims=True))
    sums.append(jnp.sum(dpre, axis=0, keepdims=True))
    sums.append(jnp.zeros((3, 2 * STATE), F32))
    bcacc_ref[...] += jnp.concatenate(sums, axis=0)
    dpair_ref[...] = dval.astype(BF)
    dpbuf[CHUNK : CHUNK + 8, :] = dpbuf[0:8, :]
    lanes = lanes2[0:128, :]
    by_head = lambda value: dot(value, lanes, ((1,), (1,)))
    direct = by_head(direct_s[...])
    direct_inter = by_head(inter_s[...])
    row_inter = by_head(row_s[...])
    across = lax.dot_general(
        across_s[...], lanes.astype(F32), (((1,), (1,)), ((), ())), precision=HIGHEST,
        preferred_element_type=F32)[0:1]
    rows = jnp.concatenate(row_list + [jnp.zeros((CHUNK - 2 * pairs, 128), F32)], axis=0).T
    upper_b = (sub <= lane).astype(BF)
    strict_b = (sub > lane).astype(BF)
    grad_decay = rows + across + dot(upper_b, row_inter.astype(BF))
    grad_decay = grad_decay + dot(strict_b, (step * direct_inter).astype(BF))
    dstep = direct + grad_decay * rate
    draw = dstep * sigmoid(dt_raw + hpar_ref[0:1, :])
    hacc_ref[0:1, :] += jnp.sum(draw, axis=0, keepdims=True)
    hacc_ref[1:2, :] += jnp.sum(grad_decay * step, axis=0, keepdims=True) * rate
    mid = inner // 2
    dh_ref[:, mid : mid + 128] = jnp.where(lane < pairs, draw, 0.0).astype(BF)
    dh_ref[:, inner + 128 :] = jnp.where(lane >= pairs, draw, 0.0).astype(BF)


def ssd_backward(h1, pair, z, dgated, start, aux, segrow, xpar, bcpar, hpar):
    length, inner = z.shape
    chunks = length // CHUNK
    width = h1.shape[1]
    whole = lambda arr: pl.BlockSpec(arr.shape, lambda c: (0,) * arr.ndim)
    rows = lambda cols: pl.BlockSpec((CHUNK, cols), lambda c: (chunks - 1 - c, 0))
    before = lambda cols: pl.BlockSpec(
        (8, cols), lambda c: (jnp.maximum((chunks - 1 - c) * (CHUNK // 8) - 1, 0), 0))
    fixed = lambda r, cols: pl.BlockSpec((r, cols), lambda c: (0, 0))
    return pl.pallas_call(
        ssd_backward_kernel,
        grid=(chunks,),
        in_specs=[
            rows(width), before(width), rows(2 * STATE), before(2 * STATE),
            rows(inner), rows(inner), rows(inner), rows(128),
            pl.BlockSpec((1, 1, CHUNK), lambda c: (chunks - 1 - c, 0, 0)),
            whole(xpar), whole(bcpar), whole(hpar),
        ],
        out_specs=[
            rows(width), rows(2 * STATE),
            fixed(8, inner), fixed(8, 2 * STATE), fixed(8, 128),
        ],
        out_shape=[
            jax.ShapeDtypeStruct((length, width), BF),
            jax.ShapeDtypeStruct((length, 2 * STATE), BF),
            jax.ShapeDtypeStruct((8, inner), F32),
            jax.ShapeDtypeStruct((8, 2 * STATE), F32),
            jax.ShapeDtypeStruct((8, 128), F32),
        ],
        scratch_shapes=[
            pltpu.VMEM((CHUNK + 8, inner), F32),
            pltpu.VMEM((CHUNK + 8, 2 * STATE), F32),
            pltpu.VMEM((CHUNK + 8, inner), F32),
            pltpu.VMEM((CHUNK + 8, 2 * STATE), F32),
            pltpu.VMEM((STATE, inner), F32),
            pltpu.VMEM((256, inner), BF),
            pltpu.VMEM((CHUNK, inner), F32),
            pltpu.VMEM((CHUNK, inner), F32),
            pltpu.VMEM((CHUNK, inner), F32),
            pltpu.VMEM((CHUNK, inner), F32),
            pltpu.VMEM((CHUNK, inner), BF),
            pltpu.VMEM((CHUNK, inner), BF),
            pltpu.VMEM((CHUNK, inner), BF),
            pltpu.VMEM((CHUNK, inner), BF),
            pltpu.VMEM((CHUNK, inner), BF),
            pltpu.VMEM((8, inner), F32),
        ],
        compiler_params=pltpu.CompilerParams(vmem_limit_bytes=VMEM_LIMIT),
        name="ssd_backward",
    )(h1, h1, pair, pair, z, dgated, start, aux, segrow, xpar, bcpar, hpar)


def segment_tables(seg):
    length = seg.shape[0]
    chunks = length // CHUNK
    value = seg.astype(F32)
    far = jnp.full((TAPS,), -1.0, F32)
    cols = [value]
    for k in range(1, TAPS):
        cols.append((value == jnp.concatenate([far[:k], value[:-k]])).astype(F32))
    for k in range(1, TAPS):
        cols.append((value == jnp.concatenate([value[k:], far[:k]])).astype(F32))
    by_chunk = value.reshape(chunks, CHUNK)
    ends = by_chunk[:, -1:]
    before = jnp.concatenate([far[:1, None], ends[:-1]], axis=0)
    cols.append((by_chunk == before).astype(F32).reshape(-1))
    cols.append((by_chunk == ends).astype(F32).reshape(-1))
    aux = jnp.stack(cols, axis=1)
    return jnp.pad(aux, ((0, 0), (0, 128 - aux.shape[1]))), by_chunk[:, None, :]


BLOCK = 256
REACH = 512


def rope_tables(length):
    position = jnp.arange(length).astype(F32)
    freqs = jnp.exp(-(jnp.arange(0, HD, 2).astype(F32) / HD) * math.log(THETA))
    angle = position[:, None] * freqs[None, :]
    cosine, sine = jnp.cos(angle), jnp.sin(angle)
    return (
        jnp.concatenate([cosine] * 4, axis=1),
        jnp.concatenate([-sine, sine, -sine, sine], axis=1),
    )


def turn(values, cosine, sine):
    lane = lax.broadcasted_iota(jnp.int32, values.shape, 1)
    swapped = jnp.where(
        lane % HD < HD // 2, pltpu.roll(values, 128 - HD // 2, 1), pltpu.roll(values, HD // 2, 1)
    )
    return values * cosine + swapped * sine


def attention_forward_kernel(
    qkv_ref, cos_ref, sin_ref, segcol_ref, segrow_ref, out_ref, turned_ref, lse_ref
):
    length = qkv_ref.shape[0]
    groups = KVHEADS
    cosine, sine = cos_ref[...], sin_ref[...]
    for t in range(groups + 1):
        cols = slice(128 * t, 128 * t + 128)
        turned_ref[:, cols] = turn(qkv_ref[:, cols].astype(F32), cosine, sine).astype(BF)
    key_at, value_at = 128 * groups, 128 * (groups + 1)
    lane = lax.broadcasted_iota(jnp.int32, (BLOCK, 128), 1)
    for b in range(length // BLOCK):
        rows = slice(b * BLOCK, (b + 1) * BLOCK)
        first = max(0, b * BLOCK - REACH)
        keys = slice(first, (b + 1) * BLOCK)
        many = (b + 1) * BLOCK - first
        at_row = lax.broadcasted_iota(jnp.int32, (BLOCK, many), 0) + b * BLOCK
        at_col = lax.broadcasted_iota(jnp.int32, (BLOCK, many), 1) + first
        allowed = (at_row >= at_col) & (segcol_ref[rows, 0:1] == segrow_ref[:, keys])
        lse = jnp.zeros((BLOCK, 128), F32)
        for g in range(groups):
            key = turned_ref[keys, key_at + 64 * g : key_at + 64 * g + 64]
            value = qkv_ref[keys, value_at + 64 * g : value_at + 64 * g + 64]
            parts = []
            for s in range(2):
                query = turned_ref[rows, 128 * g + 64 * s : 128 * g + 64 * s + 64]
                scores = dot(query, key, ((1,), (1,))) * HD ** (-0.5)
                scores = jnp.where(allowed, scores, NEG)
                peak = jnp.max(scores, axis=1, keepdims=True)
                weights = jnp.exp(scores - peak)
                total = jnp.sum(weights, axis=1, keepdims=True)
                probs = (weights * (1.0 / total)).astype(BF)
                parts.append(dot(probs, value))
                lse = jnp.where(lane == 2 * g + s, peak + jnp.log(total), lse)
            out_ref[rows, 128 * g : 128 * g + 128] = jnp.concatenate(parts, axis=1).astype(BF)
        lse_ref[rows, :] = lse


def attention_forward(qkv, cosine, sine, aux, segrow):
    length = qkv.shape[0]
    return pl.pallas_call(
        attention_forward_kernel,
        out_shape=[
            jax.ShapeDtypeStruct((length, 128 * KVHEADS), BF),
            jax.ShapeDtypeStruct((length, 128 * (KVHEADS + 1)), BF),
            jax.ShapeDtypeStruct((length, 128), F32),
        ],
        compiler_params=pltpu.CompilerParams(vmem_limit_bytes=VMEM_LIMIT),
        name="attention_forward",
    )(qkv, cosine, sine, aux, segrow)


def attention_backward_kernel(
    qkv_ref, turned_ref, datt_ref, lse_ref, delta_ref, cos_ref, sin_ref, segcol_ref, segrow_ref,
    dqkv_ref, dkey, dvalue,
):
    length = qkv_ref.shape[0]
    groups = KVHEADS
    key_at, value_at = 128 * groups, 128 * (groups + 1)
    dkey[...] = jnp.zeros_like(dkey)
    dvalue[...] = jnp.zeros_like(dvalue)
    for b in range(length // BLOCK):
        rows = slice(b * BLOCK, (b + 1) * BLOCK)
        first = max(0, b * BLOCK - REACH)
        keys = slice(first, (b + 1) * BLOCK)
        many = (b + 1) * BLOCK - first
        at_key = lax.broadcasted_iota(jnp.int32, (many, BLOCK), 0) + first
        at_row = lax.broadcasted_iota(jnp.int32, (many, BLOCK), 1) + b * BLOCK
        allowed = (at_row >= at_key) & (segcol_ref[keys, 0:1] == segrow_ref[:, rows])
        dquery = []
        for g in range(groups):
            key = turned_ref[keys, key_at + 64 * g : key_at + 64 * g + 64]
            value = qkv_ref[keys, value_at + 64 * g : value_at + 64 * g + 64]
            dk = jnp.zeros((many, HD), F32)
            dv = jnp.zeros((many, HD), F32)
            for s in range(2):
                head = 2 * g + s
                half = slice(128 * g + 64 * s, 128 * g + 64 * s + 64)
                query = turned_ref[rows, half]
                datt = datt_ref[rows, half]
                scores = dot(key, query, ((1,), (1,))) * HD ** (-0.5)
                probs = jnp.exp(jnp.where(allowed, scores, NEG) - lse_ref[head : head + 1, rows])
                dprobs = dot(value, datt, ((1,), (1,)))
                dscores = (probs * (dprobs - delta_ref[head : head + 1, rows])).astype(BF)
                dk = dk + dot(dscores, query)
                dv = dv + dot(probs.astype(BF), datt)
                dquery.append(dot(dscores, key, ((0,), (0,))) * HD ** (-0.5))
            dkey[keys, 64 * g : 64 * g + 64] += dk * HD ** (-0.5)
            dvalue[keys, 64 * g : 64 * g + 64] += dv
        for g in range(groups):
            tile = jnp.concatenate([dquery[2 * g], dquery[2 * g + 1]], axis=1)
            dqkv_ref[rows, 128 * g : 128 * g + 128] = turn(
                tile, cos_ref[rows, :], -sin_ref[rows, :]
            ).astype(BF)
    dqkv_ref[:, key_at : key_at + 128] = turn(dkey[...], cos_ref[...], -sin_ref[...]).astype(BF)
    dqkv_ref[:, value_at : value_at + 128] = dvalue[...].astype(BF)


def attention_backward(qkv, turned, datt, lse, delta, cosine, sine, aux, segrow):
    length = qkv.shape[0]
    return pl.pallas_call(
        attention_backward_kernel,
        out_shape=jax.ShapeDtypeStruct(qkv.shape, BF),
        scratch_shapes=[pltpu.VMEM((length, 128), F32), pltpu.VMEM((length, 128), F32)],
        compiler_params=pltpu.CompilerParams(vmem_limit_bytes=VMEM_LIMIT),
        name="attention_backward",
    )(qkv, turned, datt, lse, delta, cosine, sine, aux, segrow)


def core_swap(value):
    return lax.ppermute(value, "head", [(0, 1), (1, 0), (2, 3), (3, 2)])


def half_swap(value):
    return lax.ppermute(value, "head", [(0, 2), (2, 0), (1, 3), (3, 1)])


def half_groups(dp):
    return [[d * 4 + 2 * half + core for d in range(dp) for half in range(2)] for core in range(2)]


def ordered(is_first, mine, other, axis):
    return jnp.where(
        is_first,
        jnp.concatenate([mine, other], axis=axis),
        jnp.concatenate([other, mine], axis=axis),
    )


BITS = (2, 4, 1)


def pair_list(dp, low_heads, bit):
    pairs = []
    for d in range(dp):
        for slot in range(4):
            flip = low_heads[slot % 2]
            target = (d ^ bit) * 4 + slot if flip else d * 4 + (slot ^ 2)
            pairs.append((d * 4 + slot, target))
    return pairs


def dp_swap(value, bit):
    return lax.ppermute(value, "dp", [(d, d ^ bit) for d in range(8)])


def near_swap(value, step):
    return lax.ppermute(value, ("dp", "head"), pair_list(8, (step == 1, step == 0), 1))


def append(value, arrived):
    return jnp.concatenate([value, arrived], axis=0)


class Order:
    def __init__(self):
        self.last = None

    def __call__(self, *values):
        held = values if self.last is None else values + (self.last,)
        held = lax.optimization_barrier(held)
        self.last = held[0]
        return held[0] if len(values) == 1 else held[: len(values)]


class Gather:
    def along(self, piece):
        self.piece = piece
        self.first = dp_swap(piece, BITS[0])

    def join(self, first):
        return append(self.piece, first)

    def across(self, pair):
        self.pair = pair
        self.second = dp_swap(pair, BITS[1])

    def join2(self, second):
        return append(self.pair, second)

    def near_step(self, quad):
        self.quad = quad
        self.third = near_swap(quad, 0)

    def join3(self, third):
        return append(self.quad, third)

    def far_step(self, near):
        self.near = near
        self.far = near_swap(near, 1)


def gather_whole(piece, dp, is_first):
    rows, cols = piece.shape
    both = lax.all_gather(
        piece, ("dp", "head"), axis=0, tiled=False, axis_index_groups=half_groups(dp)
    ).reshape(dp, 2, rows, cols)
    mine = jnp.where(is_first, both[:, 0], both[:, 1]).reshape(dp * rows, cols)
    other = jnp.where(is_first, both[:, 1], both[:, 0]).reshape(dp * rows, cols)
    lines = lambda value, side: value.reshape(4, 2, -1, cols)[:, side].reshape(-1, cols)
    return append(lines(mine, 0), lines(other, 0)), append(lines(mine, 1), lines(other, 1))


def unpack_kernel(groups, place, near_a, near_b, far_a, far_b, *outs):
    first = place[0] == 0
    step = near_a.shape[0]
    own = pl.ds(pl.multiple_of(place[1] * step, step), step)
    neighbour = pl.ds(pl.multiple_of((1 - place[1]) * step, step), step)
    for out, (at, size) in zip(outs, groups):
        cols = slice(at, at + size)
        one, two = near_b[:, cols], far_a[:, cols]
        out[own, :size] = near_a[:, cols]
        out[neighbour, size:] = far_b[:, cols]
        out[neighbour, :size] = jnp.where(first, two, one)
        out[own, size:] = jnp.where(first, one, two)


def unpack(near, far, place, groups):
    total, cols = near.shape
    step = total // 8
    view = lambda shift: pl.BlockSpec((step, cols), lambda i, _: (i + shift, 0))
    return pl.pallas_call(
        functools.partial(unpack_kernel, groups),
        grid_spec=pltpu.PrefetchScalarGridSpec(
            num_scalar_prefetch=1,
            grid=(4,),
            in_specs=[view(0), view(4), view(0), view(4)],
            out_specs=[
                pl.BlockSpec((2 * step, 2 * size), lambda i, place: (place[2 + i], 0)) for _, size in groups
            ],
        ),
        out_shape=[jax.ShapeDtypeStruct((total, 2 * size), BF) for _, size in groups],
        compiler_params=pltpu.CompilerParams(vmem_limit_bytes=VMEM_LIMIT),
        name="unpack",
    )(place, near, near, far, far)


def pack_kernel(count, place, *refs):
    ins, (send, two, keep) = refs[:count], refs[count:]
    first = place[0] == 0
    step = keep.shape[0]
    own = pl.ds(pl.multiple_of(place[1] * step, step), step)
    neighbour = pl.ds(pl.multiple_of((1 - place[1]) * step, step), step)
    at = 0
    for ref in ins:
        size = ref.shape[1] // 2
        cols = slice(at, at + size)
        mixed = (ref[neighbour, :size], ref[own, size:])
        keep[:, cols] = ref[own, :size]
        send[1, :, cols] = ref[neighbour, size:]
        send[0, :, cols] = jnp.where(first, mixed[0], mixed[1])
        two[:, cols] = jnp.where(first, mixed[1], mixed[0])
        at += size


def pack(grads, place):
    total = grads[0].shape[0]
    step = total // 8
    cols = sum(grad.shape[1] for grad in grads) // 2
    return pl.pallas_call(
        functools.partial(pack_kernel, len(grads)),
        grid_spec=pltpu.PrefetchScalarGridSpec(
            num_scalar_prefetch=1,
            grid=(4,),
            in_specs=[
                pl.BlockSpec((2 * step, grad.shape[1]), lambda i, place: (place[2 + i], 0)) for grad in grads
            ],
            out_specs=[
                pl.BlockSpec((2, step, cols), lambda i, _: (0, i, 0)),
                pl.BlockSpec((step, cols), lambda i, _: (i, 0)),
                pl.BlockSpec((step, cols), lambda i, _: (i, 0)),
            ],
        ),
        out_shape=[
            jax.ShapeDtypeStruct((2, total // 2, cols), BF),
            jax.ShapeDtypeStruct((total // 2, cols), BF),
            jax.ShapeDtypeStruct((total // 2, cols), BF),
        ],
        compiler_params=pltpu.CompilerParams(vmem_limit_bytes=VMEM_LIMIT),
        name="pack",
    )(place, *grads)


def long(value):
    return value.astype(F32)


class Scatter:
    def __init__(self, grads, place):
        self.rows = grads[0].shape[0] // 8
        self.send, self.two, self.keep = pack(grads, place)

    def far_step(self, send):
        self.got = near_swap(send, 1)

    def sum2(self, got):
        self.got = got
        return (long(self.two) + long(got[1])).astype(BF)

    def near_step(self, part):
        self.got2 = near_swap(part, 0)

    def kept(self, part):
        return long(self.keep[part]) + long(self.got[0, part]) + long(self.got2[part])

    def sum3(self, got2):
        self.got2 = got2
        return self.kept(slice(2 * self.rows, 4 * self.rows)).astype(BF)

    def across(self, part):
        self.got3 = dp_swap(part, BITS[1])

    def lower(self, part):
        return self.kept(part) + long(self.got3[part])

    def sum4(self, got3):
        self.got3 = got3
        return self.lower(slice(self.rows, 2 * self.rows)).astype(BF)

    def along(self, part):
        self.got4 = dp_swap(part, BITS[0])

    def result(self, got4):
        return self.lower(slice(0, self.rows)) + long(got4)


def scatter_whole(grads, dp, is_first):
    rows = grads[0].shape[0] // dp
    half_of = lambda grad, side: grad[:, side * (grad.shape[1] // 2) : (side + 1) * (grad.shape[1] // 2)]
    mine, other = [
        jnp.concatenate([half_of(grad, side) for grad in grads], axis=1).reshape(dp, 1, rows, -1)
        for side in range(2)
    ]
    both = ordered(is_first, mine, other, 1).reshape(dp * 2 * rows, -1)
    return lax.psum_scatter(
        both, ("dp", "head"), scatter_dimension=0, tiled=True, axis_index_groups=half_groups(dp)
    ).astype(F32)


def load_kernel(place, tok_ref, cot_ref, gain_ref, rows_ref, cot_out, normed_ref, scale_ref):
    rows = tok_ref[...]
    rows_ref[...] = rows
    cot_out[...] = cot_ref[...]
    rows = rows.astype(F32)
    scale = lax.rsqrt(jnp.mean(rows * rows, axis=1, keepdims=True) + EPSILON)
    scale_ref[...] = scale
    normed_ref[...] = (rows * scale * gain_ref[...]).astype(BF)


def load(tokens, cotangent, gain, half, length):
    width = tokens.shape[1]
    step = 256
    steps = length // step
    picked = pl.BlockSpec((step, width), lambda i, place: (place[0] * steps + i, 0))
    plain = pl.BlockSpec((step, width), lambda i, place: (i, 0))
    return pl.pallas_call(
        load_kernel,
        grid_spec=pltpu.PrefetchScalarGridSpec(
            num_scalar_prefetch=1,
            grid=(steps,),
            in_specs=[picked, picked, pl.BlockSpec((1, width), lambda i, place: (0, 0))],
            out_specs=[plain, plain, plain, pl.BlockSpec((step, 1), lambda i, place: (i, 0))],
        ),
        out_shape=[jax.ShapeDtypeStruct((length, width), BF)] * 3
        + [jax.ShapeDtypeStruct((length, 1), F32)],
        compiler_params=pltpu.CompilerParams(vmem_limit_bytes=VMEM_LIMIT),
        name="load",
    )(half, tokens, cotangent, gain)


def store_kernel(place, mine_ref, got_ref, got2_ref, out_ref):
    step = pl.program_id(0)
    for index, ref in enumerate((mine_ref, got_ref, got2_ref)):

        @pl.when((step >= place[2 * index]) & (step < place[2 * index + 1]))
        def _():
            out_ref[...] = ref[...]


def part_of(mine, core):
    return lax.dynamic_slice_in_dim(mine, core * (mine.shape[0] // 2), mine.shape[0] // 2, 0)


def store(mine, got, got2, half, core):
    length, width = mine.shape
    step = 256
    per = length // step
    begin = jnp.stack(
        [half * per, (1 - half) * per + core * (per // 2), (1 - half) * per + (1 - core) * (per // 2)])
    many = jnp.array([per, per // 2, per // 2])
    place = jnp.stack([begin, begin + many], axis=1).reshape(-1).astype(jnp.int32)
    part = lambda index, size: pl.BlockSpec(
        (step, width), lambda i, place: (jnp.clip(i - place[2 * index], 0, size - 1), 0))
    return pl.pallas_call(
        store_kernel,
        grid_spec=pltpu.PrefetchScalarGridSpec(
            num_scalar_prefetch=1,
            grid=(2 * per,),
            in_specs=[part(0, per), part(1, per // 2), part(2, per // 2)],
            out_specs=pl.BlockSpec((step, width), lambda i, place: (i, 0)),
        ),
        out_shape=jax.ShapeDtypeStruct((2 * length, width), BF),
        compiler_params=pltpu.CompilerParams(vmem_limit_bytes=VMEM_LIMIT),
        name="store",
    )(place, mine, got, got2)


def first_piece_kernel(slot, x_ref, dt_ref, bc_ref, key_ref, value_ref, out_ref):
    inner = x_ref.shape[1]
    heads = dt_ref.shape[1]
    rows = x_ref.shape[0]
    out_ref[:, :inner] = x_ref[...].astype(BF)
    steps = dt_ref[...]
    out_ref[:, inner : inner + 128] = jnp.concatenate(
        [steps, steps, jnp.zeros((rows, 128 - 2 * heads), F32)], axis=1).astype(BF)
    sources = (bc_ref.at[:, :128], bc_ref.at[:, 128:], key_ref, value_ref)
    for index, ref in enumerate(sources):

        @pl.when(slot[0] == index)
        def _():
            out_ref[:, inner + 128 :] = ref[...].astype(BF)


def first_piece(slot, x, dt, bc, key, value):
    vmem = pl.BlockSpec(memory_space=pltpu.VMEM)
    return pl.pallas_call(
        first_piece_kernel,
        in_specs=[pl.BlockSpec(memory_space=pltpu.SMEM)] + [vmem] * 5,
        out_specs=vmem,
        out_shape=jax.ShapeDtypeStruct((x.shape[0], x.shape[1] + 256), BF),
        compiler_params=pltpu.CompilerParams(vmem_limit_bytes=VMEM_LIMIT),
        name="first_piece",
    )(slot[None].astype(jnp.int32), x, dt, bc, key, value)


def other_pieces_kernel(z_ref, q_ref, out_w, o_ref, gate_ref, up_ref, down_ref, p2, p3, p4, p5):
    join = lambda *parts: jnp.concatenate(parts, axis=1).astype(BF)
    p2[...] = join(z_ref[...], q_ref[...])
    p3[...] = join(out_w[...].T, o_ref[...].T)
    p4[...] = join(gate_ref[...], up_ref[...])
    p5[...] = down_ref[...].T.astype(BF)


def other_pieces(z, q, out_w, o, gate, up, down):
    rows = z.shape[0]
    vmem = pl.BlockSpec(memory_space=pltpu.VMEM)
    shape = lambda cols: jax.ShapeDtypeStruct((rows, cols), BF)
    return pl.pallas_call(
        other_pieces_kernel,
        in_specs=[vmem] * 7,
        out_specs=[vmem] * 4,
        out_shape=[
            shape(z.shape[1] + q.shape[1]), shape(out_w.shape[0] + o.shape[0]),
            shape(gate.shape[1] + up.shape[1]), shape(down.shape[0]),
        ],
        compiler_params=pltpu.CompilerParams(vmem_limit_bytes=VMEM_LIMIT),
        name="other_pieces",
    )(z, q, out_w, o, gate, up, down)


def shared_kernel(place, bc_ref, kv_ref, keep, send):
    half, core = place[0], place[1]
    step = bc_ref.shape[0] // 4
    for out, which in ((keep, core), (send, 1 - core)):
        for side in range(2):
            slot = 2 * (half if side == 0 else 1 - half) + which
            rows = pl.ds(pl.multiple_of(slot * step, step), step)
            for col in range(4):
                ref = bc_ref if col < 2 else kv_ref
                out[col * step : (col + 1) * step, 128 * side : 128 * side + 128] = ref[
                    rows, 128 * (col % 2) : 128 * (col % 2) + 128]


def shared_rows(grad_bc, grad_kv, half, core):
    total = grad_bc.shape[0]
    step = 128
    spec = pl.BlockSpec((step, 256), lambda i, _: (i, 0))
    return pl.pallas_call(
        shared_kernel,
        grid_spec=pltpu.PrefetchScalarGridSpec(
            num_scalar_prefetch=1,
            grid=(total // step,),
            in_specs=[spec, spec],
            out_specs=[spec, spec],
        ),
        out_shape=[jax.ShapeDtypeStruct((total, 256), BF)] * 2,
        compiler_params=pltpu.CompilerParams(vmem_limit_bytes=VMEM_LIMIT),
        name="shared_rows",
    )(jnp.stack([half, core]).astype(jnp.int32), grad_bc, grad_kv)


def products_kernel(count, *refs):
    out = refs[-1]
    total = dot(refs[0][...], refs[count][...], ((1,), (1,)))
    for i in range(1, count):
        total = total + dot(refs[i][...], refs[count + i][...], ((1,), (1,)))
    out[...] = total.astype(out.dtype)


def products(lefts, rights, dtype):
    length = lefts[0].shape[0]
    width = rights[0].shape[0]
    step = 256
    return pl.pallas_call(
        functools.partial(products_kernel, len(lefts)),
        grid=(length // step,),
        in_specs=[pl.BlockSpec((step, left.shape[1]), lambda i: (i, 0)) for left in lefts]
        + [pl.BlockSpec(right.shape, lambda i: (0, 0)) for right in rights],
        out_specs=pl.BlockSpec((step, width), lambda i: (i, 0)),
        out_shape=jax.ShapeDtypeStruct((length, width), dtype),
        compiler_params=pltpu.CompilerParams(vmem_limit_bytes=VMEM_LIMIT),
        name="products",
    )(*lefts, *rights)


def core_sum(part):
    part = part.astype(BF)
    return part.astype(F32) + core_swap(part).astype(F32)


def wide(mine, other, width):
    return jnp.concatenate([mine[:, :width], other[:, :width]], axis=1)


def norm_back(grad, values, scale, gain):
    weighted = grad * gain
    inner = jnp.mean(weighted * values, axis=-1, keepdims=True)
    return scale * weighted - values * (scale * scale * scale * inner), jnp.sum(
        grad * (values * scale), axis=0
    )


def body(
    tokens, segments, cotangent, gain_in, mamba_gate_weight, mamba_input_weight, w_dt, w_bc,
    convolution_input_taps, convolution_input_bias, conv_bc, conv_bc_bias, dt_bias, a_log, d_skip,
    w_q, w_k, w_v, w_o, mamba_output_weight, gain_ffn, w_gate, w_up, w_down,
):
    length = segments.shape[1]
    width = tokens.shape[1]
    rows_here = mamba_gate_weight.shape[0]
    dp = width // rows_here
    inner = mamba_gate_weight.shape[1]
    heads = w_dt.shape[1]
    qcols = w_q.shape[1]
    hidden_cols = w_gate.shape[1]
    slot = lax.axis_index("head")
    half = slot // 2
    core = slot % 2
    is_first = half == 0
    place_dp = lax.axis_index("dp")
    if dp == 8:
        route = jnp.stack([core, place_dp % 2] + [(place_dp // 2) ^ i for i in range(4)])
    else:
        route = jnp.concatenate([jnp.zeros((2,), jnp.int32), jnp.arange(4)])
    route = route.astype(jnp.int32)
    gain_in, gain_ffn = gain_in[None], gain_ffn[None]

    short = lambda value: value.astype(BF)
    first_core = core == 0
    flip = lambda tile: jnp.where(is_first, tile, jnp.concatenate([tile[:, HD:], tile[:, :HD]], axis=1))
    flips = lambda tile: jnp.concatenate([flip(tile[:, :128]), flip(tile[:, 128:])], axis=1)
    cols = ((0,), (0,))
    own = half[None].astype(jnp.int32)
    ringed = dp == 8
    order = Order()

    def tables(segments):
        seg = lax.dynamic_index_in_dim(segments, half, 0, keepdims=False)
        return segment_tables(seg) + rope_tables(length)

    piece1 = first_piece(slot, mamba_input_weight, w_dt, w_bc, w_k, w_v)
    rest = (mamba_gate_weight, w_q, mamba_output_weight, w_o, w_gate, w_up, w_down)
    shapes1 = ((0, inner + 128), (inner + 128, 128))
    shapes2 = shapes3 = ((0, inner), (inner, qcols))
    shapes4 = ((0, hidden_cols), (hidden_cols, hidden_cols))
    shapes5 = ((0, hidden_cols),)
    g1, g2, g3, g4, g5 = [Gather() for _ in range(5)]
    if ringed:
        g1.along(piece1)
        held = order(g1.first, tokens, cotangent, segments, *rest)
        first1, tokens, cotangent, segments = held[:4]
        pieces = other_pieces(*held[4:])
        pair1, *pieces = order(g1.join(first1), *pieces)
        g1.across(pair1)
        for g, piece in zip((g2, g3, g4, g5), pieces):
            g.along(piece)
    else:
        pieces = (
            jnp.concatenate([short(mamba_gate_weight), short(w_q)], axis=1),
            jnp.concatenate([short(mamba_output_weight).T, short(w_o).T], axis=1),
            jnp.concatenate([short(w_gate), short(w_up)], axis=1), short(w_down).T)
        ways = [gather_whole(piece, dp, is_first) for piece in (piece1,) + pieces]
    rows_b, upstream, normed, scale = load(tokens, cotangent, gain_in, own, length)
    aux, segrow, cosine, sine = tables(segments)
    seg_line = aux[:, 0][None]
    per_head = jnp.pad(jnp.stack([dt_bias, a_log, d_skip]), ((0, 5), (0, 128 - heads)))
    small = jnp.concatenate(
        [jnp.concatenate([convolution_input_taps, convolution_input_bias[None],
                          jnp.repeat(d_skip, HD)[None], jnp.zeros((2, inner), F32)], axis=0), per_head],
        axis=1)
    small_other = half_swap(small)
    xpar = jnp.concatenate([small[:, :inner], small_other[:, :inner]], axis=1)
    head_par = jnp.concatenate(
        [small[:2, inner : inner + heads], small_other[:2, inner : inner + heads],
         jnp.zeros((2, 128 - 2 * heads), F32)], axis=1)
    lane = jnp.arange(128) < 2 * heads
    hpar = jnp.concatenate(
        [head_par[:1], jnp.where(lane, -jnp.exp(head_par[1:]), 0.0), jnp.zeros((6, 128), F32)], axis=0)
    bcpar = jnp.concatenate([conv_bc, conv_bc_bias[None], jnp.zeros((3, conv_bc.shape[1]), F32)], axis=0)
    rows = rows_b.astype(F32)

    if ringed:
        second1, normed, aux, cosine, sine, xpar, hpar = order(
            g1.second, normed, aux, cosine, sine, xpar, hpar)
        quad1, first2 = order(g1.join2(second1), g2.first)
        g1.near_step(quad1)
        pair2, third1 = order(g2.join(first2), g1.third)
        g2.across(pair2)
        near1, second2 = order(g1.join3(third1), g2.second)
        g1.far_step(near1)
        quad2, first3 = order(g2.join2(second2), g3.first)
        g2.near_step(quad2)
        pair3, third2 = order(g3.join(first3), g2.third)
        g3.across(pair3)
        near2, far1 = order(g2.join3(third2), g1.far)
        g2.far_step(near2)
        ways1 = (g1.near, far1)
    else:
        ways1 = ways[0]
    weight1, quarters = unpack(*ways1, route, shapes1)
    swap_halves = lambda tile: jnp.concatenate([tile[:, 128:], tile[:, :128]], axis=1)
    quarters = jnp.where(is_first, quarters, swap_halves(quarters))
    others = core_swap(quarters)
    h1 = dot(normed, weight1)
    if ringed:
        h1, second3, first4 = order(h1, g3.second, g4.first)
        quad3, pair4 = g3.join2(second3), g4.join(first4)
        quad3, pair4, others = order(quad3, pair4, others)
        g3.near_step(quad3)
        g4.across(pair4)
    c0 = jnp.where(first_core, quarters, others)
    c1 = jnp.where(first_core, others, quarters)
    weight_bc = jnp.concatenate([c0[:, :128], c1[:, :128]], axis=1)
    weight_kv = flips(jnp.concatenate([c0[:, 128:], c1[:, 128:]], axis=1))
    pair = dot(normed, weight_bc)
    keyvalue = short(dot(normed, weight_kv))
    if ringed:
        third3, pair, keyvalue = order(g3.third, pair, keyvalue)
        near3, far2 = order(g3.join3(third3), g2.far)
        g3.far_step(near3)
        ways2 = (g2.near, far2)
    else:
        ways2 = ways[1]
    weight_z, weight_q = unpack(*ways2, route, shapes2)
    z = short(dot(normed, weight_z))
    qkv = jnp.concatenate([short(dot(normed, weight_q)), keyvalue], axis=1)
    if ringed:
        second4, first5, z, qkv = order(g4.second, g5.first, z, qkv)
        quad4, pair5, qkv = order(g4.join2(second4), g5.join(first5), qkv)
        g4.near_step(quad4)
        g5.across(pair5)

    attended, turned, lse = attention_forward(qkv, cosine, sine, aux, seg_line)
    if ringed:
        third4, far3, attended = order(g4.third, g3.far, attended)
        near4, second5 = order(g4.join3(third4), g5.second)
        g4.far_step(near4)
        quad5, z = order(g5.join2(second5), z)
        g5.near_step(quad5)
        ways3 = (g3.near, far3)
    else:
        ways3 = ways[2]
    gated, scan, start = ssd_forward(h1, pair, z, aux, segrow, xpar, bcpar, hpar)
    weight_out, weight_o = unpack(*ways3, route, shapes3)
    if ringed:
        third5, gated, weight_out = order(g5.third, gated, weight_out)
        near5, gated = order(g5.join3(third5), gated)
        g5.far_step(near5)
    mixed = dot(gated, weight_out, ((1,), (1,))) + dot(attended, weight_o, ((1,), (1,)))
    state = rows + core_sum(mixed)

    scale_ffn = lax.rsqrt(jnp.mean(state * state, axis=-1, keepdims=True) + EPSILON)
    normed_ffn = short(state * scale_ffn * gain_ffn)
    if ringed:
        normed_ffn, far4 = order(normed_ffn, g4.far)
        ways4 = (g4.near, far4)
    else:
        ways4 = ways[3]
    weight_gate, weight_up = unpack(*ways4, route, shapes4)
    gate = dot(normed_ffn, weight_gate)
    up = dot(normed_ffn, weight_up)
    sig = jax.nn.sigmoid(gate)
    hidden = short(gate * sig * up)
    grad_down = short(dot(upstream, hidden, cols))
    if ringed:
        s5 = Scatter([grad_down], route)
        send5, hidden, far5 = order(s5.send, hidden, g5.far)
        s5.far_step(send5)
        ways5 = (g5.near, far5)
    else:
        ways5 = ways[4]
    (weight_down,) = unpack(*ways5, route, shapes5)
    whole = short(dot(hidden, weight_down, ((1,), (1,))))
    if ringed:
        whole, upstream = order(whole, upstream)
    whole_got = core_swap(whole)

    dhidden = dot(upstream, weight_down)
    dgate = short(dhidden * up * (sig * (1.0 + gate * (1.0 - sig))))
    dup = short(dhidden * (gate * sig))
    grad_gate = short(dot(normed_ffn, dgate, cols))
    grad_up = short(dot(normed_ffn, dup, cols))
    if ringed:
        s4 = Scatter([grad_gate, grad_up], route)
        send4, whole_got, dgate, dup = order(s4.send, whole_got, dgate, dup)
        s4.far_step(send4)
    out_mine = short(state + (long(whole) + long(whole_got)))
    dnormed_part = short(dot(dgate, weight_gate, ((1,), (1,))) + dot(dup, weight_up, ((1,), (1,))))
    if ringed:
        dnormed_part, out_mine, got5 = order(dnormed_part, out_mine, s5.got)
    dnormed_got = core_swap(dnormed_part)
    if ringed:
        part5, dnormed_got = order(s5.sum2(got5), dnormed_got)
        s5.near_step(part5)
    out_got = half_swap(part_of(out_mine, core))
    dstate_norm, grad_gain_ffn = norm_back(
        long(dnormed_part) + long(dnormed_got), state, scale_ffn, gain_ffn)
    dstate = long(upstream) + dstate_norm
    dmixed = short(dstate)

    dgated = dot(dmixed, weight_out)
    gate_z = long(z)
    sig_z = jax.nn.sigmoid(gate_z)
    dz = short(dgated * long(scan) * (sig_z * (1.0 + gate_z * (1.0 - sig_z))))
    dgated = short(dgated)
    datt = short(dot(dmixed, weight_o))
    if ringed:
        dgated, dz, datt, got2_5 = order(dgated, dz, datt, s5.got2)
        third_5, datt, dz = order(s5.sum3(got2_5), datt, dz)
        s5.across(third_5)
    delta = jnp.sum((long(datt) * long(attended)).reshape(length, -1, HD), axis=-1).T
    delta = jnp.pad(delta, ((0, 8 - delta.shape[0]), (0, 0)))
    dqkv = attention_backward(
        qkv, turned, datt, lse[:, :8].T, delta, cosine, sine, aux, seg_line)
    if ringed:
        dqkv, got4 = order(dqkv, s4.got)
        part4, dqkv = order(s4.sum2(got4), dqkv)
        s4.near_step(part4)
    dqry, dkv = dqkv[:, : 2 * qcols], dqkv[:, 2 * qcols :]
    second_grads = [
        short(dot(dmixed, gated, cols)), short(dot(dmixed, attended, cols)),
        short(dot(normed, dz, cols)), short(dot(normed, dqry, cols))]
    if ringed:
        s2 = Scatter(second_grads, route)
        send2, got3_5, out_got = order(s2.send, s5.got3, out_got)
        s2.far_step(send2)
        fourth_5, got2_4 = order(s5.sum4(got3_5), s4.got2)
        s5.along(fourth_5)
        third_4, dgated = order(s4.sum3(got2_4), dgated)
        s4.across(third_4)
    dh1, dpair, xacc, bcacc, hacc = ssd_backward(
        h1, pair, z, dgated, start, aux, segrow, xpar, bcpar, hpar)
    if ringed:
        dh1, dpair, got_2, got3_4, got4_5 = order(dh1, dpair, s2.got, s4.got3, s5.got4)
        part2, fourth_4, dh1, dpair = order(s2.sum2(got_2), s4.sum4(got3_4), dh1, dpair)
        s2.near_step(part2)
        s4.along(fourth_4)

    grad1 = short(dot(normed, dh1, cols))
    grad_bc = short(dot(normed, dpair, cols))
    grad_kv = flips(short(dot(normed, dkv, cols)))
    keep_shared, send_shared = shared_rows(grad_bc, grad_kv, half, core)
    if ringed:
        send_shared, dh1, grad1 = order(send_shared, dh1, grad1)
    shared_got = core_swap(send_shared)
    out_got2 = core_swap(out_got)
    bc_got = core_swap(bcacc)
    dnormed_part = products(
        [dh1, dpair, dz, dqry, dkv], [weight1, weight_bc, weight_z, weight_q, weight_kv], BF)
    if ringed:
        dnormed_part, shared_got, got2_2 = order(dnormed_part, shared_got, s2.got2)
    dnormed_got = core_swap(dnormed_part)
    grad_shared = short(long(keep_shared) + long(shared_got))
    last_grads = [grad1, grad_shared]
    if ringed:
        s1 = Scatter(last_grads, route)
        send1, third_2 = order(s1.send, s2.sum3(got2_2))
        s1.far_step(send1)
        s2.across(third_2)
        dnormed_got, third_2, out_got2 = order(dnormed_got, third_2, out_got2)
    drows, grad_gain_in = norm_back(long(dnormed_part) + long(dnormed_got), rows, scale, gain_in)
    grad_mine = short(dstate + drows)
    output = store(out_mine, out_got, out_got2, half, core)
    if ringed:
        grad_mine, got_1 = order(grad_mine, s1.got)
        part1 = order(s1.sum2(got_1))
        s1.near_step(part1)
    grad_got = half_swap(part_of(grad_mine, core))

    skip = xacc[5].reshape(2, heads, HD).sum(axis=-1)
    stretches = []
    for side in range(2):
        stretches.append(jnp.concatenate([
            xacc[:5, side * inner : (side + 1) * inner].reshape(-1),
            hacc[0, side * heads : (side + 1) * heads], hacc[1, side * heads : (side + 1) * heads],
            skip[side]]))
    stretch = stretches[0].shape[0]
    bc_sum = (bcacc + bc_got)[:5]
    vector = jnp.concatenate([
        jnp.where(is_first, stretches[0], stretches[1]), jnp.where(is_first, stretches[1], stretches[0]),
        bc_sum.reshape(-1), grad_gain_in, grad_gain_ffn])
    size = vector.shape[0]
    vector = jnp.pad(vector, (0, -size % 1024)).reshape(-1, 128)
    if ringed:
        vector = vector + half_swap(vector)
        vector, got2_1, got3_2 = order(vector + dp_swap(vector, 1), s1.got2, s2.got3)
        third_1, fourth_2, vector = order(s1.sum3(got2_1), s2.sum4(got3_2), vector)
        s1.across(third_1)
        s2.along(fourth_2)
        vector = vector + dp_swap(vector, 2)
        vector, got4_2, got4_4 = order(vector + dp_swap(vector, 4), s2.got4, s4.got4)
        sent5, sent4, sent2 = s5.result(got4_5), s4.result(got4_4), s2.result(got4_2)
        got3_1 = order(s1.got3)
        fourth_1 = order(s1.sum4(got3_1))
        s1.along(fourth_1)
        sent1 = s1.result(s1.got4)
    else:
        vector = lax.psum(vector, ("dp", "head"), axis_index_groups=half_groups(dp))
        sent5, sent4, sent2, sent1 = [
            scatter_whole(grads, dp, is_first)
            for grads in ([grad_down], [grad_gate, grad_up], second_grads, last_grads)]
    sent3, sent2 = sent2[:, : inner + qcols], sent2[:, inner + qcols :]
    grad_tokens = store(grad_mine, grad_got, core_swap(grad_got), half, core)
    vector = vector.reshape(-1)[:size]
    own = jnp.where(is_first, vector[:stretch], vector[stretch : 2 * stretch])
    taps = own[: 5 * inner].reshape(5, inner)
    per = own[5 * inner :].reshape(3, heads)
    rank = place_dp * 4 + slot
    bc_cols = conv_bc.shape[1] // (4 * dp)
    at = 2 * stretch
    bc_own = lax.dynamic_slice_in_dim(
        vector[at : at + bc_sum.size].reshape(5, -1), rank * bc_cols, bc_cols, 1)
    gain_grads = lax.dynamic_slice_in_dim(
        vector[at + bc_sum.size :].reshape(2, width), place_dp * rows_here, rows_here, 1)

    quarter_rows = rows_here // 4
    shared_own = sent1[:, inner + 128 :].reshape(4, quarter_rows, 128).swapaxes(0, 1).reshape(quarter_rows, -1)
    return (
        output,
        grad_tokens,
        gain_grads[0],
        sent2[:, :inner],
        sent1[:, :inner],
        sent1[:, inner : inner + heads] + sent1[:, inner + heads : inner + 2 * heads],
        shared_own[:, : 2 * STATE],
        taps[:4],
        taps[4],
        bc_own[:4],
        bc_own[4],
        per[0],
        per[1],
        per[2],
        sent2[:, inner:],
        shared_own[:, 2 * STATE : 2 * STATE + 128],
        shared_own[:, 2 * STATE + 128 :],
        sent3[:, inner:].T,
        sent3[:, :inner].T,
        gain_grads[1],
        sent4[:, :hidden_cols],
        sent4[:, hidden_cols:],
        sent5.T,
    )


def solution(mesh):
    in_specs = (
        P("dp", None),
        P("dp", None),
        P("dp", None),
        P(),
        P("dp", "head"),
        P("dp", "head"),
        P("dp", "head"),
        P("dp", None),
        P(None, "head"),
        P("head"),
        P(),
        P(),
        P("head"),
        P("head"),
        P("head"),
        P("dp", "head"),
        P("dp", None),
        P("dp", None),
        P("head", "dp"),
        P("head", "dp"),
        P(),
        P("dp", "head"),
        P("dp", "head"),
        P("head", "dp"),
    )
    out_specs = (
        P("dp", None),
        P("dp", None),
        P("dp"),
        P("dp", "head"),
        P("dp", "head"),
        P("dp", "head"),
        P(("dp", "head"), None),
        P(None, "head"),
        P("head"),
        P(None, ("dp", "head")),
        P(("dp", "head")),
        P("head"),
        P("head"),
        P("head"),
        P("dp", "head"),
        P(("dp", "head"), None),
        P(("dp", "head"), None),
        P("head", "dp"),
        P("head", "dp"),
        P("dp"),
        P("dp", "head"),
        P("dp", "head"),
        P("head", "dp"),
    )
    return jax.shard_map(body, mesh=mesh, in_specs=in_specs, out_specs=out_specs, check_vma=False)
```

time: 890 us -> 517 us (0.58)
  blocking collectives: 212 us -> 0 us
  waiting for transfers between devices: 261 us -> 150 us
  local copies, waits for them, and re-layouts: 151 us -> 48.8 us
  starting transfers between devices: 6.83 us -> 52 us
  Pallas kernels: 74.1 us -> 108 us
  between operations: 16.2 us -> 2.48 us
  other arithmetic: 86.8 us -> 75.7 us
    psum x1 -> x0, blocking collectives: 212 us -> none  [body(): lax.psum(jnp.concatenate([table.reshape(-1), bcacc[:5].reshape(-1)]), ('d...]
    all_gather x5 -> x0, waiting for transfers between devices: 192 us -> none  [gather(): lax.all_gather(piece, ('dp', 'head'), axis=0, tiled=False, axis_index_gro...]
    ppermute x0 -> x39, waiting for transfers between devices: none -> 145 us  [the longest x18 85.8 us: near_swap(): lax.ppermute(value, ('dp', 'head'), pair_list(8, (step == 1, step == 0), 1))]
    reduce_scatter x3 -> x0, waiting for transfers between devices: 68.9 us -> none  [scatter_sum(): lax.psum_scatter(both, ('dp', 'head'), scatter_dimension=0, tiled=True, a...]
    pallas_call x0 -> x16, Pallas kernels: none -> 51.7 us  [the longest x2 13.1 us: store(): pl.pallas_call(store_kernel, grid_spec=pltpu.PrefetchScalarGridSpec(num_s...]
    ppermute x0 -> x39, starting transfers between devices: none -> 43.7 us  [the longest x21 24.1 us: dp_swap(): return lax.ppermute(value, 'dp', [(d, d ^ bit) for d in range(8)])]
    unnamed x187 -> x235, local copies, waits for them, and re-layouts: 62.5 us -> 26.2 us
    select_n x16 -> x4, other arithmetic: 35 us -> 0.32 us  [the longest x1 0.16 us: body(): quarters = jnp.where(is_first, quarters, swap_halves(quarters))]
  transfers between devices with their start and end apart: 19 -> 52, of which waited for: 6 -> 20; matrix products, arithmetic and copies ran while one was open for 29% -> 32% of each run, Pallas kernels for 8% -> 20%
where the time goes in v2:
time: 517 us; the launch traced here: 507 us
  waiting for transfers between devices  150 us (29%)
  Pallas kernels  108 us (21%)
  other arithmetic  75.7 us (15%)
  matrix products  70.5 us (14%)
  starting transfers between devices  52 us (10%)
  local copies, waits for them, and re-layouts  48.8 us (9%)
    ppermute x18, waiting for transfers between devices, near_swap(): lax.ppermute(value, ('dp', 'head'), pair_list(8, (step == 1, step == 0), 1))  85.8 us
    dot_general x25, matrix products, dot(): lax.dot_general(left, right, (dims, ((), ())), preferred_element_type=F32)  70.5 us
    ppermute x21, waiting for transfers between devices, dp_swap(): return lax.ppermute(value, 'dp', [(d, d ^ bit) for d in range(8)])  59.2 us
    pallas_call x1, Pallas kernels, ssd_backward(): pl.pallas_call(ssd_backward_kernel, grid=(chunks,), in_specs=[rows(width)...  28.2 us
    unnamed x235, local copies, waits for them, and re-layouts  26.2 us
    ppermute x21, starting transfers between devices, dp_swap(): return lax.ppermute(value, 'dp', [(d, d ^ bit) for d in range(8)])  24.1 us
    ppermute x18, starting transfers between devices, near_swap(): lax.ppermute(value, ('dp', 'head'), pair_list(8, (step == 1, step == 0), 1))  19.6 us
    convert_element_type x5, other arithmetic, body(): short = lambda value: value.astype(BF)  17.4 us
  transfers between devices with their start and end apart: 52, of which 20 were waited for; matrix products, arithmetic and copies ran while one was open for 32% of the time, Pallas kernels for 20%

profile of v2, /device:TPU:0, one launch (start us, length us, event | category | flops | bytes accessed | tf_op | source)
XLA Modules:
  0.0 507.2 jit_solution(13660523204946220731)
XLA Ops:
  28.4 8.2 %collective-permute-done.1 = bf16[256,640]{1,0:T(8,128)(2,1)} collective-permute-done((bf16[256,640]{1,0:T(8,128)(2,1)}, bf16[256,640]{1,0:T(8,128)(2,1)}, u32[]{:S(2)}, u32[]{:S(2)}) %collective-permute-start.1) | collective-permute-done | bytes 327712 | tf_op jit(solution)/shard_map/ppermute | solution.py:598
  39.4 9.1 %collective-permute-done.4 = bf16[512,640]{1,0:T(8,128)(2,1)S(1)} collective-permute-done((bf16[512,640]{1,0:T(8,128)(2,1)S(1)}, bf16[512,640]{1,0:T(8,128)(2,1)S(1)}, u32[]{:S(2)}, u32[]{:S(2)}) %collective-permute-start.4) | collective-permute-done | bytes 655392 | tf_op jit(solution)/shard_map/ppermute | solution.py:602
  49.7 10.7 %collective-permute-done.5 = bf16[256,512]{1,0:T(8,128)(2,1)S(1)} collective-permute-done((bf16[256,512]{1,0:T(8,128)(2,1)S(1)}, bf16[256,512]{1,0:T(8,128)(2,1)S(1)}, u32[]{:S(2)}, u32[]{:S(2)}) %collective-permute-start.5) | collective-permute-done | bytes 262176 | tf_op jit(solution)/shard_map/ppermute | solution.py:598
  71.1 10.3 %collective-permute-done.7 = bf16[512,512]{1,0:T(8,128)(2,1)} collective-permute-done((bf16[512,512]{1,0:T(8,128)(2,1)}, bf16[512,512]{1,0:T(8,128)(2,1)}, u32[]{:S(2)}, u32[]{:S(2)}) %collective-permute-start.7) | collective-permute-done | bytes 524320 | tf_op jit(solution)/shard_map/ppermute | solution.py:602
  98.7 8.7 %collective-permute-done.14 = bf16[512,512]{1,0:T(8,128)(2,1)S(1)} collective-permute-done((bf16[512,512]{1,0:T(8,128)(2,1)S(1)}, bf16[512,512]{1,0:T(8,128)(2,1)S(1)}, u32[]{:S(2)}, u32[]{:S(2)}) %collective-permute-start.14) | collective-permute-done | bytes 524320 | tf_op jit(solution)/shard_map/ppermute | solution.py:602
  120.8 8.2 %attention_forward.1 = (bf16[1024,256]{1,0:T(8,128)(2,1)S(1)}, bf16[1024,384]{1,0:T(8,128)(2,1)S(1)}, f32[1024,128]{1,0:T(8,128)S(1)}) custom-call(bf16[1024,512]{1,0:T(8,128)(2,1)S(1)} %pad_maximum_fusion.4.qkv_ref, f32[1024,128]{1,0:T(8,128)S(1)} %get-tuple-element.252.cos_ref, f32[1024,128]{1,0:T(8,128)S(1)} %copy-done.11, ...), custom_call_target="tpu_custom_call" | custom-call | tf_op jit(solution)/shard_map/attention_forward/pallas_call | solution.py:495
  129.1 5.3 %collective-permute-done.16 = bf16[512,1024]{1,0:T(8,128)(2,1)S(1)} collective-permute-done((bf16[512,1024]{1,0:T(8,128)(2,1)S(1)}, bf16[512,1024]{1,0:T(8,128)(2,1)S(1)}, u32[]{:S(2)}, u32[]{:S(2)}) %collective-permute-start.16) | collective-permute-done | bytes 1048608 | tf_op jit(solution)/shard_map/ppermute | solution.py:602
  138.3 10.5 %ssd_forward.1 = (bf16[1024,768]{1,0:T(8,128)(2,1)S(1)}, bf16[1024,768]{1,0:T(8,128)(2,1)S(1)}, bf16[1024,768]{1,0:T(8,128)(2,1)}) custom-call(f32[1024,1024]{1,0:T(8,128)} %fusion.78.h_ref.prev_ref, f32[1024,256]{1,0:T(8,128)S(1)} %fusion.64.pair_ref.pair_prev_ref, bf16[1024,768]{1,0:T(8,128)(2,1)} %convolution_convert_fusion.7.z_ref, ...), custom_call_target="tpu_custom_call" | custom-call | tf_op jit(solution)/shard_map/ssd_forward/pallas_call | solution.py:178
  159.7 19.4 %collective-permute-done.21.far_a.far_b = bf16[1024,1024]{1,0:T(8,128)(2,1)S(1)} collective-permute-done((bf16[1024,1024]{1,0:T(8,128)(2,1)}, bf16[1024,1024]{1,0:T(8,128)(2,1)S(1)}, u32[]{:S(2)}, u32[]{:S(2)}) %collective-permute-start.21) | collective-permute-done | bytes 2097184 | tf_op jit(solution)/shard_map/ppermute | solution.py:602
  200.2 5.9 %convolution_convert_fusion.3 = bf16[1024,1024]{1,0:T(8,128)(2,1)} fusion(bf16[1024,1024]{1,0:T(8,128)(2,1)} %copy-done.112, bf16[1024,1024]{1,0:T(8,128)(2,1)S(1)} %unpack.9), kind=kOutput, calls=%fused_computation.44 | convolution fusion | flops 2148532224 | bytes 6291456 | tf_op jit(solution)/shard_map/dot_general | solution.py:27
  221.8 5.5 %fusion.81 = f32[1024,1024]{1,0:T(8,128)S(1)} fusion(bf16[1024,1024]{1,0:T(8,128)(2,1)} %copy-done.109, bf16[1024,1024]{1,0:T(8,128)(2,1)S(1)} %get-tuple-element.279), kind=kOutput, calls=%fused_computation.221 | convolution fusion | flops 2147483648 | bytes 8388608 | tf_op jit(solution)/shard_map/dot_general | solution.py:27
  244.5 5.0 multiply_reduce_fusion
  265.5 14.5 %collective-permute-done.26 = bf16[512,512]{1,0:T(8,128)(2,1)S(1)} collective-permute-done((bf16[512,512]{1,0:T(8,128)(2,1)S(1)}, bf16[512,512]{1,0:T(8,128)(2,1)S(1)}, u32[]{:S(2)}, u32[]{:S(2)}) %collective-permute-start.26) | collective-permute-done | bytes 524320 | tf_op jit(solution)/shard_map/ppermute | solution.py:602
  293.8 9.3 %attention_backward.1 = bf16[1024,512]{1,0:T(8,128)(2,1)S(1)} custom-call(bf16[1024,512]{1,0:T(8,128)(2,1)S(1)} %copy-done.5, bf16[1024,384]{1,0:T(8,128)(2,1)S(1)} %copy-done.32, bf16[1024,256]{1,0:T(8,128)(2,1)S(1)} %copy-done.20, f32[8,1024]{1,0:T(8,128)S(1)} %slice_bitcast_fusion.2.lse_ref, f32[8,1024]{1,0:T(8,128)S(1)} %pad.22.delta_ref, ...), custom_call_target="tpu_custom_call" | custom-call | tf_op jit(solution)/shard_map/attention_backward/pallas_call | solution.py:555
  320.5 15.5 %collective-permute-done.30 = bf16[512,1024]{1,0:T(8,128)(2,1)S(1)} collective-permute-done((bf16[512,1024]{1,0:T(8,128)(2,1)}, bf16[512,1024]{1,0:T(8,128)(2,1)S(1)}, u32[]{:S(2)}, u32[]{:S(2)}) %collective-permute-start.30) | collective-permute-done | bytes 1048608 | tf_op jit(solution)/shard_map/ppermute | solution.py:602
  341.1 28.2 %ssd_backward.1 = (bf16[1024,1024]{1,0:T(8,128)(2,1)}, bf16[1024,256]{1,0:T(8,128)(2,1)S(1)}, f32[8,768]{1,0:T(8,128)S(1)}, f32[8,256]{1,0:T(8,128)S(1)}, f32[8,128]{1,0:T(8,128)S(1)}) custom-call(f32[1024,1024]{1,0:T(8,128)} %fusion.78.h_ref.prev_ref, f32[1024,1024]{1,0:T(8,128)} %fusion.78.h_ref.prev_ref, f32[1024,256]{1,0:T(8,128)S(1)} %copy-done.3, ...), custom_call_target="tpu_custom_call" | custom-call | tf_op jit(solution)/shard_map/ssd_backward/pallas_call | solution.py:370
  375.1 5.5 %convolution_convert_fusion.refs_0_ = bf16[1024,1024]{1,0:T(8,128)(2,1)} fusion(bf16[1024,1024]{1,0:T(8,128)(2,1)} %get-tuple-element.226, bf16[1024,1024]{1,0:T(8,128)(2,1)S(1)} %copy-done.78), kind=kOutput, calls=%fused_computation.41 | convolution fusion | flops 2148532224 | bytes 6291456 | tf_op jit(solution)/shard_map/dot_general | solution.py:27
  381.6 9.3 %products.1 = bf16[1024,1024]{1,0:T(8,128)(2,1)} custom-call(bf16[1024,1024]{1,0:T(8,128)(2,1)} %get-tuple-element.334.refs_0_, bf16[1024,256]{1,0:T(8,128)(2,1)S(1)} %get-tuple-element.330.refs_1_, bf16[1024,768]{1,0:T(8,128)(2,1)S(1)} %copy-done.22, bf16[1024,256]{1,0:T(8,128)(2,1)S(1)} %get-tuple-element.474.refs_3_, ...), custom_call_target="tpu_custom_call" | custom-call | tf_op jit(solution)/shard_map/products/pallas_call | solution.py:958
  413.1 7.7 %fusion.3.mine_ref = bf16[1024,1024]{1,0:T(8,128)(2,1)} fusion(bf16[1024,1024]{1,0:T(8,128)(2,1)S(1)} %get-tuple-element.198, bf16[1024,1024]{1,0:T(8,128)(2,1)} %collective-permute-done.36, bf16[1024,1024]{1,0:T(8,128)(2,1)} %products.1, f32[1024]{0:T(1024)S(1)} %fusion.27, f32[1024]{0:T(1024)S(1)} %copy-done.62, f32[1024]{0:T(1024)S(1)} %reduce, ...), kind=kLoop, calls=%fused_computation.7 | loop fusion | flops 19922944 | bytes 18898944 | tf_op jit(solution)/shard_map/convert_element_type | solution.py:1012
  432.8 18.0 %collective-permute-done.45 = bf16[256,1024]{1,0:T(8,128)(2,1)S(1)} collective-permute-done((bf16[256,1024]{1,0:T(8,128)(2,1)}, bf16[256,1024]{1,0:T(8,128)(2,1)S(1)}, u32[]{:S(2)}, u32[]{:S(2)}) %collective-permute-start.45) | collective-permute-done | bytes 524320 | tf_op jit(solution)/shard_map/ppermute | solution.py:598
  464.9 7.0 %store.2 = bf16[2048,1024]{1,0:T(8,128)(2,1)} custom-call(s32[6]{0:T(128)S(1)} %reshape.317.place, bf16[1024,1024]{1,0:T(8,128)(2,1)S(1)} %copy-done, bf16[512,1024]{1,0:T(8,128)(2,1)} %collective-permute-done.29.got_ref, bf16[512,1024]{1,0:T(8,128)(2,1)} %collective-permute-done.37.got2_ref), custom_call_target="tpu_custom_call" | custom-call | tf_op jit(solution)/shard_map/store/pallas_call | solution.py:848
  483.5 5.4 %collective-permute-done.50 = bf16[256,640]{1,0:T(8,128)(2,1)} collective-permute-done((bf16[256,640]{1,0:T(8,128)(2,1)}, bf16[256,640]{1,0:T(8,128)(2,1)}, u32[]{:S(2)}, u32[]{:S(2)}) %collective-permute-start.50) | collective-permute-done | bytes 327712 | tf_op jit(solution)/shard_map/ppermute | solution.py:598
  491.4 5.4 %collective-permute-done.51 = bf16[128,640]{1,0:T(8,128)(2,1)S(1)} collective-permute-done((bf16[128,640]{1,0:T(8,128)(2,1)S(1)}, bf16[128,640]{1,0:T(8,128)(2,1)S(1)}, u32[]{:S(2)}, u32[]{:S(2)}) %collective-permute-start.51) | collective-permute-done | bytes 163872 | tf_op jit(solution)/shard_map/ppermute | solution.py:598
  500.8 6.2 %store.3 = bf16[2048,1024]{1,0:T(8,128)(2,1)} custom-call(s32[6]{0:T(128)S(1)} %reshape.317.place, bf16[1024,1024]{1,0:T(8,128)(2,1)S(1)} %copy-done.1, bf16[512,1024]{1,0:T(8,128)(2,1)S(1)} %collective-permute-done.39.got_ref, bf16[512,1024]{1,0:T(8,128)(2,1)} %collective-permute-done.40.got2_ref), custom_call_target="tpu_custom_call" | custom-call | tf_op jit(solution)/shard_map/store/pallas_call | solution.py:848
  (513 shorter events, 266.1 us)
Async XLA Ops:
  18.9 18.9 %collective-permute-start.3 = (bf16[128,512]{1,0:T(8,128)(2,1)}, bf16[128,512]{1,0:T(8,128)(2,1)}, u32[]{:S(2)}, u32[]{:S(2)}) collective-permute-start(bf16[128,512]{1,0:T(8,128)(2,1)} %get-tuple-element.212), channel_id=1, source_target_pairs={{0,8},{4,12},{8,0},{12,4},{16,24},{20,28},{24,16},{28,20},{1,9},{5... | collective-permute-start | bytes 393224 | tf_op jit(solution)/shard_map/ppermute | solution.py:598
  60.3 23.5 %collective-permute-start.8 = (bf16[1024,640]{1,0:T(8,128)(2,1)}, bf16[1024,640]{1,0:T(8,128)(2,1)}, u32[]{:S(2)}, u32[]{:S(2)}) collective-permute-start(bf16[1024,640]{1,0:T(8,128)(2,1)} %pad_maximum_fusion.1.near_a.near_b), channel_id=1, source_target_pairs={{0,4},{1,3},{2,6},{3,1},{4,0},{5,7},{6,2},{7,5},{8,12},{9,11},{10,... | collective-permute-start | bytes 3932168 | tf_op jit(solution)/shard_map/ppermute | solution.py:602
  68.1 46.1 %collective-permute-start.13 = (bf16[128,512]{1,0:T(8,128)(2,1)}, bf16[128,512]{1,0:T(8,128)(2,1)S(1)}, u32[]{:S(2)}, u32[]{:S(2)}) collective-permute-start(bf16[128,512]{1,0:T(8,128)(2,1)} %copy-done.53), channel_id=1, source_target_pairs={{0,8},{4,12},{8,0},{12,4},{16,24},{20,28},{24,16},{28,20},{1,9},{5... | collective-permute-start | bytes 393224 | tf_op jit(solution)/shard_map/ppermute | solution.py:598
  68.1 25.7 %collective-permute-start.10 = (bf16[128,1024]{1,0:T(8,128)(2,1)S(1)}, bf16[128,1024]{1,0:T(8,128)(2,1)S(1)}, u32[]{:S(2)}, u32[]{:S(2)}) collective-permute-start(bf16[128,1024]{1,0:T(8,128)(2,1)S(1)} %get-tuple-element.230), channel_id=1, source_target_pairs={{0,8},{4,12},{8,0},{12,4},{16,24},{20,28},{24,16},{28,20},{1,9},{5... | collective-permute-start | bytes 786440 | tf_op jit(solution)/shard_map/ppermute | solution.py:598
  87.4 20.0 %collective-permute-start.15 = (bf16[1024,512]{1,0:T(8,128)(2,1)S(1)}, bf16[1024,512]{1,0:T(8,128)(2,1)S(1)}, u32[]{:S(2)}, u32[]{:S(2)}) collective-permute-start(bf16[1024,512]{1,0:T(8,128)(2,1)S(1)} %pad_maximum_fusion.2.near_a.near_b), channel_id=1, source_target_pairs={{0,4},{1,3},{2,6},{3,1},{4,0},{5,7},{6,2},{7,5},{8,12},{9,11},{10,... | collective-permute-start | bytes 3145736 | tf_op jit(solution)/shard_map/ppermute | solution.py:602
  94.3 24.7 %collective-permute-start.12 = (bf16[256,1024]{1,0:T(8,128)(2,1)S(1)}, bf16[256,1024]{1,0:T(8,128)(2,1)S(1)}, u32[]{:S(2)}, u32[]{:S(2)}) collective-permute-start(bf16[256,1024]{1,0:T(8,128)(2,1)S(1)} %pad_maximum_fusion.12), channel_id=1, source_target_pairs={{0,16},{4,20},{8,24},{12,28},{16,0},{20,4},{24,8},{28,12},{1,17},{... | collective-permute-start | bytes 1572872 | tf_op jit(solution)/shard_map/ppermute | solution.py:598
  108.8 20.2 %collective-permute-start.17 = (bf16[1024,512]{1,0:T(8,128)(2,1)S(1)}, bf16[1024,512]{1,0:T(8,128)(2,1)S(1)}, u32[]{:S(2)}, u32[]{:S(2)}) collective-permute-start(bf16[1024,512]{1,0:T(8,128)(2,1)S(1)} %pad_maximum_fusion.3.near_a.near_b), channel_id=1, source_target_pairs={{0,4},{1,3},{2,6},{3,1},{4,0},{5,7},{6,2},{7,5},{8,12},{9,11},{10,... | collective-permute-start | bytes 3145736 | tf_op jit(solution)/shard_map/ppermute | solution.py:602
  152.9 26.2 %collective-permute-start.21 = (bf16[1024,1024]{1,0:T(8,128)(2,1)}, bf16[1024,1024]{1,0:T(8,128)(2,1)S(1)}, u32[]{:S(2)}, u32[]{:S(2)}) collective-permute-start(bf16[1024,1024]{1,0:T(8,128)(2,1)} %pad_maximum_fusion.near_a.near_b), channel_id=1, source_target_pairs={{0,4},{1,3},{2,6},{3,1},{4,0},{5,7},{6,2},{7,5},{8,12},{9,11},{10,... | collective-permute-start | bytes 6291464 | tf_op jit(solution)/shard_map/ppermute | solution.py:602
  154.0 44.0 %collective-permute-start.22 = (bf16[1024,512]{1,0:T(8,128)(2,1)S(1)}, bf16[1024,512]{1,0:T(8,128)(2,1)S(1)}, u32[]{:S(2)}, u32[]{:S(2)}) collective-permute-start(bf16[1024,512]{1,0:T(8,128)(2,1)S(1)} %pad_maximum_fusion.6.near_a.near_b), channel_id=1, source_target_pairs={{0,4},{1,3},{2,6},{3,1},{4,0},{5,7},{6,2},{7,5},{8,12},{9,11},{10,... | collective-permute-start | bytes 3145736 | tf_op jit(solution)/shard_map/ppermute | solution.py:602
  199.0 37.0 %collective-permute-start.24 = (bf16[2,512,512]{2,1,0:T(8,128)(2,1)}, bf16[2,512,512]{2,1,0:T(8,128)(2,1)}, u32[]{:S(2)}, u32[]{:S(2)}) collective-permute-start(bf16[2,512,512]{2,1,0:T(8,128)(2,1)} %get-tuple-element.283), channel_id=1, source_target_pairs={{0,4},{1,3},{2,6},{3,1},{4,0},{5,7},{6,2},{7,5},{8,12},{9,11},{10,... | collective-permute-start | bytes 3145736 | tf_op jit(solution)/shard_map/ppermute | solution.py:602
  239.4 63.7 %collective-permute-start.27 = (bf16[2,512,1024]{2,1,0:T(8,128)(2,1)}, bf16[2,512,1024]{2,1,0:T(8,128)(2,1)}, u32[]{:S(2)}, u32[]{:S(2)}) collective-permute-start(bf16[2,512,1024]{2,1,0:T(8,128)(2,1)} %copy-done.63), channel_id=1, source_target_pairs={{0,4},{1,3},{2,6},{3,1},{4,0},{5,7},{6,2},{7,5},{8,12},{9,11},{10,... | collective-permute-start | bytes 6291464 | tf_op jit(solution)/shard_map/ppermute | solution.py:602
  242.5 72.5 %collective-permute-start.29 = (bf16[512,1024]{1,0:T(8,128)(2,1)}, bf16[512,1024]{1,0:T(8,128)(2,1)}, u32[]{:S(2)}, u32[]{:S(2)}) collective-permute-start(bf16[512,1024]{1,0:T(8,128)(2,1)} %constant_dynamic-slice_fusion.3), channel_id=1, source_target_pairs={{0,2},{2,0},{1,3},{3,1},{4,6},{6,4},{5,7},{7,5},{8,10},{10,8},{9,1... | collective-permute-start | bytes 3145736 | tf_op jit(solution)/shard_map/ppermute | solution.py:569
  249.5 30.5 %collective-permute-start.26 = (bf16[512,512]{1,0:T(8,128)(2,1)S(1)}, bf16[512,512]{1,0:T(8,128)(2,1)S(1)}, u32[]{:S(2)}, u32[]{:S(2)}) collective-permute-start(bf16[512,512]{1,0:T(8,128)(2,1)S(1)} %fusion.23), channel_id=1, source_target_pairs={{0,2},{1,5},{2,0},{3,7},{4,6},{5,1},{6,4},{7,3},{8,10},{9,13},{10,... | collective-permute-start | bytes 1572872 | tf_op jit(solution)/shard_map/ppermute | solution.py:602
  281.9 33.0 %collective-permute-start.28 = (bf16[256,512]{1,0:T(8,128)(2,1)}, bf16[256,512]{1,0:T(8,128)(2,1)}, u32[]{:S(2)}, u32[]{:S(2)}) collective-permute-start(bf16[256,512]{1,0:T(8,128)(2,1)} %fusion.41), channel_id=1, source_target_pairs={{0,16},{4,20},{8,24},{12,28},{16,0},{20,4},{24,8},{28,12},{1,17},{... | collective-permute-start | bytes 786440 | tf_op jit(solution)/shard_map/ppermute | solution.py:598
  314.9 54.4 %collective-permute-start.31 = (bf16[2,512,1024]{2,1,0:T(8,128)(2,1)}, bf16[2,512,1024]{2,1,0:T(8,128)(2,1)S(1)}, u32[]{:S(2)}, u32[]{:S(2)}) collective-permute-start(bf16[2,512,1024]{2,1,0:T(8,128)(2,1)} %get-tuple-element.318), channel_id=1, source_target_pairs={{0,4},{1,3},{2,6},{3,1},{4,0},{5,7},{6,2},{7,5},{8,12},{9,11},{10,... | collective-permute-start | bytes 6291464 | tf_op jit(solution)/shard_map/ppermute | solution.py:602
  315.1 20.9 %collective-permute-start.30 = (bf16[512,1024]{1,0:T(8,128)(2,1)}, bf16[512,1024]{1,0:T(8,128)(2,1)S(1)}, u32[]{:S(2)}, u32[]{:S(2)}) collective-permute-start(bf16[512,1024]{1,0:T(8,128)(2,1)} %fusion.17), channel_id=1, source_target_pairs={{0,2},{1,5},{2,0},{3,7},{4,6},{5,1},{6,4},{7,3},{8,10},{9,13},{10,... | collective-permute-start | bytes 3145736 | tf_op jit(solution)/shard_map/ppermute | solution.py:602
  338.4 30.9 %collective-permute-start.32 = (bf16[256,1024]{1,0:T(8,128)(2,1)}, bf16[256,1024]{1,0:T(8,128)(2,1)}, u32[]{:S(2)}, u32[]{:S(2)}) collective-permute-start(bf16[256,1024]{1,0:T(8,128)(2,1)} %fusion.22), channel_id=1, source_target_pairs={{0,16},{4,20},{8,24},{12,28},{16,0},{20,4},{24,8},{28,12},{1,17},{... | collective-permute-start | bytes 1572872 | tf_op jit(solution)/shard_map/ppermute | solution.py:598
  339.1 30.2 %collective-permute-start.33 = (bf16[128,512]{1,0:T(8,128)(2,1)S(1)}, bf16[128,512]{1,0:T(8,128)(2,1)S(1)}, u32[]{:S(2)}, u32[]{:S(2)}) collective-permute-start(bf16[128,512]{1,0:T(8,128)(2,1)S(1)} %fusion.54), channel_id=1, source_target_pairs={{0,8},{4,12},{8,0},{12,4},{16,24},{20,28},{24,16},{28,20},{1,9},{5... | collective-permute-start | bytes 393224 | tf_op jit(solution)/shard_map/ppermute | solution.py:598
  409.5 18.3 %collective-permute-start.42 = (f32[64,128]{1,0:T(8,128)S(1)}, f32[64,128]{1,0:T(8,128)S(1)}, u32[]{:S(2)}, u32[]{:S(2)}) collective-permute-start(f32[64,128]{1,0:T(8,128)S(1)} %pad_bitcast_fusion), channel_id=1, source_target_pairs={{0,2},{2,0},{1,3},{3,1},{4,6},{6,4},{5,7},{7,5},{8,10},{10,8},{9,1... | collective-permute-start | bytes 98312 | tf_op jit(solution)/shard_map/ppermute | solution.py:569
  424.0 26.9 %collective-permute-start.44 = (bf16[512,640]{1,0:T(8,128)(2,1)S(1)}, bf16[512,640]{1,0:T(8,128)(2,1)S(1)}, u32[]{:S(2)}, u32[]{:S(2)}) collective-permute-start(bf16[512,640]{1,0:T(8,128)(2,1)S(1)} %fusion.18), channel_id=1, source_target_pairs={{0,2},{1,5},{2,0},{3,7},{4,6},{5,1},{6,4},{7,3},{8,10},{9,13},{10,... | collective-permute-start | bytes 1966088 | tf_op jit(solution)/shard_map/ppermute | solution.py:602
  425.3 25.6 %collective-permute-start.45 = (bf16[256,1024]{1,0:T(8,128)(2,1)}, bf16[256,1024]{1,0:T(8,128)(2,1)S(1)}, u32[]{:S(2)}, u32[]{:S(2)}) collective-permute-start(bf16[256,1024]{1,0:T(8,128)(2,1)} %fusion.20), channel_id=1, source_target_pairs={{0,16},{4,20},{8,24},{12,28},{16,0},{20,4},{24,8},{28,12},{1,17},{... | collective-permute-start | bytes 1572872 | tf_op jit(solution)/shard_map/ppermute | solution.py:598
  428.8 45.0 %collective-permute-start.49 = (bf16[128,1024]{1,0:T(8,128)(2,1)}, bf16[128,1024]{1,0:T(8,128)(2,1)}, u32[]{:S(2)}, u32[]{:S(2)}) collective-permute-start(bf16[128,1024]{1,0:T(8,128)(2,1)} %fusion.39), channel_id=1, source_target_pairs={{0,8},{4,12},{8,0},{12,4},{16,24},{20,28},{24,16},{28,20},{1,9},{5... | collective-permute-start | bytes 786440 | tf_op jit(solution)/shard_map/ppermute | solution.py:598
  455.1 18.7 %collective-permute-start.48 = (bf16[128,1024]{1,0:T(8,128)(2,1)}, bf16[128,1024]{1,0:T(8,128)(2,1)S(1)}, u32[]{:S(2)}, u32[]{:S(2)}) collective-permute-start(bf16[128,1024]{1,0:T(8,128)(2,1)} %fusion.36), channel_id=1, source_target_pairs={{0,8},{4,12},{8,0},{12,4},{16,24},{20,28},{24,16},{28,20},{1,9},{5... | collective-permute-start | bytes 786440 | tf_op jit(solution)/shard_map/ppermute | solution.py:598
  463.5 25.4 %collective-permute-start.39 = (bf16[512,1024]{1,0:T(8,128)(2,1)}, bf16[512,1024]{1,0:T(8,128)(2,1)S(1)}, u32[]{:S(2)}, u32[]{:S(2)}) collective-permute-start(bf16[512,1024]{1,0:T(8,128)(2,1)} %constant_dynamic-slice_fusion.2), channel_id=1, source_target_pairs={{0,2},{2,0},{1,3},{3,1},{4,6},{6,4},{5,7},{7,5},{8,10},{10,8},{9,1... | collective-permute-start | bytes 3145736 | tf_op jit(solution)/shard_map/ppermute | solution.py:569
  (142 other events, 1031.8 us)

commit v3 on v2

--- a/solution.py
+++ b/solution.py
@@ -20,7 +20,11 @@
 HIGHEST = lax.Precision.HIGHEST
 BF = jnp.bfloat16
 F32 = jnp.float32
-VMEM_LIMIT = 48 * 1024 * 1024
+MIB = 1024 * 1024
+
+
+def cost(micros):
+    return pl.CostEstimate(flops=0, transcendentals=0, bytes_accessed=int(micros * 1.107e6))
 
 
 def dot(left, right, dims=((1,), (0,))):
@@ -198,7 +202,8 @@
             pltpu.VMEM((CHUNK, inner), F32),
             pltpu.VMEM((CHUNK, inner), F32),
         ],
-        compiler_params=pltpu.CompilerParams(vmem_limit_bytes=VMEM_LIMIT),
+        compiler_params=pltpu.CompilerParams(vmem_limit_bytes=20 * MIB),
+        cost_estimate=cost(10),
         name="ssd_forward",
     )(h1, pair, z, aux, segrow, xpar, bcpar, hpar)
 
@@ -206,7 +211,7 @@
 def ssd_backward_kernel(
     h_ref, prev_ref, pair_ref, pair_prev_ref, z_ref, dgated_ref, start_ref, aux_ref,
     segrow_ref, xpar_ref, bcpar_ref, hpar_ref,
-    dh_ref, dpair_ref, xacc_ref, bcacc_ref, hacc_ref,
+    dh_ref, dpair_ref, acc_ref,
     xbuf, pbuf, dxbuf, dpbuf, dstate, lanes2, step_s, enter_s, leave_s, came_s, dcame_s, sent_s,
     direct_s, inter_s, row_s, across_s,
 ):
@@ -222,9 +227,7 @@
         dxbuf[CHUNK : CHUNK + 8, :] = jnp.zeros((8, inner), F32)
         dpbuf[CHUNK : CHUNK + 8, :] = jnp.zeros((8, 2 * STATE), F32)
         dstate[...] = jnp.zeros_like(dstate)
-        xacc_ref[...] = jnp.zeros_like(xacc_ref)
-        bcacc_ref[...] = jnp.zeros_like(bcacc_ref)
-        hacc_ref[...] = jnp.zeros_like(hacc_ref)
+        acc_ref[...] = jnp.zeros_like(acc_ref)
         across_s[...] = jnp.zeros_like(across_s)
         lanes2[0:128, :] = head_lanes(inner)
         lanes2[128:256, :] = head_lanes(inner)
@@ -312,7 +315,7 @@
         sums.append(jnp.sum(dpre, axis=0, keepdims=True))
         sums.append(jnp.sum(dscan_f * act, axis=0, keepdims=True))
         sums.append(jnp.zeros((2, 128), F32))
-        xacc_ref[:, cols] += jnp.concatenate(sums, axis=0)
+        acc_ref[:, cols] += jnp.concatenate(sums, axis=0)
         dh_ref[:, place_of(cols, inner)] = dval.astype(BF)
     dxbuf[CHUNK : CHUNK + 8, :] = dxbuf[0:8, :]
     grad_inter_b = grad_inter_t.astype(BF)
@@ -333,7 +336,7 @@
         sums.append(jnp.sum(dpre * shifted_pair[k - 1], axis=0, keepdims=True))
     sums.append(jnp.sum(dpre, axis=0, keepdims=True))
     sums.append(jnp.zeros((3, 2 * STATE), F32))
-    bcacc_ref[...] += jnp.concatenate(sums, axis=0)
+    acc_ref[:, inner : inner + 2 * STATE] += jnp.concatenate(sums, axis=0)
     dpair_ref[...] = dval.astype(BF)
     dpbuf[CHUNK : CHUNK + 8, :] = dpbuf[0:8, :]
     lanes = lanes2[0:128, :]
@@ -351,8 +354,10 @@
     grad_decay = grad_decay + dot(strict_b, (step * direct_inter).astype(BF))
     dstep = direct + grad_decay * rate
     draw = dstep * sigmoid(dt_raw + hpar_ref[0:1, :])
-    hacc_ref[0:1, :] += jnp.sum(draw, axis=0, keepdims=True)
-    hacc_ref[1:2, :] += jnp.sum(grad_decay * step, axis=0, keepdims=True) * rate
+    acc_ref[:, inner + 2 * STATE :] += jnp.concatenate([
+        jnp.sum(draw, axis=0, keepdims=True),
+        jnp.sum(grad_decay * step, axis=0, keepdims=True) * rate,
+        jnp.zeros((6, 128), F32)], axis=0)
     mid = inner // 2
     dh_ref[:, mid : mid + 128] = jnp.where(lane < pairs, draw, 0.0).astype(BF)
     dh_ref[:, inner + 128 :] = jnp.where(lane >= pairs, draw, 0.0).astype(BF)
@@ -378,14 +383,12 @@
         ],
         out_specs=[
             rows(width), rows(2 * STATE),
-            fixed(8, inner), fixed(8, 2 * STATE), fixed(8, 128),
+            fixed(8, inner + 2 * STATE + 128),
         ],
         out_shape=[
             jax.ShapeDtypeStruct((length, width), BF),
             jax.ShapeDtypeStruct((length, 2 * STATE), BF),
-            jax.ShapeDtypeStruct((8, inner), F32),
-            jax.ShapeDtypeStruct((8, 2 * STATE), F32),
-            jax.ShapeDtypeStruct((8, 128), F32),
+            jax.ShapeDtypeStruct((8, inner + 2 * STATE + 128), F32),
         ],
         scratch_shapes=[
             pltpu.VMEM((CHUNK + 8, inner), F32),
@@ -405,7 +408,8 @@
             pltpu.VMEM((CHUNK, inner), BF),
             pltpu.VMEM((8, inner), F32),
         ],
-        compiler_params=pltpu.CompilerParams(vmem_limit_bytes=VMEM_LIMIT),
+        compiler_params=pltpu.CompilerParams(vmem_limit_bytes=20 * MIB),
+        cost_estimate=cost(28),
         name="ssd_backward",
     )(h1, h1, pair, pair, z, dgated, start, aux, segrow, xpar, bcpar, hpar)
 
@@ -487,7 +491,7 @@
                 parts.append(dot(probs, value))
                 lse = jnp.where(lane == 2 * g + s, peak + jnp.log(total), lse)
             out_ref[rows, 128 * g : 128 * g + 128] = jnp.concatenate(parts, axis=1).astype(BF)
-        lse_ref[rows, :] = lse
+        lse_ref[:, rows] = lse.T[0:8, :]
 
 
 def attention_forward(qkv, cosine, sine, aux, segrow):
@@ -497,9 +501,10 @@
         out_shape=[
             jax.ShapeDtypeStruct((length, 128 * KVHEADS), BF),
             jax.ShapeDtypeStruct((length, 128 * (KVHEADS + 1)), BF),
-            jax.ShapeDtypeStruct((length, 128), F32),
+            jax.ShapeDtypeStruct((8, length), F32),
         ],
-        compiler_params=pltpu.CompilerParams(vmem_limit_bytes=VMEM_LIMIT),
+        compiler_params=pltpu.CompilerParams(vmem_limit_bytes=20 * MIB),
+        cost_estimate=cost(8),
         name="attention_forward",
     )(qkv, cosine, sine, aux, segrow)
 
@@ -556,9 +561,144 @@
         attention_backward_kernel,
         out_shape=jax.ShapeDtypeStruct(qkv.shape, BF),
         scratch_shapes=[pltpu.VMEM((length, 128), F32), pltpu.VMEM((length, 128), F32)],
-        compiler_params=pltpu.CompilerParams(vmem_limit_bytes=VMEM_LIMIT),
+        compiler_params=pltpu.CompilerParams(vmem_limit_bytes=20 * MIB),
+        cost_estimate=cost(9),
         name="attention_backward",
     )(qkv, turned, datt, lse, delta, cosine, sine, aux, segrow)
+
+
+def feed_forward_kernel(
+    rows_ref, part_ref, got_ref, up_ref, gain_ref, gate_w, up_w, down_w,
+    state_ref, normed_ref, hidden_ref, dgate_ref, dup_ref, whole_ref, dnormed_ref,
+):
+    state = rows_ref[...].astype(F32) + (part_ref[...].astype(F32) + got_ref[...].astype(F32))
+    state_ref[...] = state
+    scale = lax.rsqrt(jnp.mean(state * state, axis=1, keepdims=True) + EPSILON)
+    normed = (state * scale * gain_ref[...]).astype(BF)
+    normed_ref[...] = normed.T
+    gate = dot(normed, gate_w[...])
+    up = dot(normed, up_w[...])
+    sig = sigmoid(gate)
+    act = gate * sig
+    hidden = (act * up).astype(BF)
+    hidden_ref[...] = hidden
+    whole_ref[...] = dot(hidden, down_w[...], ((1,), (1,))).astype(BF)
+    dhidden = dot(up_ref[...], down_w[...])
+    dup = (dhidden * act).astype(BF)
+    dup_ref[...] = dup
+    dgate = (dhidden * up * (sig * (1.0 + gate * (1.0 - sig)))).astype(BF)
+    dgate_ref[...] = dgate
+    dnormed_ref[...] = (
+        dot(dgate, gate_w[...], ((1,), (1,))) + dot(dup, up_w[...], ((1,), (1,)))).astype(BF)
+
+
+def feed_forward(rows, part, got, upstream, gain, gate_w, up_w, down_w):
+    length, width = rows.shape
+    units = gate_w.shape[1]
+    step = 256
+    block = lambda cols: pl.BlockSpec((step, cols), lambda i: (i, 0))
+    whole = lambda arr: pl.BlockSpec(arr.shape, lambda i: (0, 0))
+    shape = lambda cols, kind=BF: jax.ShapeDtypeStruct((length, cols), kind)
+    return pl.pallas_call(
+        feed_forward_kernel,
+        grid=(length // step,),
+        in_specs=[block(width)] * 4 + [whole(gain), whole(gate_w), whole(up_w), whole(down_w)],
+        out_specs=[block(width), pl.BlockSpec((width, step), lambda i: (0, i))]
+        + [block(units)] * 3 + [block(width)] * 2,
+        out_shape=[shape(width, F32), jax.ShapeDtypeStruct((width, length), BF)]
+        + [shape(units)] * 3 + [shape(width)] * 2,
+        compiler_params=pltpu.CompilerParams(vmem_limit_bytes=44 * MIB),
+        cost_estimate=cost(18),
+        name="feed_forward",
+    )(rows, part, got, upstream, gain, gate_w, up_w, down_w)
+
+
+def norm_gradient(grad, values, scale, gain):
+    weighted = grad * gain
+    inner = jnp.mean(weighted * values, axis=1, keepdims=True)
+    return scale * weighted - values * (scale * scale * scale * inner), jnp.sum(
+        grad * (values * scale), axis=0, keepdims=True)
+
+
+def middle_kernel(
+    state_ref, up_ref, dpart_ref, dgot_ref, gain_ref, scan_ref, z_ref, att_ref,
+    out_w, o_w, dmixed_ref, dgated_ref, dz_ref, datt_ref, delta_ref, gacc_ref, dmixed_t,
+):
+    @pl.when(pl.program_id(0) == 0)
+    def _():
+        gacc_ref[...] = jnp.zeros_like(gacc_ref)
+
+    state = state_ref[...]
+    scale = lax.rsqrt(jnp.mean(state * state, axis=1, keepdims=True) + EPSILON)
+    grad, gain_grad = norm_gradient(
+        dpart_ref[...].astype(F32) + dgot_ref[...].astype(F32), state, scale, gain_ref[...])
+    gacc_ref[0:1, :] += gain_grad
+    dmixed = (up_ref[...].astype(F32) + grad).astype(BF)
+    dmixed_ref[...] = dmixed
+    dmixed_t[...] = dmixed.T
+    dgated = dot(dmixed, out_w[...])
+    dgated_ref[...] = dgated.astype(BF)
+    gate = z_ref[...].astype(F32)
+    sig = sigmoid(gate)
+    dz_ref[...] = (dgated * scan_ref[...].astype(F32) * (sig * (1.0 + gate * (1.0 - sig)))).astype(BF)
+    datt = dot(dmixed, o_w[...]).astype(BF)
+    datt_ref[...] = datt
+    product = datt.astype(F32) * att_ref[...].astype(F32)
+    channel = lax.broadcasted_iota(jnp.int32, (product.shape[1], 128), 0)
+    head = lax.broadcasted_iota(jnp.int32, (product.shape[1], 128), 1)
+    delta = dot_exact(product, (channel // HD == head).astype(F32))
+    delta_ref[...] = delta.T[0:8, :]
+
+
+def middle(state, upstream, dpart, dgot, gain, scan, z, att, out_w, o_w):
+    length, width = state.shape
+    step = 256
+    block = lambda arr: pl.BlockSpec((step, arr.shape[1]), lambda i: (i, 0))
+    whole = lambda arr: pl.BlockSpec(arr.shape, lambda i: (0, 0))
+    like = lambda arr: jax.ShapeDtypeStruct(arr.shape, BF)
+    return pl.pallas_call(
+        middle_kernel,
+        grid=(length // step,),
+        in_specs=[block(arr) for arr in (state, upstream, dpart, dgot)]
+        + [whole(gain), block(scan), block(z), block(att), whole(out_w), whole(o_w)],
+        out_specs=[block(upstream)] + [block(scan)] * 2
+        + [block(att), pl.BlockSpec((8, step), lambda i: (0, i)), pl.BlockSpec((8, width), lambda i: (0, 0)),
+           pl.BlockSpec((width, step), lambda i: (0, i))],
+        out_shape=[like(upstream)] + [like(scan)] * 2 + [like(att)]
+        + [jax.ShapeDtypeStruct((8, length), F32), jax.ShapeDtypeStruct((8, width), F32),
+           jax.ShapeDtypeStruct((width, length), BF)],
+        compiler_params=pltpu.CompilerParams(vmem_limit_bytes=36 * MIB),
+        cost_estimate=cost(11),
+        name="middle",
+    )(state, upstream, dpart, dgot, gain, scan, z, att, out_w, o_w)
+
+
+def last_norm_kernel(dpart_ref, dgot_ref, rows_ref, dmixed_ref, scale_ref, gain_ref, out_ref, gacc_ref):
+    @pl.when(pl.program_id(0) == 0)
+    def _():
+        gacc_ref[...] = jnp.zeros_like(gacc_ref)
+
+    grad, gain_grad = norm_gradient(
+        dpart_ref[...].astype(F32) + dgot_ref[...].astype(F32), rows_ref[...].astype(F32),
+        scale_ref[...], gain_ref[...])
+    gacc_ref[0:1, :] += gain_grad
+    out_ref[...] = (dmixed_ref[...].astype(F32) + grad).astype(BF)
+
+
+def last_norm(dpart, dgot, rows, dmixed, scale, gain):
+    length, width = rows.shape
+    step = 256
+    block = pl.BlockSpec((step, width), lambda i: (i, 0))
+    return pl.pallas_call(
+        last_norm_kernel,
+        grid=(length // step,),
+        in_specs=[block] * 4 + [pl.BlockSpec((step, 1), lambda i: (i, 0)), pl.BlockSpec((1, width), lambda i: (0, 0))],
+        out_specs=[block, pl.BlockSpec((8, width), lambda i: (0, 0))],
+        out_shape=[jax.ShapeDtypeStruct((length, width), BF), jax.ShapeDtypeStruct((8, width), F32)],
+        compiler_params=pltpu.CompilerParams(vmem_limit_bytes=20 * MIB),
+        cost_estimate=cost(4.5),
+        name="last_norm",
+    )(dpart, dgot, rows, dmixed, scale, gain)
 
 
 def core_swap(value):
@@ -684,65 +824,104 @@
             ],
         ),
         out_shape=[jax.ShapeDtypeStruct((total, 2 * size), BF) for _, size in groups],
-        compiler_params=pltpu.CompilerParams(vmem_limit_bytes=VMEM_LIMIT),
+        compiler_params=pltpu.CompilerParams(vmem_limit_bytes=20 * MIB),
+        cost_estimate=cost(3),
         name="unpack",
     )(place, near, near, far, far)
 
 
-def pack_kernel(count, place, *refs):
-    ins, (send, two, keep) = refs[:count], refs[count:]
+def grads_kernel(spans, place, *refs):
+    count = len(spans)
+    lefts = refs[:count]
+    mines, others = refs[count : 2 * count], refs[2 * count : 3 * count]
+    send, two, keep, whole = refs[3 * count :]
+    step = pl.program_id(0)
+    for left, mine, other, (begin, end) in zip(lefts, mines, others, spans):
+
+        @pl.when((step >= begin) & (step < end))
+        def _():
+            both = jnp.concatenate([mine[...], other[...]], axis=1)
+            whole[...] = both if left is None else dot(left[...], both).astype(BF)
+
     first = place[0] == 0
-    step = keep.shape[0]
-    own = pl.ds(pl.multiple_of(place[1] * step, step), step)
-    neighbour = pl.ds(pl.multiple_of((1 - place[1]) * step, step), step)
-    at = 0
-    for ref in ins:
-        size = ref.shape[1] // 2
-        cols = slice(at, at + size)
-        mixed = (ref[neighbour, :size], ref[own, size:])
-        keep[:, cols] = ref[own, :size]
-        send[1, :, cols] = ref[neighbour, size:]
-        send[0, :, cols] = jnp.where(first, mixed[0], mixed[1])
-        two[:, cols] = jnp.where(first, mixed[1], mixed[0])
-        at += size
-
-
-def pack(grads, place):
-    total = grads[0].shape[0]
-    step = total // 8
-    cols = sum(grad.shape[1] for grad in grads) // 2
+    rows = keep.shape[0] // 4
+    for line in range(4):
+        at = pl.multiple_of(place[2 + line] * (2 * rows), 2 * rows)
+        own = pl.ds(at + pl.multiple_of(place[1] * rows, rows), rows)
+        neighbour = pl.ds(at + pl.multiple_of((1 - place[1]) * rows, rows), rows)
+        here = slice(line * rows, (line + 1) * rows)
+        one, other = whole[neighbour, :128], whole[own, 128:]
+        keep[here, :] = whole[own, :128]
+        send[1, here, :] = whole[neighbour, 128:]
+        send[0, here, :] = jnp.where(first, one, other)
+        two[here, :] = jnp.where(first, other, one)
+
+
+def grads(pairs, place):
+    total = pairs[0][1].shape[0]
+    spans, at = [], 0
+    for _, right in pairs:
+        tiles = right.shape[1] // 256
+        spans.append((at, at + tiles))
+        at += tiles
+    cols = 128 * at
+    lefts = [left for left, _ in pairs if left is not None]
+    keys = []
+    for left in lefts:
+        if not any(left is key for key in keys):
+            keys.append(left)
+    index_of = [None if left is None else [left is key for key in keys].index(True) for left, _ in pairs]
+
+    def kernel(place, *refs):
+        arrays, rest = refs[: len(keys)], refs[len(keys) :]
+        chosen = tuple(None if index is None else arrays[index] for index in index_of)
+        grads_kernel(spans, place, *chosen, *rest)
+
+    def view(right, span, side):
+        tiles = span[1] - span[0]
+        return pl.BlockSpec(
+            (right.shape[0], 128),
+            lambda i, place: (0, side * tiles + jnp.clip(i - span[0], 0, tiles - 1)))
+
+    views = [view(right, span, side) for side in range(2) for (_, right), span in zip(pairs, spans)]
+    rights = [right for _, right in pairs]
     return pl.pallas_call(
-        functools.partial(pack_kernel, len(grads)),
+        kernel,
         grid_spec=pltpu.PrefetchScalarGridSpec(
             num_scalar_prefetch=1,
-            grid=(4,),
-            in_specs=[
-                pl.BlockSpec((2 * step, grad.shape[1]), lambda i, place: (place[2 + i], 0)) for grad in grads
+            grid=(at,),
+            in_specs=[pl.BlockSpec(key.shape, lambda i, place: (0, 0)) for key in keys] + views,
+            out_specs=[
+                pl.BlockSpec((2, total // 2, 128), lambda i, _: (0, 0, i)),
+                pl.BlockSpec((total // 2, 128), lambda i, _: (0, i)),
+                pl.BlockSpec((total // 2, 128), lambda i, _: (0, i)),
             ],
-            out_specs=[
-                pl.BlockSpec((2, step, cols), lambda i, _: (0, i, 0)),
-                pl.BlockSpec((step, cols), lambda i, _: (i, 0)),
-                pl.BlockSpec((step, cols), lambda i, _: (i, 0)),
-            ],
+            scratch_shapes=[pltpu.VMEM((total, 256), BF)],
         ),
         out_shape=[
             jax.ShapeDtypeStruct((2, total // 2, cols), BF),
             jax.ShapeDtypeStruct((total // 2, cols), BF),
             jax.ShapeDtypeStruct((total // 2, cols), BF),
         ],
-        compiler_params=pltpu.CompilerParams(vmem_limit_bytes=VMEM_LIMIT),
-        name="pack",
-    )(place, *grads)
+        compiler_params=pltpu.CompilerParams(vmem_limit_bytes=28 * MIB),
+        cost_estimate=cost(6),
+        name="grads",
+    )(place, *keys, *rights, *rights)
 
 
 def long(value):
     return value.astype(F32)
 
 
+def beside(*parts):
+    return jnp.concatenate(parts, axis=1)
+
+
 class Scatter:
-    def __init__(self, grads, place):
-        self.rows = grads[0].shape[0] // 8
-        self.send, self.two, self.keep = pack(grads, place)
+    def __init__(self, pairs, place):
+        self.rows = pairs[0][1].shape[0] // 8
+        self.send, self.two, self.keep = grads(pairs, place)
+        self.extra = None
 
     def far_step(self, send):
         self.got = near_swap(send, 1)
@@ -755,7 +934,8 @@
         self.got2 = near_swap(part, 0)
 
     def kept(self, part):
-        return long(self.keep[part]) + long(self.got[0, part]) + long(self.got2[part])
+        total = long(self.keep[part]) + long(self.got[0, part]) + long(self.got2[part])
+        return total if self.extra is None else total + self.extra[part]
 
     def sum3(self, got2):
         self.got2 = got2
@@ -778,7 +958,8 @@
         return self.lower(slice(0, self.rows)) + long(got4)
 
 
-def scatter_whole(grads, dp, is_first):
+def scatter_whole(pairs, dp, is_first):
+    grads = [right if left is None else dot(left, right).astype(BF) for left, right in pairs]
     rows = grads[0].shape[0] // dp
     half_of = lambda grad, side: grad[:, side * (grad.shape[1] // 2) : (side + 1) * (grad.shape[1] // 2)]
     mine, other = [
@@ -791,14 +972,17 @@
     ).astype(F32)
 
 
-def load_kernel(place, tok_ref, cot_ref, gain_ref, rows_ref, cot_out, normed_ref, scale_ref):
+def load_kernel(place, tok_ref, cot_ref, gain_ref, rows_ref, cot_out, normed_ref, scale_ref, normed_t, cot_t):
     rows = tok_ref[...]
     rows_ref[...] = rows
     cot_out[...] = cot_ref[...]
+    cot_t[...] = cot_ref[...].T
     rows = rows.astype(F32)
     scale = lax.rsqrt(jnp.mean(rows * rows, axis=1, keepdims=True) + EPSILON)
     scale_ref[...] = scale
-    normed_ref[...] = (rows * scale * gain_ref[...]).astype(BF)
+    normed = (rows * scale * gain_ref[...]).astype(BF)
+    normed_ref[...] = normed
+    normed_t[...] = normed.T
 
 
 def load(tokens, cotangent, gain, half, length):
@@ -813,50 +997,56 @@
             num_scalar_prefetch=1,
             grid=(steps,),
             in_specs=[picked, picked, pl.BlockSpec((1, width), lambda i, place: (0, 0))],
-            out_specs=[plain, plain, plain, pl.BlockSpec((step, 1), lambda i, place: (i, 0))],
+            out_specs=[plain, plain, plain, pl.BlockSpec((step, 1), lambda i, place: (i, 0))]
+            + [pl.BlockSpec((width, step), lambda i, place: (0, i))] * 2,
         ),
         out_shape=[jax.ShapeDtypeStruct((length, width), BF)] * 3
-        + [jax.ShapeDtypeStruct((length, 1), F32)],
-        compiler_params=pltpu.CompilerParams(vmem_limit_bytes=VMEM_LIMIT),
+        + [jax.ShapeDtypeStruct((length, 1), F32)]
+        + [jax.ShapeDtypeStruct((width, length), BF)] * 2,
+        compiler_params=pltpu.CompilerParams(vmem_limit_bytes=20 * MIB),
+        cost_estimate=cost(4.5),
         name="load",
     )(half, tokens, cotangent, gain)
 
 
-def store_kernel(place, mine_ref, got_ref, got2_ref, out_ref):
+def store_kernel(place, *refs):
     step = pl.program_id(0)
-    for index, ref in enumerate((mine_ref, got_ref, got2_ref)):
+    for index, ref in enumerate(refs[:-1]):
 
         @pl.when((step >= place[2 * index]) & (step < place[2 * index + 1]))
         def _():
-            out_ref[...] = ref[...]
+            refs[-1][...] = ref[...]
 
 
 def part_of(mine, core):
     return lax.dynamic_slice_in_dim(mine, core * (mine.shape[0] // 2), mine.shape[0] // 2, 0)
 
 
-def store(mine, got, got2, half, core):
-    length, width = mine.shape
+def store(parts, half, core):
+    width = parts[0].shape[1]
+    length = sum(part.shape[0] for part in parts) // 2
     step = 256
     per = length // step
-    begin = jnp.stack(
-        [half * per, (1 - half) * per + core * (per // 2), (1 - half) * per + (1 - core) * (per // 2)])
-    many = jnp.array([per, per // 2, per // 2])
-    place = jnp.stack([begin, begin + many], axis=1).reshape(-1).astype(jnp.int32)
-    part = lambda index, size: pl.BlockSpec(
+    begin = [half * per, (1 - half) * per + core * (per // 2), (1 - half) * per + (1 - core) * (per // 2)]
+    if len(parts) == 4:
+        begin = [half * per + core * (per // 2), half * per + (1 - core) * (per // 2)] + begin[1:]
+    many = [part.shape[0] // step for part in parts]
+    place = jnp.stack([value for at, size in zip(begin, many) for value in (at, at + size)]).astype(jnp.int32)
+    view = lambda index, size: pl.BlockSpec(
         (step, width), lambda i, place: (jnp.clip(i - place[2 * index], 0, size - 1), 0))
     return pl.pallas_call(
         store_kernel,
         grid_spec=pltpu.PrefetchScalarGridSpec(
             num_scalar_prefetch=1,
             grid=(2 * per,),
-            in_specs=[part(0, per), part(1, per // 2), part(2, per // 2)],
+            in_specs=[view(index, size) for index, size in enumerate(many)],
             out_specs=pl.BlockSpec((step, width), lambda i, place: (i, 0)),
         ),
         out_shape=jax.ShapeDtypeStruct((2 * length, width), BF),
-        compiler_params=pltpu.CompilerParams(vmem_limit_bytes=VMEM_LIMIT),
+        compiler_params=pltpu.CompilerParams(vmem_limit_bytes=20 * MIB),
+        cost_estimate=cost(5),
         name="store",
-    )(place, mine, got, got2)
+    )(place, *parts)
 
 
 def first_piece_kernel(slot, x_ref, dt_ref, bc_ref, key_ref, value_ref, out_ref):
@@ -882,7 +1072,8 @@
         in_specs=[pl.BlockSpec(memory_space=pltpu.SMEM)] + [vmem] * 5,
         out_specs=vmem,
         out_shape=jax.ShapeDtypeStruct((x.shape[0], x.shape[1] + 256), BF),
-        compiler_params=pltpu.CompilerParams(vmem_limit_bytes=VMEM_LIMIT),
+        compiler_params=pltpu.CompilerParams(vmem_limit_bytes=20 * MIB),
+        cost_estimate=cost(1),
         name="first_piece",
     )(slot[None].astype(jnp.int32), x, dt, bc, key, value)
 
@@ -907,7 +1098,8 @@
             shape(z.shape[1] + q.shape[1]), shape(out_w.shape[0] + o.shape[0]),
             shape(gate.shape[1] + up.shape[1]), shape(down.shape[0]),
         ],
-        compiler_params=pltpu.CompilerParams(vmem_limit_bytes=VMEM_LIMIT),
+        compiler_params=pltpu.CompilerParams(vmem_limit_bytes=20 * MIB),
+        cost_estimate=cost(1),
         name="other_pieces",
     )(z, q, out_w, o, gate, up, down)
 
@@ -938,7 +1130,8 @@
             out_specs=[spec, spec],
         ),
         out_shape=[jax.ShapeDtypeStruct((total, 256), BF)] * 2,
-        compiler_params=pltpu.CompilerParams(vmem_limit_bytes=VMEM_LIMIT),
+        compiler_params=pltpu.CompilerParams(vmem_limit_bytes=20 * MIB),
+        cost_estimate=cost(2),
         name="shared_rows",
     )(jnp.stack([half, core]).astype(jnp.int32), grad_bc, grad_kv)
 
@@ -962,26 +1155,14 @@
         + [pl.BlockSpec(right.shape, lambda i: (0, 0)) for right in rights],
         out_specs=pl.BlockSpec((step, width), lambda i: (i, 0)),
         out_shape=jax.ShapeDtypeStruct((length, width), dtype),
-        compiler_params=pltpu.CompilerParams(vmem_limit_bytes=VMEM_LIMIT),
+        compiler_params=pltpu.CompilerParams(vmem_limit_bytes=28 * MIB),
+        cost_estimate=cost(6),
         name="products",
     )(*lefts, *rights)
 
 
-def core_sum(part):
-    part = part.astype(BF)
-    return part.astype(F32) + core_swap(part).astype(F32)
-
-
 def wide(mine, other, width):
     return jnp.concatenate([mine[:, :width], other[:, :width]], axis=1)
-
-
-def norm_back(grad, values, scale, gain):
-    weighted = grad * gain
-    inner = jnp.mean(weighted * values, axis=-1, keepdims=True)
-    return scale * weighted - values * (scale * scale * scale * inner), jnp.sum(
-        grad * (values * scale), axis=0
-    )
 
 
 def body(
@@ -1022,6 +1203,13 @@
         seg = lax.dynamic_index_in_dim(segments, half, 0, keepdims=False)
         return segment_tables(seg) + rope_tables(length)
 
+    def own_sums(mine, other):
+        low, at = 2 * inner, 2 * inner + 2 * STATE
+        return jnp.concatenate([
+            mine[:, :inner] + other[:, inner:low], mine[:, low:at] + other[:, low:at],
+            mine[:, at : at + heads] + other[:, at + heads : at + 2 * heads],
+            jnp.zeros((8, 128 - heads), F32), mine[:, at + 128 :] + other[:, at + 128 :]], axis=1)
+
     piece1 = first_piece(slot, mamba_input_weight, w_dt, w_bc, w_k, w_v)
     rest = (mamba_gate_weight, w_q, mamba_output_weight, w_o, w_gate, w_up, w_down)
     shapes1 = ((0, inner + 128), (inner + 128, 128))
@@ -1029,22 +1217,24 @@
     shapes4 = ((0, hidden_cols), (hidden_cols, hidden_cols))
     shapes5 = ((0, hidden_cols),)
     g1, g2, g3, g4, g5 = [Gather() for _ in range(5)]
+    scan_params = (convolution_input_taps, convolution_input_bias, dt_bias, a_log, d_skip)
     if ringed:
         g1.along(piece1)
-        held = order(g1.first, tokens, cotangent, segments, *rest)
+        held = order(g1.first, tokens, cotangent, segments, *rest, *scan_params)
         first1, tokens, cotangent, segments = held[:4]
-        pieces = other_pieces(*held[4:])
+        convolution_input_taps, convolution_input_bias, dt_bias, a_log, d_skip = held[11:]
+        pieces = other_pieces(*held[4:11])
         pair1, *pieces = order(g1.join(first1), *pieces)
         g1.across(pair1)
-        for g, piece in zip((g2, g3, g4, g5), pieces):
-            g.along(piece)
+        piece2, piece3, piece4, piece5 = pieces
+        g2.along(piece2)
     else:
         pieces = (
             jnp.concatenate([short(mamba_gate_weight), short(w_q)], axis=1),
             jnp.concatenate([short(mamba_output_weight).T, short(w_o).T], axis=1),
             jnp.concatenate([short(w_gate), short(w_up)], axis=1), short(w_down).T)
         ways = [gather_whole(piece, dp, is_first) for piece in (piece1,) + pieces]
-    rows_b, upstream, normed, scale = load(tokens, cotangent, gain_in, own, length)
+    rows_b, upstream, normed, scale, normed_t, upstream_t = load(tokens, cotangent, gain_in, own, length)
     aux, segrow, cosine, sine = tables(segments)
     seg_line = aux[:, 0][None]
     per_head = jnp.pad(jnp.stack([dt_bias, a_log, d_skip]), ((0, 5), (0, 128 - heads)))
@@ -1061,24 +1251,27 @@
     hpar = jnp.concatenate(
         [head_par[:1], jnp.where(lane, -jnp.exp(head_par[1:]), 0.0), jnp.zeros((6, 128), F32)], axis=0)
     bcpar = jnp.concatenate([conv_bc, conv_bc_bias[None], jnp.zeros((3, conv_bc.shape[1]), F32)], axis=0)
-    rows = rows_b.astype(F32)
 
     if ringed:
-        second1, normed, aux, cosine, sine, xpar, hpar = order(
-            g1.second, normed, aux, cosine, sine, xpar, hpar)
-        quad1, first2 = order(g1.join2(second1), g2.first)
+        second1, first2, normed, aux, cosine, sine, xpar, hpar = order(
+            g1.second, g2.first, normed, aux, cosine, sine, xpar, hpar)
+        quad1, pair2, piece3 = order(g1.join2(second1), g2.join(first2), piece3)
         g1.near_step(quad1)
-        pair2, third1 = order(g2.join(first2), g1.third)
         g2.across(pair2)
-        near1, second2 = order(g1.join3(third1), g2.second)
+        g3.along(piece3)
+        third1, second2, first3 = order(g1.third, g2.second, g3.first)
+        near1, quad2, pair3, piece4 = order(g1.join3(third1), g2.join2(second2), g3.join(first3), piece4)
         g1.far_step(near1)
-        quad2, first3 = order(g2.join2(second2), g3.first)
         g2.near_step(quad2)
-        pair3, third2 = order(g3.join(first3), g2.third)
         g3.across(pair3)
-        near2, far1 = order(g2.join3(third2), g1.far)
+        g4.along(piece4)
+        far1, third2, second3, first4 = order(g1.far, g2.third, g3.second, g4.first)
+        near2, quad3, pair4, piece5 = order(g2.join3(third2), g3.join2(second3), g4.join(first4), piece5)
         g2.far_step(near2)
-        ways1 = (g1.near, far1)
+        g3.near_step(quad3)
+        g4.across(pair4)
+        g5.along(piece5)
+        ways1 = (near1, far1)
     else:
         ways1 = ways[0]
     weight1, quarters = unpack(*ways1, route, shapes1)
@@ -1086,12 +1279,6 @@
     quarters = jnp.where(is_first, quarters, swap_halves(quarters))
     others = core_swap(quarters)
     h1 = dot(normed, weight1)
-    if ringed:
-        h1, second3, first4 = order(h1, g3.second, g4.first)
-        quad3, pair4 = g3.join2(second3), g4.join(first4)
-        quad3, pair4, others = order(quad3, pair4, others)
-        g3.near_step(quad3)
-        g4.across(pair4)
     c0 = jnp.where(first_core, quarters, others)
     c1 = jnp.where(first_core, others, quarters)
     weight_bc = jnp.concatenate([c0[:, :128], c1[:, :128]], axis=1)
@@ -1099,230 +1286,203 @@
     pair = dot(normed, weight_bc)
     keyvalue = short(dot(normed, weight_kv))
     if ringed:
-        third3, pair, keyvalue = order(g3.third, pair, keyvalue)
-        near3, far2 = order(g3.join3(third3), g2.far)
+        far2, third3, second4, first5, h1, pair, keyvalue = order(
+            g2.far, g3.third, g4.second, g5.first, h1, pair, keyvalue)
+        near3, quad4, pair5 = order(g3.join3(third3), g4.join2(second4), g5.join(first5))
         g3.far_step(near3)
-        ways2 = (g2.near, far2)
+        g4.near_step(quad4)
+        g5.across(pair5)
+        ways2 = (near2, far2)
     else:
         ways2 = ways[1]
     weight_z, weight_q = unpack(*ways2, route, shapes2)
     z = short(dot(normed, weight_z))
     qkv = jnp.concatenate([short(dot(normed, weight_q)), keyvalue], axis=1)
-    if ringed:
-        second4, first5, z, qkv = order(g4.second, g5.first, z, qkv)
-        quad4, pair5, qkv = order(g4.join2(second4), g5.join(first5), qkv)
-        g4.near_step(quad4)
-        g5.across(pair5)
 
     attended, turned, lse = attention_forward(qkv, cosine, sine, aux, seg_line)
     if ringed:
-        third4, far3, attended = order(g4.third, g3.far, attended)
-        near4, second5 = order(g4.join3(third4), g5.second)
+        far3, third4, second5, attended, z = order(g3.far, g4.third, g5.second, attended, z)
+        near4, quad5, z = order(g4.join3(third4), g5.join2(second5), z)
         g4.far_step(near4)
-        quad5, z = order(g5.join2(second5), z)
         g5.near_step(quad5)
-        ways3 = (g3.near, far3)
+        ways3 = (near3, far3)
     else:
         ways3 = ways[2]
     gated, scan, start = ssd_forward(h1, pair, z, aux, segrow, xpar, bcpar, hpar)
     weight_out, weight_o = unpack(*ways3, route, shapes3)
+    mixed = products([gated, attended], [weight_out, weight_o], BF)
+    mixed_got = core_swap(mixed)
+
     if ringed:
-        third5, gated, weight_out = order(g5.third, gated, weight_out)
-        near5, gated = order(g5.join3(third5), gated)
+        third5, mixed = order(g5.third, mixed)
+        near5 = order(g5.join3(third5))
         g5.far_step(near5)
-    mixed = dot(gated, weight_out, ((1,), (1,))) + dot(attended, weight_o, ((1,), (1,)))
-    state = rows + core_sum(mixed)
-
-    scale_ffn = lax.rsqrt(jnp.mean(state * state, axis=-1, keepdims=True) + EPSILON)
-    normed_ffn = short(state * scale_ffn * gain_ffn)
-    if ringed:
-        normed_ffn, far4 = order(normed_ffn, g4.far)
-        ways4 = (g4.near, far4)
+        far4 = order(g4.far)
+        ways4 = (near4, far4)
     else:
         ways4 = ways[3]
     weight_gate, weight_up = unpack(*ways4, route, shapes4)
-    gate = dot(normed_ffn, weight_gate)
-    up = dot(normed_ffn, weight_up)
-    sig = jax.nn.sigmoid(gate)
-    hidden = short(gate * sig * up)
-    grad_down = short(dot(upstream, hidden, cols))
     if ringed:
-        s5 = Scatter([grad_down], route)
-        send5, hidden, far5 = order(s5.send, hidden, g5.far)
-        s5.far_step(send5)
-        ways5 = (g5.near, far5)
+        weight_gate, weight_up, far5, mixed_got = order(weight_gate, weight_up, g5.far, mixed_got)
+        ways5 = (near5, far5)
     else:
         ways5 = ways[4]
     (weight_down,) = unpack(*ways5, route, shapes5)
-    whole = short(dot(hidden, weight_down, ((1,), (1,))))
+    state, normed_ffn_t, hidden, dgate, dup, whole, dnormed_part = feed_forward(
+        rows_b, mixed, mixed_got, upstream, gain_ffn, weight_gate, weight_up, weight_down)
+    whole_got = core_swap(whole)
+    dnormed_got = core_swap(dnormed_part)
+    down_pairs = [(upstream_t, hidden)]
+    ffn_pairs = [(normed_ffn_t, dgate), (normed_ffn_t, dup)]
     if ringed:
-        whole, upstream = order(whole, upstream)
-    whole_got = core_swap(whole)
-
-    dhidden = dot(upstream, weight_down)
-    dgate = short(dhidden * up * (sig * (1.0 + gate * (1.0 - sig))))
-    dup = short(dhidden * (gate * sig))
-    grad_gate = short(dot(normed_ffn, dgate, cols))
-    grad_up = short(dot(normed_ffn, dup, cols))
+        s5 = Scatter(down_pairs, route)
+        send5, normed_ffn_t, whole_got = order(s5.send, normed_ffn_t, whole_got)
+        s5.far_step(send5)
+        ffn_pairs = [(normed_ffn_t, dgate), (normed_ffn_t, dup)]
+        s4 = Scatter(ffn_pairs, route)
+    out_mine = short(state + (long(whole) + long(whole_got)))
     if ringed:
-        s4 = Scatter([grad_gate, grad_up], route)
-        send4, whole_got, dgate, dup = order(s4.send, whole_got, dgate, dup)
+        send4, got5, dnormed_got = order(s4.send, s5.got, dnormed_got)
+        part5, send4, dnormed_got = order(s5.sum2(got5), send4, dnormed_got)
         s4.far_step(send4)
-    out_mine = short(state + (long(whole) + long(whole_got)))
-    dnormed_part = short(dot(dgate, weight_gate, ((1,), (1,))) + dot(dup, weight_up, ((1,), (1,))))
+        s5.near_step(part5)
+    dmixed, dgated, dz, datt, delta, gacc_ffn, dmixed_t = middle(
+        state, upstream, dnormed_part, dnormed_got, gain_ffn, scan, z, attended, weight_out, weight_o)
+    dqkv = attention_backward(qkv, turned, datt, lse, delta, cosine, sine, aux, seg_line)
     if ringed:
-        dnormed_part, out_mine, got5 = order(dnormed_part, out_mine, s5.got)
-    dnormed_got = core_swap(dnormed_part)
-    if ringed:
-        part5, dnormed_got = order(s5.sum2(got5), dnormed_got)
-        s5.near_step(part5)
-    out_got = half_swap(part_of(out_mine, core))
-    dstate_norm, grad_gain_ffn = norm_back(
-        long(dnormed_part) + long(dnormed_got), state, scale_ffn, gain_ffn)
-    dstate = long(upstream) + dstate_norm
-    dmixed = short(dstate)
-
-    dgated = dot(dmixed, weight_out)
-    gate_z = long(z)
-    sig_z = jax.nn.sigmoid(gate_z)
-    dz = short(dgated * long(scan) * (sig_z * (1.0 + gate_z * (1.0 - sig_z))))
-    dgated = short(dgated)
-    datt = short(dot(dmixed, weight_o))
-    if ringed:
-        dgated, dz, datt, got2_5 = order(dgated, dz, datt, s5.got2)
-        third_5, datt, dz = order(s5.sum3(got2_5), datt, dz)
-        s5.across(third_5)
-    delta = jnp.sum((long(datt) * long(attended)).reshape(length, -1, HD), axis=-1).T
-    delta = jnp.pad(delta, ((0, 8 - delta.shape[0]), (0, 0)))
-    dqkv = attention_backward(
-        qkv, turned, datt, lse[:, :8].T, delta, cosine, sine, aux, seg_line)
-    if ringed:
-        dqkv, got4 = order(dqkv, s4.got)
-        part4, dqkv = order(s4.sum2(got4), dqkv)
+        dqkv, got4, got2_5, out_mine = order(dqkv, s4.got, s5.got2, out_mine)
+        part4, dqkv, dz = order(s4.sum2(got4), dqkv, dz)
         s4.near_step(part4)
     dqry, dkv = dqkv[:, : 2 * qcols], dqkv[:, 2 * qcols :]
-    second_grads = [
-        short(dot(dmixed, gated, cols)), short(dot(dmixed, attended, cols)),
-        short(dot(normed, dz, cols)), short(dot(normed, dqry, cols))]
+    second_pairs = [(dmixed_t, gated), (dmixed_t, attended), (normed_t, dz), (normed_t, dqry)]
+    grad_kv = short(dot(normed_t, dkv))
     if ringed:
-        s2 = Scatter(second_grads, route)
-        send2, got3_5, out_got = order(s2.send, s5.got3, out_got)
+        s2 = Scatter(second_pairs, route)
+        send2, got2_4, grad_kv = order(s2.send, s4.got2, grad_kv)
+        third_4, send2, dgated = order(beside(s4.sum3(got2_4), s5.sum3(got2_5)), send2, dgated)
         s2.far_step(send2)
-        fourth_5, got2_4 = order(s5.sum4(got3_5), s4.got2)
-        s5.along(fourth_5)
-        third_4, dgated = order(s4.sum3(got2_4), dgated)
-        s4.across(third_4)
-    dh1, dpair, xacc, bcacc, hacc = ssd_backward(
+        got3_4 = dp_swap(third_4, BITS[1])
+    dh1, dpair, acc = ssd_backward(
         h1, pair, z, dgated, start, aux, segrow, xpar, bcpar, hpar)
     if ringed:
-        dh1, dpair, got_2, got3_4, got4_5 = order(dh1, dpair, s2.got, s4.got3, s5.got4)
-        part2, fourth_4, dh1, dpair = order(s2.sum2(got_2), s4.sum4(got3_4), dh1, dpair)
+        dh1, dpair, acc, got_2, got3_4 = order(dh1, dpair, acc, s2.got, got3_4)
+        part2, fourth_4, dh1, dpair, out_part, acc = order(
+            s2.sum2(got_2),
+            beside(s4.sum4(got3_4[:, : 2 * hidden_cols]), s5.sum4(got3_4[:, 2 * hidden_cols :])),
+            dh1, dpair, part_of(out_mine, core), jnp.concatenate([acc, gacc_ffn], axis=1))
         s2.near_step(part2)
-        s4.along(fourth_4)
-
-    grad1 = short(dot(normed, dh1, cols))
-    grad_bc = short(dot(normed, dpair, cols))
-    grad_kv = flips(short(dot(normed, dkv, cols)))
-    keep_shared, send_shared = shared_rows(grad_bc, grad_kv, half, core)
-    if ringed:
-        send_shared, dh1, grad1 = order(send_shared, dh1, grad1)
+        got4_4 = dp_swap(fourth_4, BITS[0])
+        acc_got = dp_swap(acc, BITS[1])
+    else:
+        acc = jnp.concatenate([acc, gacc_ffn], axis=1)
+        out_part = part_of(out_mine, core)
+    out_got = half_swap(out_part)
+
+    grad_bc = short(dot(normed_t, dpair))
+    keep_shared, send_shared = shared_rows(grad_bc, flips(grad_kv), half, core)
     shared_got = core_swap(send_shared)
-    out_got2 = core_swap(out_got)
-    bc_got = core_swap(bcacc)
     dnormed_part = products(
         [dh1, dpair, dz, dqry, dkv], [weight1, weight_bc, weight_z, weight_q, weight_kv], BF)
+    dnormed_send = part_of(dnormed_part, 1 - core)
+    dnormed_own = part_of(dnormed_part, core)
     if ringed:
-        dnormed_part, shared_got, got2_2 = order(dnormed_part, shared_got, s2.got2)
-    dnormed_got = core_swap(dnormed_part)
+        dnormed_send, dnormed_own, got2_2, got4_4, shared_got, acc = order(
+            dnormed_send, dnormed_own, s2.got2, got4_4, shared_got, acc + acc_got)
+        third_2, acc, dnormed_send = order(s2.sum3(got2_2), acc, dnormed_send)
+        acc_got = dp_swap(acc, BITS[0])
+        s2.across(third_2)
+    dnormed_got = core_swap(dnormed_send)
     grad_shared = short(long(keep_shared) + long(shared_got))
-    last_grads = [grad1, grad_shared]
+    last_pairs = [(normed_t, dh1), (None, grad_shared)]
     if ringed:
-        s1 = Scatter(last_grads, route)
-        send1, third_2 = order(s1.send, s2.sum3(got2_2))
+        s1 = Scatter(last_pairs, route)
+        send1, acc, out_got = order(s1.send, acc + acc_got, out_got)
         s1.far_step(send1)
-        s2.across(third_2)
-        dnormed_got, third_2, out_got2 = order(dnormed_got, third_2, out_got2)
-    drows, grad_gain_in = norm_back(long(dnormed_part) + long(dnormed_got), rows, scale, gain_in)
-    grad_mine = short(dstate + drows)
-    output = store(out_mine, out_got, out_got2, half, core)
+        acc_got = half_swap(acc)
+        sent4 = s4.result(got4_4[:, : 2 * hidden_cols])
+        sent5 = s5.result(got4_4[:, 2 * hidden_cols :]).T
+    grad_mine, gacc_in = last_norm(
+        dnormed_own, dnormed_got, part_of(rows_b, core), part_of(dmixed, core), part_of(scale, core), gain_in)
     if ringed:
-        grad_mine, got_1 = order(grad_mine, s1.got)
-        part1 = order(s1.sum2(got_1))
+        grad_mine, gacc_in, sent4, sent5 = order(grad_mine, gacc_in, sent4, sent5)
+        gacc_in, got3_2 = order(gacc_in + core_swap(gacc_in), s2.got3)
+        fourth_2, gacc_in = order(s2.sum4(got3_2), gacc_in)
+        s2.along(fourth_2)
+        gains_got = half_swap(gacc_in)
+        out_got2 = core_swap(out_got)
+        output = store([out_mine, out_got, out_got2], half, core)
+        got_1, output, acc, gacc_in = order(s1.got, output, own_sums(acc, acc_got), gacc_in + gains_got)
+        part1, gacc_in, acc = order(s1.sum2(got_1), gacc_in, acc)
+        gains_got = dp_swap(gacc_in, BITS[2])
+        acc_got = dp_swap(acc, BITS[2])
         s1.near_step(part1)
-    grad_got = half_swap(part_of(grad_mine, core))
-
-    skip = xacc[5].reshape(2, heads, HD).sum(axis=-1)
-    stretches = []
-    for side in range(2):
-        stretches.append(jnp.concatenate([
-            xacc[:5, side * inner : (side + 1) * inner].reshape(-1),
-            hacc[0, side * heads : (side + 1) * heads], hacc[1, side * heads : (side + 1) * heads],
-            skip[side]]))
-    stretch = stretches[0].shape[0]
-    bc_sum = (bcacc + bc_got)[:5]
-    vector = jnp.concatenate([
-        jnp.where(is_first, stretches[0], stretches[1]), jnp.where(is_first, stretches[1], stretches[0]),
-        bc_sum.reshape(-1), grad_gain_in, grad_gain_ffn])
-    size = vector.shape[0]
-    vector = jnp.pad(vector, (0, -size % 1024)).reshape(-1, 128)
-    if ringed:
-        vector = vector + half_swap(vector)
-        vector, got2_1, got3_2 = order(vector + dp_swap(vector, 1), s1.got2, s2.got3)
-        third_1, fourth_2, vector = order(s1.sum3(got2_1), s2.sum4(got3_2), vector)
+        grad_got = half_swap(grad_mine)
+        got2_1, gacc_in, acc = order(s1.got2, gacc_in + gains_got, acc + acc_got)
+        bc_got = core_swap(acc[:, inner : inner + 2 * STATE])
+        blocks = gacc_in[0].reshape(4, 2 * rows_here)
+        gain_rows = jnp.concatenate([
+            lax.dynamic_slice(blocks, ((place_dp // 2) ^ i, (place_dp % 2) * rows_here), (1, rows_here))
+            for i in range(4)], axis=1).reshape(-1, 1)
+        s1.extra = jnp.pad(gain_rows, ((0, 0), (inner + 2 * heads, 256 - 2 * heads - 1)))
+        third_1 = order(s1.sum3(got2_1))
         s1.across(third_1)
-        s2.along(fourth_2)
-        vector = vector + dp_swap(vector, 2)
-        vector, got4_2, got4_4 = order(vector + dp_swap(vector, 4), s2.got4, s4.got4)
-        sent5, sent4, sent2 = s5.result(got4_5), s4.result(got4_4), s2.result(got4_2)
-        got3_1 = order(s1.got3)
-        fourth_1 = order(s1.sum4(got3_1))
+        sent2 = s2.result(s2.got4)
+        got3_1, sent2, grad_got, bc_got = order(s1.got3, sent2, grad_got, bc_got)
+        fourth_1, grad_got = order(s1.sum4(got3_1), grad_got)
         s1.along(fourth_1)
+        grad_near, grad_got2 = core_swap(grad_mine), core_swap(grad_got)
+        grad_near, grad_got2 = order(grad_near, grad_got2)
+        grad_tokens = store([grad_mine, grad_near, grad_got, grad_got2], half, core)
         sent1 = s1.result(s1.got4)
+        gain_grads_in = sent1[:, inner + 2 * heads]
     else:
-        vector = lax.psum(vector, ("dp", "head"), axis_index_groups=half_groups(dp))
+        acc = lax.psum(acc, "dp")
+        acc = own_sums(acc, half_swap(acc))
+        bc_got = core_swap(acc[:, inner : inner + 2 * STATE])
+        gain_sums = lax.psum(gacc_in[0], ("dp", "head"))
+        gain_grads_in = lax.dynamic_slice_in_dim(gain_sums, place_dp * rows_here, rows_here, 0)
         sent5, sent4, sent2, sent1 = [
-            scatter_whole(grads, dp, is_first)
-            for grads in ([grad_down], [grad_gate, grad_up], second_grads, last_grads)]
+            scatter_whole(pairs, dp, is_first)
+            for pairs in (down_pairs, ffn_pairs, second_pairs, last_pairs)]
+        sent5 = sent5.T
+        grad_got = half_swap(grad_mine)
+        output = store([out_mine, out_got, core_swap(out_got)], half, core)
+        grad_tokens = store([grad_mine, core_swap(grad_mine), grad_got, core_swap(grad_got)], half, core)
     sent3, sent2 = sent2[:, : inner + qcols], sent2[:, inner + qcols :]
-    grad_tokens = store(grad_mine, grad_got, core_swap(grad_got), half, core)
-    vector = vector.reshape(-1)[:size]
-    own = jnp.where(is_first, vector[:stretch], vector[stretch : 2 * stretch])
-    taps = own[: 5 * inner].reshape(5, inner)
-    per = own[5 * inner :].reshape(3, heads)
+    steps_at = inner + 2 * STATE
+    own = acc[:, :inner]
+    skip = own[5].reshape(heads, HD).sum(axis=-1)
     rank = place_dp * 4 + slot
-    bc_cols = conv_bc.shape[1] // (4 * dp)
-    at = 2 * stretch
-    bc_own = lax.dynamic_slice_in_dim(
-        vector[at : at + bc_sum.size].reshape(5, -1), rank * bc_cols, bc_cols, 1)
-    gain_grads = lax.dynamic_slice_in_dim(
-        vector[at + bc_sum.size :].reshape(2, width), place_dp * rows_here, rows_here, 1)
-
+    many = conv_bc.shape[1] // (4 * dp)
+    bc_own = lax.dynamic_slice_in_dim(acc[:, inner:steps_at] + bc_got, rank * many, many, 1)
+    per = acc[:2, steps_at : steps_at + heads]
+    gain_grads_ffn = lax.dynamic_slice_in_dim(acc[0, steps_at + 128 :], place_dp * rows_here, rows_here, 0)
     quarter_rows = rows_here // 4
     shared_own = sent1[:, inner + 128 :].reshape(4, quarter_rows, 128).swapaxes(0, 1).reshape(quarter_rows, -1)
     return (
         output,
         grad_tokens,
-        gain_grads[0],
+        gain_grads_in,
         sent2[:, :inner],
         sent1[:, :inner],
         sent1[:, inner : inner + heads] + sent1[:, inner + heads : inner + 2 * heads],
         shared_own[:, : 2 * STATE],
-        taps[:4],
-        taps[4],
+        own[:4],
+        own[4],
         bc_own[:4],
         bc_own[4],
         per[0],
         per[1],
-        per[2],
+        skip,
         sent2[:, inner:],
         shared_own[:, 2 * STATE : 2 * STATE + 128],
         shared_own[:, 2 * STATE + 128 :],
         sent3[:, inner:].T,
         sent3[:, :inner].T,
-        gain_grads[1],
+        gain_grads_ffn,
         sent4[:, :hidden_cols],
         sent4[:, hidden_cols:],
-        sent5.T,
+        sent5,
     )
 
 

time: 517 us -> 453 us (0.88)
  matrix products: 70.5 us -> 8.51 us
  Pallas kernels: 108 us -> 144 us
  other arithmetic: 75.7 us -> 41.2 us
  waiting for transfers between devices: 150 us -> 141 us
    dot_general x25 -> x7, matrix products: 70.5 us -> 8.51 us  [dot(): lax.dot_general(left, right, (dims, ((), ())), preferred_element_type=F32)]
    pallas_call x4 -> x7, Pallas kernels: 12.9 us -> 62 us  [the longest x4 30.2 us: grads(): pl.pallas_call(kernel, grid_spec=pltpu.PrefetchScalarGridSpec(num_scalar_...]
    ppermute x18, waiting for transfers between devices: 85.8 us -> 59.2 us  [near_swap(): lax.ppermute(value, ('dp', 'head'), pair_list(8, (step == 1, step == 0), 1))]
    ppermute x4 -> x5, waiting for transfers between devices: 0.01 us -> 13.2 us  [half_swap(): return lax.ppermute(value, 'head', [(0, 2), (2, 0), (1, 3), (3, 1)])]
    convert_element_type x5 -> x2, other arithmetic: 17.4 us -> 4.41 us  [body(): short = lambda value: value.astype(BF)]
    reduce_sum x5 -> x1, other arithmetic: 10.8 us -> 0.63 us  [body(): skip = own[5].reshape(heads, HD).sum(axis=-1)]
    ppermute x21 -> x20, waiting for transfers between devices: 59.2 us -> 68.1 us  [dp_swap(): return lax.ppermute(value, 'dp', [(d, d ^ bit) for d in range(8)])]
    unnamed x235 -> x237, local copies, waits for them, and re-layouts: 26.2 us -> 32.4 us
  transfers between devices with their start and end apart: 52 -> 54, of which waited for: 20 -> 31; matrix products, arithmetic and copies ran while one was open for 32% -> 14% of each run, Pallas kernels for 20% -> 26%
where the time goes in v3:
time: 453 us; the launch traced here: 444 us
  Pallas kernels  144 us (32%)
  waiting for transfers between devices  141 us (31%)
  starting transfers between devices  53.8 us (12%)
  local copies, waits for them, and re-layouts  51.9 us (11%)
  other arithmetic  41.2 us (9%)
  matrix products  8.51 us (2%)
    ppermute x20, waiting for transfers between devices, dp_swap(): return lax.ppermute(value, 'dp', [(d, d ^ bit) for d in range(8)])  68.1 us
    ppermute x18, waiting for transfers between devices, near_swap(): lax.ppermute(value, ('dp', 'head'), pair_list(8, (step == 1, step == 0), 1))  59.2 us
    unnamed x237, local copies, waits for them, and re-layouts  32.4 us
    pallas_call x4, Pallas kernels, grads(): pl.pallas_call(kernel, grid_spec=pltpu.PrefetchScalarGridSpec(num_scalar_...  30.2 us
    ppermute x20, starting transfers between devices, dp_swap(): return lax.ppermute(value, 'dp', [(d, d ^ bit) for d in range(8)])  25.8 us
    pallas_call x1, Pallas kernels, ssd_backward(): pl.pallas_call(ssd_backward_kernel, grid=(chunks,), in_specs=[rows(width)...  25.7 us
    pallas_call x1, Pallas kernels, feed_forward(): pl.pallas_call(feed_forward_kernel, grid=(length // step,), in_specs=[blo...  20.7 us
    ppermute x18, starting transfers between devices, near_swap(): lax.ppermute(value, ('dp', 'head'), pair_list(8, (step == 1, step == 0), 1))  20.2 us
  transfers between devices with their start and end apart: 54, of which 31 were waited for; matrix products, arithmetic and copies ran while one was open for 14% of the time, Pallas kernels for 26%

profile of v3, /device:TPU:0, one launch (start us, length us, event | category | flops | bytes accessed | tf_op | source)
XLA Modules:
  0.0 443.9 jit_solution(13705835997935683130)
XLA Ops:
  37.7 5.0 %collective-permute-done.6 = bf16[128,512]{1,0:T(8,128)(2,1)S(1)} collective-permute-done((bf16[128,512]{1,0:T(8,128)(2,1)S(1)}, bf16[128,512]{1,0:T(8,128)(2,1)S(1)}, u32[]{:S(2)}, u32[]{:S(2)}) %collective-permute-start.6) | collective-permute-done | bytes 131104 | tf_op jit(solution)/shard_map/ppermute | solution.py:738
  42.7 5.9 %collective-permute-done.5 = bf16[256,512]{1,0:T(8,128)(2,1)S(1)} collective-permute-done((bf16[256,512]{1,0:T(8,128)(2,1)S(1)}, bf16[256,512]{1,0:T(8,128)(2,1)S(1)}, u32[]{:S(2)}, u32[]{:S(2)}) %collective-permute-start.5) | collective-permute-done | bytes 262176 | tf_op jit(solution)/shard_map/ppermute | solution.py:738
  53.2 9.6 %collective-permute-done.10 = bf16[128,1024]{1,0:T(8,128)(2,1)} collective-permute-done((bf16[128,1024]{1,0:T(8,128)(2,1)S(1)}, bf16[128,1024]{1,0:T(8,128)(2,1)}, u32[]{:S(2)}, u32[]{:S(2)}) %collective-permute-start.10) | collective-permute-done | bytes 262176 | tf_op jit(solution)/shard_map/ppermute | solution.py:738
  66.0 6.0 %collective-permute-done.7.far_a.far_b = bf16[1024,640]{1,0:T(8,128)(2,1)S(1)} collective-permute-done((bf16[1024,640]{1,0:T(8,128)(2,1)S(1)}, bf16[1024,640]{1,0:T(8,128)(2,1)S(1)}, u32[]{:S(2)}, u32[]{:S(2)}) %collective-permute-start.7) | collective-permute-done | bytes 1310752 | tf_op jit(solution)/shard_map/ppermute | solution.py:742
  86.7 6.2 %collective-permute-done.14 = bf16[128,512]{1,0:T(8,128)(2,1)S(1)} collective-permute-done((bf16[128,512]{1,0:T(8,128)(2,1)S(1)}, bf16[128,512]{1,0:T(8,128)(2,1)S(1)}, u32[]{:S(2)}, u32[]{:S(2)}) %collective-permute-start.14) | collective-permute-done | bytes 131104 | tf_op jit(solution)/shard_map/ppermute | solution.py:738
  92.9 10.7 %collective-permute-done.13 = bf16[256,1024]{1,0:T(8,128)(2,1)S(1)} collective-permute-done((bf16[256,1024]{1,0:T(8,128)(2,1)S(1)}, bf16[256,1024]{1,0:T(8,128)(2,1)S(1)}, u32[]{:S(2)}, u32[]{:S(2)}) %collective-permute-start.13) | collective-permute-done | bytes 524320 | tf_op jit(solution)/shard_map/ppermute | solution.py:738
  109.9 8.3 %attention_forward.1 = (bf16[1024,256]{1,0:T(8,128)(2,1)S(1)}, bf16[1024,384]{1,0:T(8,128)(2,1)S(1)}, f32[8,1024]{1,0:T(8,128)S(1)}) custom-call(bf16[1024,512]{1,0:T(8,128)(2,1)S(1)} %pad_maximum_fusion.5.qkv_ref, f32[1024,128]{1,0:T(8,128)S(1)} %copy-done.22, f32[1024,128]{1,0:T(8,128)S(1)} %copy-done.23, f32[1024,128]{1,0:T(8,128)S(1)} %pad.16.segcol_ref.aux_ref, ...), custom_call_target="tpu_custom_call" | custom-call | bytes 8856000 | tf_op jit(solution)/shard_map/attention_forward/pallas_call | solution.py:499
  121.2 8.6 %collective-permute-done.16.far_a.far_b = bf16[1024,512]{1,0:T(8,128)(2,1)S(1)} collective-permute-done((bf16[1024,512]{1,0:T(8,128)(2,1)S(1)}, bf16[1024,512]{1,0:T(8,128)(2,1)S(1)}, u32[]{:S(2)}, u32[]{:S(2)}) %collective-permute-start.16) | collective-permute-done | bytes 1048608 | tf_op jit(solution)/shard_map/ppermute | solution.py:742
  132.5 8.4 %ssd_forward.1 = (bf16[1024,768]{1,0:T(8,128)(2,1)S(1)}, bf16[1024,768]{1,0:T(8,128)(2,1)S(1)}, bf16[1024,768]{1,0:T(8,128)(2,1)S(1)}) custom-call(f32[1024,1024]{1,0:T(8,128)S(1)} %fusion.59.h_ref.prev_ref, f32[1024,256]{1,0:T(8,128)S(1)} %fusion.47.pair_ref.pair_prev_ref, bf16[1024,768]{1,0:T(8,128)(2,1)S(1)} %convolution_convert_fusion.z_ref, ...), custom_call_target="tpu_custom_call" | custom-call | bytes 11070000 | tf_op jit(solution)/shard_map/ssd_forward/pallas_call | solution.py:182
  145.0 14.0 %collective-permute-done.19 = bf16[512,512]{1,0:T(8,128)(2,1)S(1)} collective-permute-done((bf16[512,512]{1,0:T(8,128)(2,1)S(1)}, bf16[512,512]{1,0:T(8,128)(2,1)S(1)}, u32[]{:S(2)}, u32[]{:S(2)}) %collective-permute-start.19) | collective-permute-done | bytes 524320 | tf_op jit(solution)/shard_map/ppermute | solution.py:742
  165.0 9.0 %collective-permute-done.21.far_a.far_b = bf16[1024,512]{1,0:T(8,128)(2,1)S(1)} collective-permute-done((bf16[1024,512]{1,0:T(8,128)(2,1)S(1)}, bf16[1024,512]{1,0:T(8,128)(2,1)S(1)}, u32[]{:S(2)}, u32[]{:S(2)}) %collective-permute-start.21) | collective-permute-done | bytes 1048608 | tf_op jit(solution)/shard_map/ppermute | solution.py:742
  176.6 20.7 %feed_forward.1 = (f32[1024,1024]{1,0:T(8,128)}, bf16[1024,1024]{1,0:T(8,128)(2,1)S(1)}, bf16[1024,1024]{1,0:T(8,128)(2,1)S(1)}, bf16[1024,1024]{1,0:T(8,128)(2,...) custom-call(bf16[1024,1024]{1,0:T(8,128)(2,1)} %copy-done.21, ...), custom_call_target="tpu_custom_call" | custom-call | bytes 19926000 | tf_op jit(solution)/shard_map/feed_forward/pallas_call | solution.py:602
  209.0 9.8 %grads.5 = (bf16[2,512,1024]{2,1,0:T(8,128)(2,1)}, bf16[512,1024]{1,0:T(8,128)(2,1)S(1)}, bf16[512,1024]{1,0:T(8,128)(2,1)S(1)}) custom-call(s32[6]{0:T(128)S(1)} %stack.116.place, bf16[1024,1024]{1,0:T(8,128)(2,1)S(1)} %copy-done.35, bf16[1024,1024]{1,0:T(8,128)(2,1)S(1)} %get-tuple-element.325.refs_1_.refs_3_, bf16[1024,1024]{1,0:T(8,128)(2,1)S(1)} %copy-done.18, ...), custom_call_target="tpu_custom_call" | custom-call | bytes 6642000 | tf_op jit(solution)/shard_map/grads/pallas_call | solution.py:888
  227.7 9.8 %middle.1 = (bf16[1024,1024]{1,0:T(8,128)(2,1)S(1)}, bf16[1024,768]{1,0:T(8,128)(2,1)S(1)}, bf16[1024,768]{1,0:T(8,128)(2,1)S(1)}, bf16[1024,256]{1,0:T(8,128)(2...) custom-call(f32[1024,1024]{1,0:T(8,128)} %get-tuple-element.316.state_ref, ...), custom_call_target="tpu_custom_call" | custom-call | bytes 12177000 | tf_op jit(solution)/shard_map/middle/pallas_call | solution.py:659
  238.6 9.1 %attention_backward.1 = bf16[1024,512]{1,0:T(8,128)(2,1)S(1)} custom-call(bf16[1024,512]{1,0:T(8,128)(2,1)S(1)} %pad_maximum_fusion.5.qkv_ref, bf16[1024,384]{1,0:T(8,128)(2,1)S(1)} %copy-done.54, bf16[1024,256]{1,0:T(8,128)(2,1)S(1)} %get-tuple-element.337.datt_ref, f32[8,1024]{1,0:T(8,128)S(1)} %get-tuple-element.338.lse_ref, ...), custom_call_target="tpu_custom_call" | custom-call | bytes 9963000 | tf_op jit(solution)/shard_map/attention_backward/pallas_call | solution.py:560
  253.7 9.8 %grads.6 = (bf16[2,512,1024]{2,1,0:T(8,128)(2,1)}, bf16[512,1024]{1,0:T(8,128)(2,1)S(1)}, bf16[512,1024]{1,0:T(8,128)(2,1)S(1)}) custom-call(s32[6]{0:T(128)S(1)} %stack.116.place, bf16[1024,1024]{1,0:T(8,128)(2,1)S(1)} %get-tuple-element.334.refs_0_, bf16[1024,1024]{1,0:T(8,128)(2,1)S(1)} %copy-done.11, ...), custom_call_target="tpu_custom_call" | custom-call | bytes 6642000 | tf_op jit(solution)/shard_map/grads/pallas_call | solution.py:888
  277.3 25.7 %ssd_backward.1 = (bf16[1024,1024]{1,0:T(8,128)(2,1)S(1)}, bf16[1024,256]{1,0:T(8,128)(2,1)S(1)}, f32[8,1152]{1,0:T(8,128)S(1)}) custom-call(f32[1024,1024]{1,0:T(8,128)S(1)} %copy-done.1, f32[1024,1024]{1,0:T(8,128)S(1)} %copy-done.1, f32[1024,256]{1,0:T(8,128)S(1)} %copy-done.7, f32[1024,256]{1,0:T(8,128)S(1)} %copy-done.7, ...), custom_call_target="tpu_custom_call" | custom-call | bytes 30996000 | tf_op jit(solution)/shard_map/ssd_backward/pallas_call | solution.py:375
  316.2 6.2 %products.3 = bf16[1024,1024]{1,0:T(8,128)(2,1)S(1)} custom-call(bf16[1024,1024]{1,0:T(8,128)(2,1)S(1)} %get-tuple-element.371.refs_0_.refs_1_.refs_3_, bf16[1024,256]{1,0:T(8,128)(2,1)S(1)} %get-tuple-element.372.refs_1_, bf16[1024,768]{1,0:T(8,128)(2,1)S(1)} %get-tuple-element.346.refs_4_.refs_8_.refs_2_, bf16[1024,256]{1,0:T(8,128)(2,1)S(1)} %copy-done.9, ...), custom_call_target="tpu_custom_call" | custom-call | bytes 6642000 | tf_op jit(solution)/shard_map/products/pallas_call | solution.py:1151
  337.8 5.7 %grads.7 = (bf16[2,512,640]{2,1,0:T(8,128)(2,1)}, bf16[512,640]{1,0:T(8,128)(2,1)S(1)}, bf16[512,640]{1,0:T(8,128)(2,1)S(1)}) custom-call(s32[6]{0:T(128)S(1)} %stack.116.place, bf16[1024,1024]{1,0:T(8,128)(2,1)S(1)} %copy-done.12, bf16[1024,1024]{1,0:T(8,128)(2,1)S(1)} %get-tuple-element.371.refs_0_.refs_1_.refs_3_, ...), custom_call_target="tpu_custom_call" | custom-call | bytes 6642000 | tf_op jit(solution)/shard_map/grads/pallas_call | solution.py:888
  356.2 16.5 %collective-permute-done.42 = bf16[256,1024]{1,0:T(8,128)(2,1)S(1)} collective-permute-done((bf16[256,1024]{1,0:T(8,128)(2,1)S(1)}, bf16[256,1024]{1,0:T(8,128)(2,1)S(1)}, u32[]{:S(2)}, u32[]{:S(2)}) %collective-permute-start.42) | collective-permute-done | bytes 524320 | tf_op jit(solution)/shard_map/ppermute | solution.py:738
  378.7 7.2 %store.2 = bf16[2048,1024]{1,0:T(8,128)(2,1)} custom-call(s32[6]{0:T(128)S(1)} %stack.138.place, bf16[1024,1024]{1,0:T(8,128)(2,1)S(1)} %copy-done.2, bf16[512,1024]{1,0:T(8,128)(2,1)} %collective-permute-done.36.refs_1_, bf16[512,1024]{1,0:T(8,128)(2,1)} %collective-permute-done.38.refs_2_), custom_call_target="tpu_custom_call" | custom-call | bytes 5535000 | tf_op jit(solution)/shard_map/store/pallas_call | solution.py:1037
  398.9 7.1 %collective-permute-done.45 = bf16[512,640]{1,0:T(8,128)(2,1)} collective-permute-done((bf16[512,640]{1,0:T(8,128)(2,1)}, bf16[512,640]{1,0:T(8,128)(2,1)}, u32[]{:S(2)}, u32[]{:S(2)}) %collective-permute-start.45) | collective-permute-done | bytes 655392 | tf_op jit(solution)/shard_map/ppermute | solution.py:742
  411.3 7.2 %collective-permute-done.50.refs_2_ = bf16[512,1024]{1,0:T(8,128)(2,1)S(1)} collective-permute-done((bf16[512,1024]{1,0:T(8,128)(2,1)S(1)}, bf16[512,1024]{1,0:T(8,128)(2,1)S(1)}, u32[]{:S(2)}, u32[]{:S(2)}) %collective-permute-start.50) | collective-permute-done | bytes 1048608 | tf_op jit(solution)/shard_map/ppermute | solution.py:709
  437.3 6.2 %store.3 = bf16[2048,1024]{1,0:T(8,128)(2,1)} custom-call(s32[8]{0:T(128)S(1)} %stack.143.place, bf16[512,1024]{1,0:T(8,128)(2,1)S(1)} %get-tuple-element.399.refs_0_, bf16[512,1024]{1,0:T(8,128)(2,1)S(1)} %collective-permute-done.44.refs_1_, bf16[512,1024]{1,0:T(8,128)(2,1)S(1)} %collective-permute-done.50.refs_2_, ...), custom_call_target="tpu_custom_call" | custom-call | bytes 5535000 | tf_op jit(solution)/shard_map/store/pallas_call | solution.py:1037
  (488 shorter events, 208.5 us)
Async XLA Ops:
  13.2 17.3 %collective-permute-start.3 = (f32[8,512]{1,0:T(8,128)S(1)}, f32[8,512]{1,0:T(8,128)S(1)}, u32[]{:S(2)}, u32[]{:S(2)}) collective-permute-start(f32[8,512]{1,0:T(8,128)S(1)} %pad_maximum_fusion.25), channel_id=1, source_target_pairs={{0,2},{2,0},{1,3},{3,1},{4,6},{6,4},{5,7},{7,5},{8,10},{10,8},{9,1... | collective-permute-start | bytes 49160 | tf_op jit(solution)/shard_map/ppermute | solution.py:709
  16.6 16.5 %collective-permute-start.1 = (bf16[256,640]{1,0:T(8,128)(2,1)S(1)}, bf16[256,640]{1,0:T(8,128)(2,1)S(1)}, u32[]{:S(2)}, u32[]{:S(2)}) collective-permute-start(bf16[256,640]{1,0:T(8,128)(2,1)S(1)} %pad_maximum_fusion.19), channel_id=1, source_target_pairs={{0,16},{4,20},{8,24},{12,28},{16,0},{20,4},{24,8},{28,12},{1,17},{... | collective-permute-start | bytes 983048 | tf_op jit(solution)/shard_map/ppermute | solution.py:738
  50.2 21.7 %collective-permute-start.7 = (bf16[1024,640]{1,0:T(8,128)(2,1)S(1)}, bf16[1024,640]{1,0:T(8,128)(2,1)S(1)}, u32[]{:S(2)}, u32[]{:S(2)}) collective-permute-start(bf16[1024,640]{1,0:T(8,128)(2,1)S(1)} %pad_maximum_fusion.1.near_a.near_b), channel_id=1, source_target_pairs={{0,4},{1,3},{2,6},{3,1},{4,0},{5,7},{6,2},{7,5},{8,12},{9,11},{10,... | collective-permute-start | bytes 3932168 | tf_op jit(solution)/shard_map/ppermute | solution.py:742
  77.1 26.5 %collective-permute-start.11 = (bf16[1024,512]{1,0:T(8,128)(2,1)S(1)}, bf16[1024,512]{1,0:T(8,128)(2,1)S(1)}, u32[]{:S(2)}, u32[]{:S(2)}) collective-permute-start(bf16[1024,512]{1,0:T(8,128)(2,1)S(1)} %pad_maximum_fusion.2.near_a.near_b), channel_id=1, source_target_pairs={{0,4},{1,3},{2,6},{3,1},{4,0},{5,7},{6,2},{7,5},{8,12},{9,11},{10,... | collective-permute-start | bytes 3145736 | tf_op jit(solution)/shard_map/ppermute | solution.py:742
  77.5 15.4 %collective-permute-start.12 = (bf16[512,512]{1,0:T(8,128)(2,1)S(1)}, bf16[512,512]{1,0:T(8,128)(2,1)S(1)}, u32[]{:S(2)}, u32[]{:S(2)}) collective-permute-start(bf16[512,512]{1,0:T(8,128)(2,1)S(1)} %pad_maximum_fusion.12), channel_id=1, source_target_pairs={{0,2},{1,5},{2,0},{3,7},{4,6},{5,1},{6,4},{7,3},{8,10},{9,13},{10,... | collective-permute-start | bytes 1572872 | tf_op jit(solution)/shard_map/ppermute | solution.py:742
  79.1 24.5 %collective-permute-start.13 = (bf16[256,1024]{1,0:T(8,128)(2,1)S(1)}, bf16[256,1024]{1,0:T(8,128)(2,1)S(1)}, u32[]{:S(2)}, u32[]{:S(2)}) collective-permute-start(bf16[256,1024]{1,0:T(8,128)(2,1)S(1)} %pad_maximum_fusion.13), channel_id=1, source_target_pairs={{0,16},{4,20},{8,24},{12,28},{16,0},{20,4},{24,8},{28,12},{1,17},{... | collective-permute-start | bytes 1572872 | tf_op jit(solution)/shard_map/ppermute | solution.py:738
  103.8 26.1 %collective-permute-start.16 = (bf16[1024,512]{1,0:T(8,128)(2,1)S(1)}, bf16[1024,512]{1,0:T(8,128)(2,1)S(1)}, u32[]{:S(2)}, u32[]{:S(2)}) collective-permute-start(bf16[1024,512]{1,0:T(8,128)(2,1)S(1)} %pad_maximum_fusion.3.near_a.near_b), channel_id=1, source_target_pairs={{0,4},{1,3},{2,6},{3,1},{4,0},{5,7},{6,2},{7,5},{8,12},{9,11},{10,... | collective-permute-start | bytes 3145736 | tf_op jit(solution)/shard_map/ppermute | solution.py:742
  105.4 24.5 %collective-permute-start.17 = (bf16[512,1024]{1,0:T(8,128)(2,1)S(1)}, bf16[512,1024]{1,0:T(8,128)(2,1)S(1)}, u32[]{:S(2)}, u32[]{:S(2)}) collective-permute-start(bf16[512,1024]{1,0:T(8,128)(2,1)S(1)} %pad_maximum_fusion.4), channel_id=1, source_target_pairs={{0,2},{1,5},{2,0},{3,7},{4,6},{5,1},{6,4},{7,3},{8,10},{9,13},{10,... | collective-permute-start | bytes 3145736 | tf_op jit(solution)/shard_map/ppermute | solution.py:742
  130.9 31.7 %collective-permute-start.20 = (bf16[1024,1024]{1,0:T(8,128)(2,1)S(1)}, bf16[1024,1024]{1,0:T(8,128)(2,1)S(1)}, u32[]{:S(2)}, u32[]{:S(2)}) collective-permute-start(bf16[1024,1024]{1,0:T(8,128)(2,1)S(1)} %pad_maximum_fusion.near_a.near_b), channel_id=1, source_target_pairs={{0,4},{1,3},{2,6},{3,1},{4,0},{5,7},{6,2},{7,5},{8,12},{9,11},{10,... | collective-permute-start | bytes 6291464 | tf_op jit(solution)/shard_map/ppermute | solution.py:742
  144.0 29.9 %collective-permute-start.22 = (bf16[1024,1024]{1,0:T(8,128)(2,1)S(1)}, bf16[1024,1024]{1,0:T(8,128)(2,1)S(1)}, u32[]{:S(2)}, u32[]{:S(2)}) collective-permute-start(bf16[1024,1024]{1,0:T(8,128)(2,1)S(1)} %products.2.part_ref), channel_id=1, source_target_pairs={{0,1},{1,0},{2,3},{3,2},{4,5},{5,4},{6,7},{7,6},{8,9},{9,8},{10,11... | collective-permute-start | bytes 6291464 | tf_op jit(solution)/shard_map/ppermute | solution.py:705
  198.7 20.1 %collective-permute-start.25 = (bf16[1024,1024]{1,0:T(8,128)(2,1)}, bf16[1024,1024]{1,0:T(8,128)(2,1)S(1)}, u32[]{:S(2)}, u32[]{:S(2)}) collective-permute-start(bf16[1024,1024]{1,0:T(8,128)(2,1)} %get-tuple-element.317.dpart_ref), channel_id=1, source_target_pairs={{0,1},{1,0},{2,3},{3,2},{4,5},{5,4},{6,7},{7,6},{8,9},{9,8},{10,11... | collective-permute-start | bytes 6291464 | tf_op jit(solution)/shard_map/ppermute | solution.py:705
  220.9 30.3 %collective-permute-start.26 = (bf16[2,512,1024]{2,1,0:T(8,128)(2,1)}, bf16[2,512,1024]{2,1,0:T(8,128)(2,1)S(1)}, u32[]{:S(2)}, u32[]{:S(2)}) collective-permute-start(bf16[2,512,1024]{2,1,0:T(8,128)(2,1)} %get-tuple-element.340), channel_id=1, source_target_pairs={{0,4},{1,3},{2,6},{3,1},{4,0},{5,7},{6,2},{7,5},{8,12},{9,11},{10,... | collective-permute-start | bytes 6291464 | tf_op jit(solution)/shard_map/ppermute | solution.py:742
  222.4 25.3 %collective-permute-start.27 = (bf16[512,512]{1,0:T(8,128)(2,1)S(1)}, bf16[512,512]{1,0:T(8,128)(2,1)S(1)}, u32[]{:S(2)}, u32[]{:S(2)}) collective-permute-start(bf16[512,512]{1,0:T(8,128)(2,1)S(1)} %fusion.7), channel_id=1, source_target_pairs={{0,2},{1,5},{2,0},{3,7},{4,6},{5,1},{6,4},{7,3},{8,10},{9,13},{10,... | collective-permute-start | bytes 1572872 | tf_op jit(solution)/shard_map/ppermute | solution.py:742
  267.7 37.3 %collective-permute-start.29 = (bf16[2,512,1024]{2,1,0:T(8,128)(2,1)}, bf16[2,512,1024]{2,1,0:T(8,128)(2,1)}, u32[]{:S(2)}, u32[]{:S(2)}) collective-permute-start(bf16[2,512,1024]{2,1,0:T(8,128)(2,1)} %get-tuple-element.362), channel_id=1, source_target_pairs={{0,4},{1,3},{2,6},{3,1},{4,0},{5,7},{6,2},{7,5},{8,12},{9,11},{10,... | collective-permute-start | bytes 6291464 | tf_op jit(solution)/shard_map/ppermute | solution.py:742
  269.2 35.9 %collective-permute-start.30 = (bf16[256,1536]{1,0:T(8,128)(2,1)}, bf16[256,1536]{1,0:T(8,128)(2,1)}, u32[]{:S(2)}, u32[]{:S(2)}) collective-permute-start(bf16[256,1536]{1,0:T(8,128)(2,1)} %pad_maximum_fusion.7), channel_id=1, source_target_pairs={{0,16},{4,20},{8,24},{12,28},{16,0},{20,4},{24,8},{28,12},{1,17},{... | collective-permute-start | bytes 2359304 | tf_op jit(solution)/shard_map/ppermute | solution.py:738
  309.0 21.4 %collective-permute-start.31 = (bf16[512,1024]{1,0:T(8,128)(2,1)S(1)}, bf16[512,1024]{1,0:T(8,128)(2,1)S(1)}, u32[]{:S(2)}, u32[]{:S(2)}) collective-permute-start(bf16[512,1024]{1,0:T(8,128)(2,1)S(1)} %fusion), channel_id=1, source_target_pairs={{0,2},{1,5},{2,0},{3,7},{4,6},{5,1},{6,4},{7,3},{8,10},{9,13},{10,... | collective-permute-start | bytes 3145736 | tf_op jit(solution)/shard_map/ppermute | solution.py:742
  314.4 32.0 %collective-permute-start.36 = (bf16[512,1024]{1,0:T(8,128)(2,1)S(1)}, bf16[512,1024]{1,0:T(8,128)(2,1)}, u32[]{:S(2)}, u32[]{:S(2)}) collective-permute-start(bf16[512,1024]{1,0:T(8,128)(2,1)S(1)} %constant_dynamic-slice_fusion.6), channel_id=1, source_target_pairs={{0,2},{2,0},{1,3},{3,1},{4,6},{6,4},{5,7},{7,5},{8,10},{10,8},{9,1... | collective-permute-start | bytes 3145736 | tf_op jit(solution)/shard_map/ppermute | solution.py:709
  332.1 21.4 %collective-permute-start.40 = (bf16[512,1024]{1,0:T(8,128)(2,1)S(1)}, bf16[512,1024]{1,0:T(8,128)(2,1)S(1)}, u32[]{:S(2)}, u32[]{:S(2)}) collective-permute-start(bf16[512,1024]{1,0:T(8,128)(2,1)S(1)} %get-tuple-element.392), channel_id=1, source_target_pairs={{0,1},{1,0},{2,3},{3,2},{4,5},{5,4},{6,7},{7,6},{8,9},{9,8},{10,11... | collective-permute-start | bytes 3145736 | tf_op jit(solution)/shard_map/ppermute | solution.py:705
  347.3 38.6 %collective-permute-start.37 = (bf16[2,512,640]{2,1,0:T(8,128)(2,1)}, bf16[2,512,640]{2,1,0:T(8,128)(2,1)}, u32[]{:S(2)}, u32[]{:S(2)}) collective-permute-start(bf16[2,512,640]{2,1,0:T(8,128)(2,1)} %get-tuple-element.388), channel_id=1, source_target_pairs={{0,4},{1,3},{2,6},{3,1},{4,0},{5,7},{6,2},{7,5},{8,12},{9,11},{10,... | collective-permute-start | bytes 3932168 | tf_op jit(solution)/shard_map/ppermute | solution.py:742
  352.0 20.7 %collective-permute-start.42 = (bf16[256,1024]{1,0:T(8,128)(2,1)S(1)}, bf16[256,1024]{1,0:T(8,128)(2,1)S(1)}, u32[]{:S(2)}, u32[]{:S(2)}) collective-permute-start(bf16[256,1024]{1,0:T(8,128)(2,1)S(1)} %fusion.4), channel_id=1, source_target_pairs={{0,16},{4,20},{8,24},{12,28},{16,0},{20,4},{24,8},{28,12},{1,17},{... | collective-permute-start | bytes 1572872 | tf_op jit(solution)/shard_map/ppermute | solution.py:738
  353.4 25.2 %collective-permute-start.38 = (bf16[512,1024]{1,0:T(8,128)(2,1)}, bf16[512,1024]{1,0:T(8,128)(2,1)}, u32[]{:S(2)}, u32[]{:S(2)}) collective-permute-start(bf16[512,1024]{1,0:T(8,128)(2,1)} %collective-permute-done.36.refs_1_), channel_id=1, source_target_pairs={{0,1},{1,0},{2,3},{3,2},{4,5},{5,4},{6,7},{7,6},{8,9},{9,8},{10,11... | collective-permute-start | bytes 3145736 | tf_op jit(solution)/shard_map/ppermute | solution.py:705
  388.0 18.0 %collective-permute-start.45 = (bf16[512,640]{1,0:T(8,128)(2,1)}, bf16[512,640]{1,0:T(8,128)(2,1)}, u32[]{:S(2)}, u32[]{:S(2)}) collective-permute-start(bf16[512,640]{1,0:T(8,128)(2,1)} %fusion.2), channel_id=1, source_target_pairs={{0,2},{1,5},{2,0},{3,7},{4,6},{5,1},{6,4},{7,3},{8,10},{9,13},{10,... | collective-permute-start | bytes 1966088 | tf_op jit(solution)/shard_map/ppermute | solution.py:742
  388.1 30.3 %collective-permute-start.50 = (bf16[512,1024]{1,0:T(8,128)(2,1)S(1)}, bf16[512,1024]{1,0:T(8,128)(2,1)S(1)}, u32[]{:S(2)}, u32[]{:S(2)}) collective-permute-start(bf16[512,1024]{1,0:T(8,128)(2,1)S(1)} %get-tuple-element.399.refs_0_), channel_id=1, source_target_pairs={{0,2},{2,0},{1,3},{3,1},{4,6},{6,4},{5,7},{7,5},{8,10},{10,8},{9,1... | collective-permute-start | bytes 3145736 | tf_op jit(solution)/shard_map/ppermute | solution.py:709
  390.1 47.1 %collective-permute-start.44 = (bf16[512,1024]{1,0:T(8,128)(2,1)S(1)}, bf16[512,1024]{1,0:T(8,128)(2,1)S(1)}, u32[]{:S(2)}, u32[]{:S(2)}) collective-permute-start(bf16[512,1024]{1,0:T(8,128)(2,1)S(1)} %get-tuple-element.399.refs_0_), channel_id=1, source_target_pairs={{0,1},{1,0},{2,3},{3,2},{4,5},{5,4},{6,7},{7,6},{8,9},{9,8},{10,11... | collective-permute-start | bytes 3145736 | tf_op jit(solution)/shard_map/ppermute | solution.py:705
  (145 other events, 1267.4 us)

commit v4 on v3

--- a/solution.py
+++ b/solution.py
@@ -1117,8 +1117,14 @@
                     rows, 128 * (col % 2) : 128 * (col % 2) + 128]
 
 
-def shared_rows(grad_bc, grad_kv, half, core):
+def shared_rows(grad_bc, grad_kv, half, core, dp):
     total = grad_bc.shape[0]
+    if total // dp != 128:
+        tiles = jnp.concatenate([grad_bc, grad_kv], axis=1).reshape(dp, 4, -1, 4, 128).swapaxes(2, 3)
+        tile = lambda slot: lax.dynamic_index_in_dim(tiles, slot, 1, keepdims=False).reshape(total, 128)
+        both = lambda which: jnp.concatenate(
+            [tile(2 * half + which), tile(2 * (1 - half) + which)], axis=1)
+        return both(core), both(1 - core)
     step = 128
     spec = pl.BlockSpec((step, 256), lambda i, _: (i, 0))
     return pl.pallas_call(
@@ -1379,7 +1385,7 @@
     out_got = half_swap(out_part)
 
     grad_bc = short(dot(normed_t, dpair))
-    keep_shared, send_shared = shared_rows(grad_bc, flips(grad_kv), half, core)
+    keep_shared, send_shared = shared_rows(grad_bc, flips(grad_kv), half, core, dp)
     shared_got = core_swap(send_shared)
     dnormed_part = products(
         [dh1, dpair, dz, dqry, dkv], [weight1, weight_bc, weight_z, weight_q, weight_kv], BF)

time: 453 us -> 453 us (level)
  no operation moved by 1% of the time
where the time goes in v4:
time: 453 us; the launch traced here: 444 us
  Pallas kernels  144 us (32%)
  waiting for transfers between devices  141 us (31%)
  starting transfers between devices  53.8 us (12%)
  local copies, waits for them, and re-layouts  51.9 us (11%)
  other arithmetic  41.2 us (9%)
  matrix products  8.51 us (2%)
    ppermute x20, waiting for transfers between devices, dp_swap(): return lax.ppermute(value, 'dp', [(d, d ^ bit) for d in range(8)])  68.1 us
    ppermute x18, waiting for transfers between devices, near_swap(): lax.ppermute(value, ('dp', 'head'), pair_list(8, (step == 1, step == 0), 1))  59.2 us
    unnamed x237, local copies, waits for them, and re-layouts  32.4 us
    pallas_call x4, Pallas kernels, grads(): pl.pallas_call(kernel, grid_spec=pltpu.PrefetchScalarGridSpec(num_scalar_...  30.2 us
    ppermute x20, starting transfers between devices, dp_swap(): return lax.ppermute(value, 'dp', [(d, d ^ bit) for d in range(8)])  25.8 us
    pallas_call x1, Pallas kernels, ssd_backward(): pl.pallas_call(ssd_backward_kernel, grid=(chunks,), in_specs=[rows(width)...  25.7 us
    pallas_call x1, Pallas kernels, feed_forward(): pl.pallas_call(feed_forward_kernel, grid=(length // step,), in_specs=[blo...  20.7 us
    ppermute x18, starting transfers between devices, near_swap(): lax.ppermute(value, ('dp', 'head'), pair_list(8, (step == 1, step == 0), 1))  20.2 us
  transfers between devices with their start and end apart: 54, of which 31 were waited for; matrix products, arithmetic and copies ran while one was open for 14% of the time, Pallas kernels for 26%

profile of v4, /device:TPU:0, one launch (start us, length us, event | category | flops | bytes accessed | tf_op | source)
XLA Modules:
  0.0 443.9 jit_solution(13705835997935683130)
XLA Ops:
  37.7 5.0 %collective-permute-done.6 = bf16[128,512]{1,0:T(8,128)(2,1)S(1)} collective-permute-done((bf16[128,512]{1,0:T(8,128)(2,1)S(1)}, bf16[128,512]{1,0:T(8,128)(2,1)S(1)}, u32[]{:S(2)}, u32[]{:S(2)}) %collective-permute-start.6) | collective-permute-done | bytes 131104 | tf_op jit(solution)/shard_map/ppermute | solution.py:738
  42.7 5.9 %collective-permute-done.5 = bf16[256,512]{1,0:T(8,128)(2,1)S(1)} collective-permute-done((bf16[256,512]{1,0:T(8,128)(2,1)S(1)}, bf16[256,512]{1,0:T(8,128)(2,1)S(1)}, u32[]{:S(2)}, u32[]{:S(2)}) %collective-permute-start.5) | collective-permute-done | bytes 262176 | tf_op jit(solution)/shard_map/ppermute | solution.py:738
  53.2 9.6 %collective-permute-done.10 = bf16[128,1024]{1,0:T(8,128)(2,1)} collective-permute-done((bf16[128,1024]{1,0:T(8,128)(2,1)S(1)}, bf16[128,1024]{1,0:T(8,128)(2,1)}, u32[]{:S(2)}, u32[]{:S(2)}) %collective-permute-start.10) | collective-permute-done | bytes 262176 | tf_op jit(solution)/shard_map/ppermute | solution.py:738
  66.0 6.0 %collective-permute-done.7.far_a.far_b = bf16[1024,640]{1,0:T(8,128)(2,1)S(1)} collective-permute-done((bf16[1024,640]{1,0:T(8,128)(2,1)S(1)}, bf16[1024,640]{1,0:T(8,128)(2,1)S(1)}, u32[]{:S(2)}, u32[]{:S(2)}) %collective-permute-start.7) | collective-permute-done | bytes 1310752 | tf_op jit(solution)/shard_map/ppermute | solution.py:742
  86.7 6.2 %collective-permute-done.14 = bf16[128,512]{1,0:T(8,128)(2,1)S(1)} collective-permute-done((bf16[128,512]{1,0:T(8,128)(2,1)S(1)}, bf16[128,512]{1,0:T(8,128)(2,1)S(1)}, u32[]{:S(2)}, u32[]{:S(2)}) %collective-permute-start.14) | collective-permute-done | bytes 131104 | tf_op jit(solution)/shard_map/ppermute | solution.py:738
  92.9 10.7 %collective-permute-done.13 = bf16[256,1024]{1,0:T(8,128)(2,1)S(1)} collective-permute-done((bf16[256,1024]{1,0:T(8,128)(2,1)S(1)}, bf16[256,1024]{1,0:T(8,128)(2,1)S(1)}, u32[]{:S(2)}, u32[]{:S(2)}) %collective-permute-start.13) | collective-permute-done | bytes 524320 | tf_op jit(solution)/shard_map/ppermute | solution.py:738
  109.9 8.3 %attention_forward.1 = (bf16[1024,256]{1,0:T(8,128)(2,1)S(1)}, bf16[1024,384]{1,0:T(8,128)(2,1)S(1)}, f32[8,1024]{1,0:T(8,128)S(1)}) custom-call(bf16[1024,512]{1,0:T(8,128)(2,1)S(1)} %pad_maximum_fusion.5.qkv_ref, f32[1024,128]{1,0:T(8,128)S(1)} %copy-done.22, f32[1024,128]{1,0:T(8,128)S(1)} %copy-done.23, f32[1024,128]{1,0:T(8,128)S(1)} %pad.16.segcol_ref.aux_ref, ...), custom_call_target="tpu_custom_call" | custom-call | bytes 8856000 | tf_op jit(solution)/shard_map/attention_forward/pallas_call | solution.py:499
  121.2 8.6 %collective-permute-done.16.far_a.far_b = bf16[1024,512]{1,0:T(8,128)(2,1)S(1)} collective-permute-done((bf16[1024,512]{1,0:T(8,128)(2,1)S(1)}, bf16[1024,512]{1,0:T(8,128)(2,1)S(1)}, u32[]{:S(2)}, u32[]{:S(2)}) %collective-permute-start.16) | collective-permute-done | bytes 1048608 | tf_op jit(solution)/shard_map/ppermute | solution.py:742
  132.5 8.4 %ssd_forward.1 = (bf16[1024,768]{1,0:T(8,128)(2,1)S(1)}, bf16[1024,768]{1,0:T(8,128)(2,1)S(1)}, bf16[1024,768]{1,0:T(8,128)(2,1)S(1)}) custom-call(f32[1024,1024]{1,0:T(8,128)S(1)} %fusion.59.h_ref.prev_ref, f32[1024,256]{1,0:T(8,128)S(1)} %fusion.47.pair_ref.pair_prev_ref, bf16[1024,768]{1,0:T(8,128)(2,1)S(1)} %convolution_convert_fusion.z_ref, ...), custom_call_target="tpu_custom_call" | custom-call | bytes 11070000 | tf_op jit(solution)/shard_map/ssd_forward/pallas_call | solution.py:182
  145.0 14.0 %collective-permute-done.19 = bf16[512,512]{1,0:T(8,128)(2,1)S(1)} collective-permute-done((bf16[512,512]{1,0:T(8,128)(2,1)S(1)}, bf16[512,512]{1,0:T(8,128)(2,1)S(1)}, u32[]{:S(2)}, u32[]{:S(2)}) %collective-permute-start.19) | collective-permute-done | bytes 524320 | tf_op jit(solution)/shard_map/ppermute | solution.py:742
  165.0 9.0 %collective-permute-done.21.far_a.far_b = bf16[1024,512]{1,0:T(8,128)(2,1)S(1)} collective-permute-done((bf16[1024,512]{1,0:T(8,128)(2,1)S(1)}, bf16[1024,512]{1,0:T(8,128)(2,1)S(1)}, u32[]{:S(2)}, u32[]{:S(2)}) %collective-permute-start.21) | collective-permute-done | bytes 1048608 | tf_op jit(solution)/shard_map/ppermute | solution.py:742
  176.6 20.7 %feed_forward.1 = (f32[1024,1024]{1,0:T(8,128)}, bf16[1024,1024]{1,0:T(8,128)(2,1)S(1)}, bf16[1024,1024]{1,0:T(8,128)(2,1)S(1)}, bf16[1024,1024]{1,0:T(8,128)(2,...) custom-call(bf16[1024,1024]{1,0:T(8,128)(2,1)} %copy-done.21, ...), custom_call_target="tpu_custom_call" | custom-call | bytes 19926000 | tf_op jit(solution)/shard_map/feed_forward/pallas_call | solution.py:602
  209.0 9.8 %grads.5 = (bf16[2,512,1024]{2,1,0:T(8,128)(2,1)}, bf16[512,1024]{1,0:T(8,128)(2,1)S(1)}, bf16[512,1024]{1,0:T(8,128)(2,1)S(1)}) custom-call(s32[6]{0:T(128)S(1)} %stack.116.place, bf16[1024,1024]{1,0:T(8,128)(2,1)S(1)} %copy-done.35, bf16[1024,1024]{1,0:T(8,128)(2,1)S(1)} %get-tuple-element.325.refs_1_.refs_3_, bf16[1024,1024]{1,0:T(8,128)(2,1)S(1)} %copy-done.18, ...), custom_call_target="tpu_custom_call" | custom-call | bytes 6642000 | tf_op jit(solution)/shard_map/grads/pallas_call | solution.py:888
  227.7 9.8 %middle.1 = (bf16[1024,1024]{1,0:T(8,128)(2,1)S(1)}, bf16[1024,768]{1,0:T(8,128)(2,1)S(1)}, bf16[1024,768]{1,0:T(8,128)(2,1)S(1)}, bf16[1024,256]{1,0:T(8,128)(2...) custom-call(f32[1024,1024]{1,0:T(8,128)} %get-tuple-element.316.state_ref, ...), custom_call_target="tpu_custom_call" | custom-call | bytes 12177000 | tf_op jit(solution)/shard_map/middle/pallas_call | solution.py:659
  238.6 9.1 %attention_backward.1 = bf16[1024,512]{1,0:T(8,128)(2,1)S(1)} custom-call(bf16[1024,512]{1,0:T(8,128)(2,1)S(1)} %pad_maximum_fusion.5.qkv_ref, bf16[1024,384]{1,0:T(8,128)(2,1)S(1)} %copy-done.54, bf16[1024,256]{1,0:T(8,128)(2,1)S(1)} %get-tuple-element.337.datt_ref, f32[8,1024]{1,0:T(8,128)S(1)} %get-tuple-element.338.lse_ref, ...), custom_call_target="tpu_custom_call" | custom-call | bytes 9963000 | tf_op jit(solution)/shard_map/attention_backward/pallas_call | solution.py:560
  253.7 9.8 %grads.6 = (bf16[2,512,1024]{2,1,0:T(8,128)(2,1)}, bf16[512,1024]{1,0:T(8,128)(2,1)S(1)}, bf16[512,1024]{1,0:T(8,128)(2,1)S(1)}) custom-call(s32[6]{0:T(128)S(1)} %stack.116.place, bf16[1024,1024]{1,0:T(8,128)(2,1)S(1)} %get-tuple-element.334.refs_0_, bf16[1024,1024]{1,0:T(8,128)(2,1)S(1)} %copy-done.11, ...), custom_call_target="tpu_custom_call" | custom-call | bytes 6642000 | tf_op jit(solution)/shard_map/grads/pallas_call | solution.py:888
  277.3 25.7 %ssd_backward.1 = (bf16[1024,1024]{1,0:T(8,128)(2,1)S(1)}, bf16[1024,256]{1,0:T(8,128)(2,1)S(1)}, f32[8,1152]{1,0:T(8,128)S(1)}) custom-call(f32[1024,1024]{1,0:T(8,128)S(1)} %copy-done.1, f32[1024,1024]{1,0:T(8,128)S(1)} %copy-done.1, f32[1024,256]{1,0:T(8,128)S(1)} %copy-done.7, f32[1024,256]{1,0:T(8,128)S(1)} %copy-done.7, ...), custom_call_target="tpu_custom_call" | custom-call | bytes 30996000 | tf_op jit(solution)/shard_map/ssd_backward/pallas_call | solution.py:375
  316.2 6.2 %products.3 = bf16[1024,1024]{1,0:T(8,128)(2,1)S(1)} custom-call(bf16[1024,1024]{1,0:T(8,128)(2,1)S(1)} %get-tuple-element.371.refs_0_.refs_1_.refs_3_, bf16[1024,256]{1,0:T(8,128)(2,1)S(1)} %get-tuple-element.372.refs_1_, bf16[1024,768]{1,0:T(8,128)(2,1)S(1)} %get-tuple-element.346.refs_4_.refs_8_.refs_2_, bf16[1024,256]{1,0:T(8,128)(2,1)S(1)} %copy-done.9, ...), custom_call_target="tpu_custom_call" | custom-call | bytes 6642000 | tf_op jit(solution)/shard_map/products/pallas_call | solution.py:1157
  337.8 5.7 %grads.7 = (bf16[2,512,640]{2,1,0:T(8,128)(2,1)}, bf16[512,640]{1,0:T(8,128)(2,1)S(1)}, bf16[512,640]{1,0:T(8,128)(2,1)S(1)}) custom-call(s32[6]{0:T(128)S(1)} %stack.116.place, bf16[1024,1024]{1,0:T(8,128)(2,1)S(1)} %copy-done.12, bf16[1024,1024]{1,0:T(8,128)(2,1)S(1)} %get-tuple-element.371.refs_0_.refs_1_.refs_3_, ...), custom_call_target="tpu_custom_call" | custom-call | bytes 6642000 | tf_op jit(solution)/shard_map/grads/pallas_call | solution.py:888
  356.2 16.5 %collective-permute-done.42 = bf16[256,1024]{1,0:T(8,128)(2,1)S(1)} collective-permute-done((bf16[256,1024]{1,0:T(8,128)(2,1)S(1)}, bf16[256,1024]{1,0:T(8,128)(2,1)S(1)}, u32[]{:S(2)}, u32[]{:S(2)}) %collective-permute-start.42) | collective-permute-done | bytes 524320 | tf_op jit(solution)/shard_map/ppermute | solution.py:738
  378.7 7.2 %store.2 = bf16[2048,1024]{1,0:T(8,128)(2,1)} custom-call(s32[6]{0:T(128)S(1)} %stack.138.place, bf16[1024,1024]{1,0:T(8,128)(2,1)S(1)} %copy-done.2, bf16[512,1024]{1,0:T(8,128)(2,1)} %collective-permute-done.36.refs_1_, bf16[512,1024]{1,0:T(8,128)(2,1)} %collective-permute-done.38.refs_2_), custom_call_target="tpu_custom_call" | custom-call | bytes 5535000 | tf_op jit(solution)/shard_map/store/pallas_call | solution.py:1037
  398.9 7.1 %collective-permute-done.45 = bf16[512,640]{1,0:T(8,128)(2,1)} collective-permute-done((bf16[512,640]{1,0:T(8,128)(2,1)}, bf16[512,640]{1,0:T(8,128)(2,1)}, u32[]{:S(2)}, u32[]{:S(2)}) %collective-permute-start.45) | collective-permute-done | bytes 655392 | tf_op jit(solution)/shard_map/ppermute | solution.py:742
  411.3 7.2 %collective-permute-done.50.refs_2_ = bf16[512,1024]{1,0:T(8,128)(2,1)S(1)} collective-permute-done((bf16[512,1024]{1,0:T(8,128)(2,1)S(1)}, bf16[512,1024]{1,0:T(8,128)(2,1)S(1)}, u32[]{:S(2)}, u32[]{:S(2)}) %collective-permute-start.50) | collective-permute-done | bytes 1048608 | tf_op jit(solution)/shard_map/ppermute | solution.py:709
  437.3 6.2 %store.3 = bf16[2048,1024]{1,0:T(8,128)(2,1)} custom-call(s32[8]{0:T(128)S(1)} %stack.143.place, bf16[512,1024]{1,0:T(8,128)(2,1)S(1)} %get-tuple-element.399.refs_0_, bf16[512,1024]{1,0:T(8,128)(2,1)S(1)} %collective-permute-done.44.refs_1_, bf16[512,1024]{1,0:T(8,128)(2,1)S(1)} %collective-permute-done.50.refs_2_, ...), custom_call_target="tpu_custom_call" | custom-call | bytes 5535000 | tf_op jit(solution)/shard_map/store/pallas_call | solution.py:1037
  (488 shorter events, 208.5 us)
Async XLA Ops:
  13.2 17.3 %collective-permute-start.3 = (f32[8,512]{1,0:T(8,128)S(1)}, f32[8,512]{1,0:T(8,128)S(1)}, u32[]{:S(2)}, u32[]{:S(2)}) collective-permute-start(f32[8,512]{1,0:T(8,128)S(1)} %pad_maximum_fusion.25), channel_id=1, source_target_pairs={{0,2},{2,0},{1,3},{3,1},{4,6},{6,4},{5,7},{7,5},{8,10},{10,8},{9,1... | collective-permute-start | bytes 49160 | tf_op jit(solution)/shard_map/ppermute | solution.py:709
  16.6 16.5 %collective-permute-start.1 = (bf16[256,640]{1,0:T(8,128)(2,1)S(1)}, bf16[256,640]{1,0:T(8,128)(2,1)S(1)}, u32[]{:S(2)}, u32[]{:S(2)}) collective-permute-start(bf16[256,640]{1,0:T(8,128)(2,1)S(1)} %pad_maximum_fusion.19), channel_id=1, source_target_pairs={{0,16},{4,20},{8,24},{12,28},{16,0},{20,4},{24,8},{28,12},{1,17},{... | collective-permute-start | bytes 983048 | tf_op jit(solution)/shard_map/ppermute | solution.py:738
  50.2 21.7 %collective-permute-start.7 = (bf16[1024,640]{1,0:T(8,128)(2,1)S(1)}, bf16[1024,640]{1,0:T(8,128)(2,1)S(1)}, u32[]{:S(2)}, u32[]{:S(2)}) collective-permute-start(bf16[1024,640]{1,0:T(8,128)(2,1)S(1)} %pad_maximum_fusion.1.near_a.near_b), channel_id=1, source_target_pairs={{0,4},{1,3},{2,6},{3,1},{4,0},{5,7},{6,2},{7,5},{8,12},{9,11},{10,... | collective-permute-start | bytes 3932168 | tf_op jit(solution)/shard_map/ppermute | solution.py:742
  77.1 26.5 %collective-permute-start.11 = (bf16[1024,512]{1,0:T(8,128)(2,1)S(1)}, bf16[1024,512]{1,0:T(8,128)(2,1)S(1)}, u32[]{:S(2)}, u32[]{:S(2)}) collective-permute-start(bf16[1024,512]{1,0:T(8,128)(2,1)S(1)} %pad_maximum_fusion.2.near_a.near_b), channel_id=1, source_target_pairs={{0,4},{1,3},{2,6},{3,1},{4,0},{5,7},{6,2},{7,5},{8,12},{9,11},{10,... | collective-permute-start | bytes 3145736 | tf_op jit(solution)/shard_map/ppermute | solution.py:742
  77.5 15.4 %collective-permute-start.12 = (bf16[512,512]{1,0:T(8,128)(2,1)S(1)}, bf16[512,512]{1,0:T(8,128)(2,1)S(1)}, u32[]{:S(2)}, u32[]{:S(2)}) collective-permute-start(bf16[512,512]{1,0:T(8,128)(2,1)S(1)} %pad_maximum_fusion.12), channel_id=1, source_target_pairs={{0,2},{1,5},{2,0},{3,7},{4,6},{5,1},{6,4},{7,3},{8,10},{9,13},{10,... | collective-permute-start | bytes 1572872 | tf_op jit(solution)/shard_map/ppermute | solution.py:742
  79.1 24.5 %collective-permute-start.13 = (bf16[256,1024]{1,0:T(8,128)(2,1)S(1)}, bf16[256,1024]{1,0:T(8,128)(2,1)S(1)}, u32[]{:S(2)}, u32[]{:S(2)}) collective-permute-start(bf16[256,1024]{1,0:T(8,128)(2,1)S(1)} %pad_maximum_fusion.13), channel_id=1, source_target_pairs={{0,16},{4,20},{8,24},{12,28},{16,0},{20,4},{24,8},{28,12},{1,17},{... | collective-permute-start | bytes 1572872 | tf_op jit(solution)/shard_map/ppermute | solution.py:738
  103.8 26.1 %collective-permute-start.16 = (bf16[1024,512]{1,0:T(8,128)(2,1)S(1)}, bf16[1024,512]{1,0:T(8,128)(2,1)S(1)}, u32[]{:S(2)}, u32[]{:S(2)}) collective-permute-start(bf16[1024,512]{1,0:T(8,128)(2,1)S(1)} %pad_maximum_fusion.3.near_a.near_b), channel_id=1, source_target_pairs={{0,4},{1,3},{2,6},{3,1},{4,0},{5,7},{6,2},{7,5},{8,12},{9,11},{10,... | collective-permute-start | bytes 3145736 | tf_op jit(solution)/shard_map/ppermute | solution.py:742
  105.4 24.5 %collective-permute-start.17 = (bf16[512,1024]{1,0:T(8,128)(2,1)S(1)}, bf16[512,1024]{1,0:T(8,128)(2,1)S(1)}, u32[]{:S(2)}, u32[]{:S(2)}) collective-permute-start(bf16[512,1024]{1,0:T(8,128)(2,1)S(1)} %pad_maximum_fusion.4), channel_id=1, source_target_pairs={{0,2},{1,5},{2,0},{3,7},{4,6},{5,1},{6,4},{7,3},{8,10},{9,13},{10,... | collective-permute-start | bytes 3145736 | tf_op jit(solution)/shard_map/ppermute | solution.py:742
  130.9 31.7 %collective-permute-start.20 = (bf16[1024,1024]{1,0:T(8,128)(2,1)S(1)}, bf16[1024,1024]{1,0:T(8,128)(2,1)S(1)}, u32[]{:S(2)}, u32[]{:S(2)}) collective-permute-start(bf16[1024,1024]{1,0:T(8,128)(2,1)S(1)} %pad_maximum_fusion.near_a.near_b), channel_id=1, source_target_pairs={{0,4},{1,3},{2,6},{3,1},{4,0},{5,7},{6,2},{7,5},{8,12},{9,11},{10,... | collective-permute-start | bytes 6291464 | tf_op jit(solution)/shard_map/ppermute | solution.py:742
  144.0 29.9 %collective-permute-start.22 = (bf16[1024,1024]{1,0:T(8,128)(2,1)S(1)}, bf16[1024,1024]{1,0:T(8,128)(2,1)S(1)}, u32[]{:S(2)}, u32[]{:S(2)}) collective-permute-start(bf16[1024,1024]{1,0:T(8,128)(2,1)S(1)} %products.2.part_ref), channel_id=1, source_target_pairs={{0,1},{1,0},{2,3},{3,2},{4,5},{5,4},{6,7},{7,6},{8,9},{9,8},{10,11... | collective-permute-start | bytes 6291464 | tf_op jit(solution)/shard_map/ppermute | solution.py:705
  198.7 20.1 %collective-permute-start.25 = (bf16[1024,1024]{1,0:T(8,128)(2,1)}, bf16[1024,1024]{1,0:T(8,128)(2,1)S(1)}, u32[]{:S(2)}, u32[]{:S(2)}) collective-permute-start(bf16[1024,1024]{1,0:T(8,128)(2,1)} %get-tuple-element.317.dpart_ref), channel_id=1, source_target_pairs={{0,1},{1,0},{2,3},{3,2},{4,5},{5,4},{6,7},{7,6},{8,9},{9,8},{10,11... | collective-permute-start | bytes 6291464 | tf_op jit(solution)/shard_map/ppermute | solution.py:705
  220.9 30.3 %collective-permute-start.26 = (bf16[2,512,1024]{2,1,0:T(8,128)(2,1)}, bf16[2,512,1024]{2,1,0:T(8,128)(2,1)S(1)}, u32[]{:S(2)}, u32[]{:S(2)}) collective-permute-start(bf16[2,512,1024]{2,1,0:T(8,128)(2,1)} %get-tuple-element.340), channel_id=1, source_target_pairs={{0,4},{1,3},{2,6},{3,1},{4,0},{5,7},{6,2},{7,5},{8,12},{9,11},{10,... | collective-permute-start | bytes 6291464 | tf_op jit(solution)/shard_map/ppermute | solution.py:742
  222.4 25.3 %collective-permute-start.27 = (bf16[512,512]{1,0:T(8,128)(2,1)S(1)}, bf16[512,512]{1,0:T(8,128)(2,1)S(1)}, u32[]{:S(2)}, u32[]{:S(2)}) collective-permute-start(bf16[512,512]{1,0:T(8,128)(2,1)S(1)} %fusion.7), channel_id=1, source_target_pairs={{0,2},{1,5},{2,0},{3,7},{4,6},{5,1},{6,4},{7,3},{8,10},{9,13},{10,... | collective-permute-start | bytes 1572872 | tf_op jit(solution)/shard_map/ppermute | solution.py:742
  267.7 37.3 %collective-permute-start.29 = (bf16[2,512,1024]{2,1,0:T(8,128)(2,1)}, bf16[2,512,1024]{2,1,0:T(8,128)(2,1)}, u32[]{:S(2)}, u32[]{:S(2)}) collective-permute-start(bf16[2,512,1024]{2,1,0:T(8,128)(2,1)} %get-tuple-element.362), channel_id=1, source_target_pairs={{0,4},{1,3},{2,6},{3,1},{4,0},{5,7},{6,2},{7,5},{8,12},{9,11},{10,... | collective-permute-start | bytes 6291464 | tf_op jit(solution)/shard_map/ppermute | solution.py:742
  269.2 35.9 %collective-permute-start.30 = (bf16[256,1536]{1,0:T(8,128)(2,1)}, bf16[256,1536]{1,0:T(8,128)(2,1)}, u32[]{:S(2)}, u32[]{:S(2)}) collective-permute-start(bf16[256,1536]{1,0:T(8,128)(2,1)} %pad_maximum_fusion.7), channel_id=1, source_target_pairs={{0,16},{4,20},{8,24},{12,28},{16,0},{20,4},{24,8},{28,12},{1,17},{... | collective-permute-start | bytes 2359304 | tf_op jit(solution)/shard_map/ppermute | solution.py:738
  309.0 21.4 %collective-permute-start.31 = (bf16[512,1024]{1,0:T(8,128)(2,1)S(1)}, bf16[512,1024]{1,0:T(8,128)(2,1)S(1)}, u32[]{:S(2)}, u32[]{:S(2)}) collective-permute-start(bf16[512,1024]{1,0:T(8,128)(2,1)S(1)} %fusion), channel_id=1, source_target_pairs={{0,2},{1,5},{2,0},{3,7},{4,6},{5,1},{6,4},{7,3},{8,10},{9,13},{10,... | collective-permute-start | bytes 3145736 | tf_op jit(solution)/shard_map/ppermute | solution.py:742
  314.4 32.0 %collective-permute-start.36 = (bf16[512,1024]{1,0:T(8,128)(2,1)S(1)}, bf16[512,1024]{1,0:T(8,128)(2,1)}, u32[]{:S(2)}, u32[]{:S(2)}) collective-permute-start(bf16[512,1024]{1,0:T(8,128)(2,1)S(1)} %constant_dynamic-slice_fusion.6), channel_id=1, source_target_pairs={{0,2},{2,0},{1,3},{3,1},{4,6},{6,4},{5,7},{7,5},{8,10},{10,8},{9,1... | collective-permute-start | bytes 3145736 | tf_op jit(solution)/shard_map/ppermute | solution.py:709
  332.1 21.4 %collective-permute-start.40 = (bf16[512,1024]{1,0:T(8,128)(2,1)S(1)}, bf16[512,1024]{1,0:T(8,128)(2,1)S(1)}, u32[]{:S(2)}, u32[]{:S(2)}) collective-permute-start(bf16[512,1024]{1,0:T(8,128)(2,1)S(1)} %get-tuple-element.392), channel_id=1, source_target_pairs={{0,1},{1,0},{2,3},{3,2},{4,5},{5,4},{6,7},{7,6},{8,9},{9,8},{10,11... | collective-permute-start | bytes 3145736 | tf_op jit(solution)/shard_map/ppermute | solution.py:705
  347.3 38.6 %collective-permute-start.37 = (bf16[2,512,640]{2,1,0:T(8,128)(2,1)}, bf16[2,512,640]{2,1,0:T(8,128)(2,1)}, u32[]{:S(2)}, u32[]{:S(2)}) collective-permute-start(bf16[2,512,640]{2,1,0:T(8,128)(2,1)} %get-tuple-element.388), channel_id=1, source_target_pairs={{0,4},{1,3},{2,6},{3,1},{4,0},{5,7},{6,2},{7,5},{8,12},{9,11},{10,... | collective-permute-start | bytes 3932168 | tf_op jit(solution)/shard_map/ppermute | solution.py:742
  352.0 20.7 %collective-permute-start.42 = (bf16[256,1024]{1,0:T(8,128)(2,1)S(1)}, bf16[256,1024]{1,0:T(8,128)(2,1)S(1)}, u32[]{:S(2)}, u32[]{:S(2)}) collective-permute-start(bf16[256,1024]{1,0:T(8,128)(2,1)S(1)} %fusion.4), channel_id=1, source_target_pairs={{0,16},{4,20},{8,24},{12,28},{16,0},{20,4},{24,8},{28,12},{1,17},{... | collective-permute-start | bytes 1572872 | tf_op jit(solution)/shard_map/ppermute | solution.py:738
  353.4 25.2 %collective-permute-start.38 = (bf16[512,1024]{1,0:T(8,128)(2,1)}, bf16[512,1024]{1,0:T(8,128)(2,1)}, u32[]{:S(2)}, u32[]{:S(2)}) collective-permute-start(bf16[512,1024]{1,0:T(8,128)(2,1)} %collective-permute-done.36.refs_1_), channel_id=1, source_target_pairs={{0,1},{1,0},{2,3},{3,2},{4,5},{5,4},{6,7},{7,6},{8,9},{9,8},{10,11... | collective-permute-start | bytes 3145736 | tf_op jit(solution)/shard_map/ppermute | solution.py:705
  388.0 18.0 %collective-permute-start.45 = (bf16[512,640]{1,0:T(8,128)(2,1)}, bf16[512,640]{1,0:T(8,128)(2,1)}, u32[]{:S(2)}, u32[]{:S(2)}) collective-permute-start(bf16[512,640]{1,0:T(8,128)(2,1)} %fusion.2), channel_id=1, source_target_pairs={{0,2},{1,5},{2,0},{3,7},{4,6},{5,1},{6,4},{7,3},{8,10},{9,13},{10,... | collective-permute-start | bytes 1966088 | tf_op jit(solution)/shard_map/ppermute | solution.py:742
  388.1 30.3 %collective-permute-start.50 = (bf16[512,1024]{1,0:T(8,128)(2,1)S(1)}, bf16[512,1024]{1,0:T(8,128)(2,1)S(1)}, u32[]{:S(2)}, u32[]{:S(2)}) collective-permute-start(bf16[512,1024]{1,0:T(8,128)(2,1)S(1)} %get-tuple-element.399.refs_0_), channel_id=1, source_target_pairs={{0,2},{2,0},{1,3},{3,1},{4,6},{6,4},{5,7},{7,5},{8,10},{10,8},{9,1... | collective-permute-start | bytes 3145736 | tf_op jit(solution)/shard_map/ppermute | solution.py:709
  390.1 47.1 %collective-permute-start.44 = (bf16[512,1024]{1,0:T(8,128)(2,1)S(1)}, bf16[512,1024]{1,0:T(8,128)(2,1)S(1)}, u32[]{:S(2)}, u32[]{:S(2)}) collective-permute-start(bf16[512,1024]{1,0:T(8,128)(2,1)S(1)} %get-tuple-element.399.refs_0_), channel_id=1, source_target_pairs={{0,1},{1,0},{2,3},{3,2},{4,5},{5,4},{6,7},{7,6},{8,9},{9,8},{10,11... | collective-permute-start | bytes 3145736 | tf_op jit(solution)/shard_map/ppermute | solution.py:705
  (145 other events, 1267.4 us)
